TPU v7x, 256 devices: a whole 4x4x8 slice. The times are simulated.
256 devices in a mesh: latent: 32 (over z, x), replica: 8 (over y, core).
Axes of the slice: x: 4, y: 4, z: 8, core: 2. Of those that a mesh axis runs over, the one named last changes fastest.
Arguments:
- tokens: bfloat16 [131072, 2048], P(('replica', 'latent')), may hold values from -6 to 6
- block_ids: int32 [131072, 2], P(('replica', 'latent')), may hold values from 0 to 255, as said below
- enc_bias: float32 [16384], P('latent'), may hold values from -1 to 0.5
- enc_master: float32 [2048, 16384], P('replica', 'latent'), may hold values from -0.125 to 0.125
- dec_master: float32 [16384, 2048], P('latent', 'replica'), may hold values from -0.5 to 0.5
- enc_first: float32 [2048, 16384], P('replica', 'latent'), may hold values from -256 to 256
- enc_second: float32 [2048, 16384], P('replica', 'latent'), may hold values from 1000 to 20000
- dec_first: float32 [16384, 2048], P('latent', 'replica'), may hold values from -32 to 32
- dec_second: float32 [16384, 2048], P('latent', 'replica'), may hold values from 20 to 400
Outputs:
- enc_master_new: float32 [2048, 16384], P('replica', 'latent')
- dec_master_new: float32 [16384, 2048], P('latent', 'replica')
- enc_first_new: float32 [2048, 16384], P('replica', 'latent')
- enc_second_new: float32 [2048, 16384], P('replica', 'latent')
- decoder_first_moment_next: float32 [16384, 2048], P('latent', 'replica')
- dec_second_new: float32 [16384, 2048], P('latent', 'replica')
Inputs may be any that keep to these rules, and one draw needn't show every extreme that they name: `block_ids`: each row names 2 different blocks. Among the 512 rows of one device (aligned blocks of rows), no block is named by more than 5 rows, and in every such group of rows some block is named by exactly 5 rows.
All inputs are finite; a program needn't handle non-finite values.
Results may differ from a plain program's by a relative error of at most 0.0041.
Values may be sent and summed in bfloat16 or wider, within the bound.
A program may use at most 128 MiB of HBM per device.

v0:
```python
import jax
import jax.numpy as jnp
from jax import lax
from jax.sharding import PartitionSpec as P

BLOCK = 64
ACT = 2


learn_rate = 0.001
adam_eps = 1e-08
first_fix = 1.0 - 0.9**10
second_fix = 1.0 - 0.95**10


def select_rows(block_list, block_nums, capacity):
    count_rows = block_list.shape[0]
    chosen = jnp.any(block_list[None, :, :] == block_nums[:, None, None], axis=-1)
    places = jnp.cumsum(chosen.astype(jnp.int32), axis=1) - 1
    slot_nums = jnp.arange(capacity, dtype=jnp.int32)
    select = chosen[:, None, :] & (places[:, None, :] == slot_nums[None, :, None])
    row_nums = jnp.arange(count_rows, dtype=jnp.int32)
    slot_rows = jnp.sum(jnp.where(select, row_nums[None, None, :], 0), axis=-1)
    filled = jnp.any(select, axis=-1)
    return (slot_rows, filled)


def adam(master_weights_full, gradient, first, second):
    first_new = 0.9 * first + 0.1 * gradient
    second_new = 0.95 * second + 0.05 * gradient * gradient
    update = first_new / first_fix / (jnp.sqrt(second_new / second_fix) + adam_eps)
    return (master_weights_full - learn_rate * update, first_new, second_new)


def local(
    tokens,
    block_ids,
    enc_bias,
    enc_master,
    dec_master,
    enc_first,
    enc_second,
    dec_first,
    dec_second,
):
    enc_weight, dec_weight = (
        lax.all_gather(enc_master.astype(jnp.bfloat16), "replica", axis=0, tiled=True),
        lax.all_gather(dec_master.astype(jnp.bfloat16), "replica", axis=1, tiled=True),
    )
    tok_count = tokens.shape[0]
    model_width = tokens.shape[1]
    lat_dev = enc_weight.shape[1]
    local_blocks = lat_dev // BLOCK
    shard_count = lax.axis_size("latent")
    block_count = local_blocks * shard_count
    capacity = max(2, 5 * tok_count * ACT // (4 * block_count))
    enc_blocks = enc_weight.reshape(model_width, local_blocks, BLOCK)
    decoder_block_list = dec_weight.reshape(local_blocks, BLOCK, model_width)
    bias_blocks = enc_bias.reshape(1, 1, local_blocks, 1, BLOCK)
    slot_rows, filled = select_rows(block_ids, jnp.arange(block_count, dtype=jnp.int32), capacity)
    send_rows = jnp.where(filled[..., None], tokens[slot_rows], jnp.zeros((), jnp.bfloat16))
    send_rows = send_rows.reshape(shard_count, 1, local_blocks, capacity, model_width)
    arrived = lax.all_to_all(send_rows, "latent", split_axis=0, concat_axis=1, tiled=True)
    preact = (
        jnp.einsum("asbnd,dbk->asbnk", arrived, enc_blocks, preferred_element_type=jnp.float32)
        + bias_blocks
    )
    values_out, slopes = jax.jvp(
        lambda inner: jax.nn.gelu(inner, approximate=True), (preact,), (jnp.ones_like(preact),)
    )
    latent_codes_active = values_out.astype(jnp.bfloat16)
    contrib = jnp.einsum(
        "xlvcw,vwh->xlvch",
        latent_codes_active,
        decoder_block_list,
        preferred_element_type=jnp.float32,
    ).astype(jnp.bfloat16)
    rows_in, latent_codes_active, slopes, contrib = (arrived, latent_codes_active, slopes, contrib)
    returned = lax.all_to_all(contrib, "latent", split_axis=1, concat_axis=0, tiled=True).reshape(
        block_count * capacity, model_width
    )
    targets = slot_rows.reshape(-1)
    occupied = filled.reshape(-1)
    onehot = (
        (targets[None, :] == jnp.arange(tok_count, dtype=jnp.int32)[:, None]) & occupied[None, :]
    ).astype(jnp.bfloat16)
    rebuilt = jnp.dot(onehot, returned, preferred_element_type=jnp.float32)
    error_rows = (rebuilt - tokens.astype(jnp.float32)).astype(jnp.bfloat16)
    send_err = jnp.where(filled[..., None], error_rows[slot_rows], jnp.zeros((), jnp.bfloat16))
    send_err = send_err.reshape(shard_count, 1, local_blocks, capacity, model_width)
    error_input_rows = lax.all_to_all(send_err, "latent", split_axis=0, concat_axis=1, tiled=True)
    coded_grad = jnp.einsum(
        "emtco,tpo->emtcp", error_input_rows, decoder_block_list, preferred_element_type=jnp.float32
    )
    pre_grad = (coded_grad * slopes).astype(jnp.bfloat16)
    dec_grad = jnp.einsum(
        "ltuje,ltujw->uew",
        latent_codes_active,
        error_input_rows,
        preferred_element_type=jnp.float32,
    ).reshape(lat_dev, model_width)
    enc_grad = jnp.einsum(
        "asbnd,asbnk->dbk", rows_in, pre_grad, preferred_element_type=jnp.float32
    ).reshape(model_width, lat_dev)
    enc_share, dec_share = (
        lax.psum_scatter(enc_grad, "replica", scatter_dimension=0, tiled=True),
        lax.psum_scatter(dec_grad, "replica", scatter_dimension=1, tiled=True),
    )
    enc_master_new, enc_first_new, enc_second_new = adam(
        enc_master, enc_share, enc_first, enc_second
    )
    dec_master_new, decoder_first_moment_next, dec_second_new = adam(
        dec_master, dec_share, dec_first, dec_second
    )
    return (
        enc_master_new,
        dec_master_new,
        enc_first_new,
        enc_second_new,
        decoder_first_moment_next,
        dec_second_new,
    )


def solution(mesh):
    return jax.shard_map(
        local,
        mesh=mesh,
        in_specs=(
            P(("replica", "latent"), None),
            P(("replica", "latent"), None),
            P("latent"),
            P("replica", "latent"),
            P("latent", "replica"),
            P("replica", "latent"),
            P("replica", "latent"),
            P("latent", "replica"),
            P("latent", "replica"),
        ),
        out_specs=(
            P("replica", "latent"),
            P("latent", "replica"),
            P("replica", "latent"),
            P("replica", "latent"),
            P("latent", "replica"),
            P("latent", "replica"),
        ),
        check_vma=False,
    )
```

profile of v0, /device:TPU:1, one launch (start us, length us, event | category | flops | bytes accessed | tf_op | source)
XLA Modules:
  0.0 609.8 jit_solution(1492007371377669889)
XLA Ops:
  7.2 0.0 copy-start
  7.2 1.0 fusion.39
  8.2 0.2 copy.59
  8.4 0.3 fusion.52
  8.8 0.1 add_add_fusion
  8.9 0.1 copy.61
  9.0 0.2 copy.62
  9.2 0.8 select_reduce_fusion
  10.0 0.6 fusion.13
  10.7 0.1 copy.66
  10.8 0.2 reshape.147
  11.0 0.0 copy-done
  11.0 6.2 %gather_fusion = bf16[1280,2048]{1,0:T(8,128)(2,1)} fusion(bf16[512,2048]{1,0:T(8,128)(2,1)S(1)} %copy-done, s32[2048]{0:T(1024)S(1)} %pad_clamp_fusion), kind=kCustom, calls=%fused_computation | custom fusion | bytes 10490880 | tf_op jit(solution)/shard_map/gather | solution.py:61
  17.3 9.8 %gather.11 = bf16[32,1,8,5,2048]{4,3,2,0,1:T(8,128)(2,1)} reshape(bf16[1280,2048]{1,0:T(8,128)(2,1)} %gather_fusion) | data formatting | bytes 10485760 | tf_op jit(solution)/shard_map/gather | solution.py:61
  27.0 0.2 copy.79
  27.2 7.5 %broadcast_select_fusion.1 = bf16[32,1,8,5,2048]{4,3,2,0,1:T(8,128)(2,1)} fusion(bf16[32,1,8,5,2048]{4,3,2,0,1:T(8,128)(2,1)} %gather.11, pred[32,8,5]{2,1,0:T(8,128)(4,1)S(1)} %bitcast.100), kind=kLoop, calls=%fused_computation.3 | loop fusion | flops 2621440 | bytes 10487040 | tf_op jit(solution)/shard_map/jit(_where)/select_n | solution.py:61
  34.7 11.7 %copy.67 = bf16[32,1,8,5,2048]{4,2,3,1,0:T(8,128)(2,1)} copy(bf16[32,1,8,5,2048]{4,3,2,0,1:T(8,128)(2,1)} %broadcast_select_fusion.1) | data formatting | bytes 10485760 | tf_op jit(solution)/shard_map/jit(_where)/select_n | solution.py:61
  46.4 12.1 %all-to-all-start = ((bf16[32,1,8,5,2048]{4,2,3,1,0:T(8,128)(2,1)}), bf16[32,1,8,5,2048]{4,2,3,1,0:T(8,128)(2,1)}, u32[]{:S(2)}, u32[]{:S(2)}) async-start(bf16[32,1,8,5,2048]{4,2,3,1,0:T(8,128)(2,1)} %copy.67), calls=%async_computation | async-start | bytes 10485760 | tf_op jit(solution)/shard_map/all_to_all | solution.py:63
  58.5 0.0 all-gather.3.cloned.1.call-start
  58.5 0.0 copy-done.3
  58.5 0.7 convert_element_type.40
  59.3 0.0 all-gather.3.cloned.1.call-update
  59.3 0.3 all-gather.5.cloned.1.call-start
  59.6 0.0 copy-done.2
  59.6 0.7 convert_element_type.42
  60.3 0.0 all-gather.5.cloned.1.call-update
  60.4 0.0 copy-done.10
  60.4 0.1 add.66
  60.5 31.1 %all-gather.3.cloned.1.call-done = bf16[2048,512]{1,0:T(8,128)(2,1)} async-done(((bf16[256,512]{1,0:T(8,128)(2,1)}), bf16[2048,512]{1,0:T(8,128)(2,1)}) %all-gather.3.cloned.1.call-update) | async-done | bytes 2097168 | tf_op jit(solution)/shard_map/all_gather | solution.py:47
  91.6 4.0 copy.69
  95.5 77.5 %all-to-all-done = bf16[32,1,8,5,2048]{4,2,3,1,0:T(8,128)(2,1)} async-done(((bf16[32,1,8,5,2048]{4,2,3,1,0:T(8,128)(2,1)}), bf16[32,1,8,5,2048]{4,2,3,1,0:T(8,128)(2,1)}, u32[]{:S(2)}, u32[]{:S(2)}) %all-to-all-start) | async-done | bytes 5242912 | tf_op jit(solution)/shard_map/all_to_all | solution.py:63
  173.0 9.3 %fusion.30 = f32[1,32,8,5,64]{4,1,3,2,0:T(8,128)S(1)} fusion(bf16[2048,8,64,1]{0,2,3,1:T(8,128)(2,1)} %bitcast.95, bf16[32,1,8,5,2048]{4,2,3,1,0:T(8,128)(2,1)} %all-to-all-done, f32[8,64]{1,0:T(8,128)S(1)} %add.66), kind=kOutput, calls=%fused_computation.30 | convolution fusion | flops 335626240 | bytes 7669760 | tf_op jit(solution)/shard_map/asbnd,dbk->asbnk/dot_general | solution.py:65
  182.3 0.0 all-gather.5.cloned.1.call-done
  182.3 3.1 convert_bitcast_fusion
  185.4 5.2 copy.70
  190.6 12.1 %all-to-all-start.1 = ((bf16[1,32,8,5,2048]{4,2,3,0,1:T(8,128)(2,1)}), bf16[1,32,8,5,2048]{4,2,3,0,1:T(8,128)(2,1)}, u32[]{:S(2)}, u32[]{:S(2)}) async-start(bf16[1,32,8,5,2048]{4,2,3,0,1:T(8,128)(2,1)} %copy.70), calls=%async_computation.1 | async-start | bytes 10485760 | tf_op jit(solution)/shard_map/all_to_all | solution.py:79
  202.7 11.5 %reduce-scatter.5.cloned.1.call-start = ((), (), s32[]{:S(2)}) async-start(), calls=%async_computation.8 | async-start | bytes 4718592 | tf_op jit(solution)/shard_map/reduce_scatter | solution.py:107
  214.3 0.1 copy.64
  214.4 0.2 and.20
  214.6 0.2 eq.47
  214.8 102.4 %all-to-all-done.1 = bf16[1,32,8,5,2048]{4,2,3,0,1:T(8,128)(2,1)} async-done(((bf16[1,32,8,5,2048]{4,2,3,0,1:T(8,128)(2,1)}), bf16[1,32,8,5,2048]{4,2,3,0,1:T(8,128)(2,1)}, u32[]{:S(2)}, u32[]{:S(2)}) %all-to-all-start.1) | async-done | bytes 5242912 | tf_op jit(solution)/shard_map/all_to_all | solution.py:79
  317.2 10.8 %copy.71 = bf16[1,32,8,5,2048]{4,3,2,1,0:T(8,128)(2,1)} copy(bf16[1,32,8,5,2048]{4,2,3,0,1:T(8,128)(2,1)} %all-to-all-done.1) | data formatting | bytes 10485760 | tf_op jit(solution)/shard_map/all_to_all | solution.py:79
  328.0 10.0 %reshape.139 = bf16[1280,2048]{1,0:T(8,128)(2,1)} reshape(bf16[1,32,8,5,2048]{4,3,2,1,0:T(8,128)(2,1)} %copy.71) | data formatting | bytes 10485760 | tf_op jit(solution)/shard_map/reshape | solution.py:79
  338.0 6.6 %subtract_convert_fusion = bf16[512,2048]{1,0:T(8,128)(2,1)} fusion(bf16[512,2048]{1,0:T(8,128)(2,1)S(1)} %copy-done, bf16[1280,2048]{1,0:T(8,128)(2,1)} %reshape.139, s32[1280]{0:T(1024)S(1)} %eq.47, pred[1280]{0:T(1024)(128)(4,1)S(1)} %and.20), kind=kOutput, calls=%fused_computation.17 | convolution fusion | flops 2688811008 | bytes 9443584 | tf_op jit(solution)/shard_map/dot_general | solution.py:87
  344.6 12.7 %gather_fusion.1 = bf16[1280,2048]{1,0:T(8,128)(2,1)} fusion(bf16[512,2048]{1,0:T(8,128)(2,1)} %subtract_convert_fusion, s32[2048]{0:T(1024)S(1)} %pad_clamp_fusion), kind=kCustom, calls=%fused_computation.1 | custom fusion | bytes 10490880 | tf_op jit(solution)/shard_map/gather | solution.py:89
  357.3 9.8 %gather.13 = bf16[32,1,8,5,2048]{4,3,2,0,1:T(8,128)(2,1)} reshape(bf16[1280,2048]{1,0:T(8,128)(2,1)} %gather_fusion.1) | data formatting | bytes 10485760 | tf_op jit(solution)/shard_map/gather | solution.py:89
  367.1 7.5 %broadcast_select_fusion = bf16[32,1,8,5,2048]{4,3,2,0,1:T(8,128)(2,1)} fusion(bf16[32,1,8,5,2048]{4,3,2,0,1:T(8,128)(2,1)} %gather.13, pred[32,8,5]{2,1,0:T(8,128)(4,1)S(1)} %bitcast.101), kind=kLoop, calls=%fused_computation.2 | loop fusion | flops 2621440 | bytes 10487040 | tf_op jit(solution)/shard_map/jit(_where)/select_n | solution.py:89
  374.6 8.8 %copy.72 = bf16[32,1,8,5,2048]{4,2,3,1,0:T(8,128)(2,1)S(1)} copy(bf16[32,1,8,5,2048]{4,3,2,0,1:T(8,128)(2,1)} %broadcast_select_fusion) | data formatting | bytes 10485760 | tf_op jit(solution)/shard_map/jit(_where)/select_n | solution.py:89
  383.4 127.1 %all_to_all.12 = bf16[32,1,8,5,2048]{4,2,3,1,0:T(8,128)(2,1)S(1)} all-to-all(bf16[32,1,8,5,2048]{4,2,3,1,0:T(8,128)(2,1)S(1)} %copy.72), channel_id=1, replica_groups=mesh['latent'=32,'replica'=8] {'latent'}, dimensions={0} | all-to-all | bytes 10485760 | tf_op jit(solution)/shard_map/all_to_all | solution.py:91
  510.4 2.3 copy-done.1
  512.7 8.1 %fusion = f32[8,64,2048,1]{2,1,3,0:T(8,128)} fusion(bf16[32,1,8,5,2048]{4,2,3,1,0:T(8,128)(2,1)S(1)} %all_to_all.12, f32[1,32,8,5,64]{4,1,3,2,0:T(8,128)S(1)} %fusion.30), kind=kOutput, calls=%fused_computation.4 | convolution fusion | flops 336281600 | bytes 9764864 | tf_op jit(solution)/shard_map/ltuje,ltujw->uew/dot_general | solution.py:96
  520.9 0.0 reduce-scatter.5.cloned.1.call-update
  520.9 0.0 reduce-scatter.3.cloned.1.call-start
  520.9 5.8 fusion.36
  526.8 10.6 %fusion.4 = f32[8,64,2048,1]{2,1,3,0:T(8,128)} fusion(bf16[32,8,5,64]{3,0,2,1:T(8,128)(2,1)S(1)} %fusion.36, bf16[32,1,8,5,2048]{4,2,3,1,0:T(8,128)(2,1)} %all-to-all-done), kind=kOutput, calls=%fused_computation.8 | convolution fusion | flops 335544320 | bytes 9601024 | tf_op jit(solution)/shard_map/asbnd,asbnk->dbk/dot_general | solution.py:102
  537.3 5.5 copy.74
  542.9 0.0 reduce-scatter.3.cloned.1.call-update
  542.9 15.5 %reduce-scatter.5.cloned.1.call-done = f32[512,256]{1,0:T(8,128)} async-done(((f32[512,2048]{1,0:T(8,128)}), f32[512,256]{1,0:T(8,128)}) %reduce-scatter.5.cloned.1.call-update) | async-done | bytes 524304 | tf_op jit(solution)/shard_map/reduce_scatter | solution.py:107
  558.4 0.0 copy-done.6
  558.4 2.4 multiply_subtract_fusion
  560.8 39.7 %reduce-scatter.3.cloned.1.call-done = f32[256,512]{1,0:T(8,128)} async-done(((f32[2048,512]{1,0:T(8,128)}), f32[256,512]{1,0:T(8,128)}) %reduce-scatter.3.cloned.1.call-update) | async-done | bytes 524304 | tf_op jit(solution)/shard_map/reduce_scatter | solution.py:106
  600.4 0.0 copy-done.4
  600.4 0.0 copy-done.9
  600.4 2.4 multiply_subtract_fusion.1
  (19 shorter events, 0.1 us)
Async XLA Ops:
  7.2 3.9 copy-start
  46.4 12.2 %copy-start.3 = (f32[256,512]{1,0:T(8,128)S(1)}, f32[256,512]{1,0:T(8,128)}, u32[]{:S(2)}) copy-start(f32[256,512]{1,0:T(8,128)} %param.12) | copy-start | bytes 1572868
  46.4 13.2 %copy-start.2 = (f32[512,256]{1,0:T(8,128)S(1)}, f32[512,256]{1,0:T(8,128)}, u32[]{:S(2)}) copy-start(f32[512,256]{1,0:T(8,128)} %param.13) | copy-start | bytes 1572868
  46.4 14.0 %copy-start.10 = (f32[512]{0:T(512)S(1)}, f32[512]{0:T(512)}, u32[]{:S(2)}) copy-start(f32[512]{0:T(512)} %param.11) | copy-start | bytes 6148
  46.4 126.7 %all-to-all-start = ((bf16[32,1,8,5,2048]{4,2,3,1,0:T(8,128)(2,1)}), bf16[32,1,8,5,2048]{4,2,3,1,0:T(8,128)(2,1)}, u32[]{:S(2)}, u32[]{:S(2)}) async-start(bf16[32,1,8,5,2048]{4,2,3,1,0:T(8,128)(2,1)} %copy.67), calls=%async_computation | async-start | bytes 10485760 | tf_op jit(solution)/shard_map/all_to_all | solution.py:63
  58.5 33.1 %all-gather.3.cloned.1.call-start = ((), (), s32[]{:S(2)}) async-start(), calls=%async_computation.5 | async-start | bytes 2359296 | tf_op jit(solution)/shard_map/all_gather | solution.py:47
  59.3 123.0 %all-gather.5.cloned.1.call-start = ((), (), s32[]{:S(2)}) async-start(), calls=%async_computation.6 | async-start | bytes 2359296 | tf_op jit(solution)/shard_map/all_gather | solution.py:48
  190.6 126.6 %all-to-all-start.1 = ((bf16[1,32,8,5,2048]{4,2,3,0,1:T(8,128)(2,1)}), bf16[1,32,8,5,2048]{4,2,3,0,1:T(8,128)(2,1)}, u32[]{:S(2)}, u32[]{:S(2)}) async-start(bf16[1,32,8,5,2048]{4,2,3,0,1:T(8,128)(2,1)} %copy.70), calls=%async_computation.1 | async-start | bytes 10485760 | tf_op jit(solution)/shard_map/all_to_all | solution.py:79
  202.7 355.6 %reduce-scatter.5.cloned.1.call-start = ((), (), s32[]{:S(2)}) async-start(), calls=%async_computation.8 | async-start | bytes 4718592 | tf_op jit(solution)/shard_map/reduce_scatter | solution.py:107
  510.4 2.3 copy-start.1
  512.7 8.2 %copy-start.5 = (bf16[512,2048]{1,0:T(8,128)(2,1)S(1)}, bf16[512,2048]{1,0:T(8,128)(2,1)}, u32[]{:S(2)}) copy-start(bf16[512,2048]{1,0:T(8,128)(2,1)} %all-gather.5.cloned.1.call-done) | copy-start | bytes 6291460
  520.9 79.5 %reduce-scatter.3.cloned.1.call-start = ((), (), s32[]{:S(2)}) async-start(), calls=%async_computation.7 | async-start | bytes 4718592 | tf_op jit(solution)/shard_map/reduce_scatter | solution.py:106
  537.3 21.0 %copy-start.6 = (f32[512,256]{1,0:T(8,128)S(1)}, f32[512,256]{1,0:T(8,128)}, u32[]{:S(2)}) copy-start(f32[512,256]{1,0:T(8,128)} %param.16) | copy-start | bytes 1572868
  537.3 21.0 %copy-start.7 = (f32[512,256]{1,0:T(8,128)S(1)}, f32[512,256]{1,0:T(8,128)}, u32[]{:S(2)}) copy-start(f32[512,256]{1,0:T(8,128)} %param.17) | copy-start | bytes 1572868
  542.9 57.6 %copy-start.4 = (f32[256,512]{1,0:T(8,128)S(1)}, f32[256,512]{1,0:T(8,128)}, u32[]{:S(2)}) copy-start(f32[256,512]{1,0:T(8,128)} %param.12) | copy-start | bytes 1572868
  542.9 57.6 %copy-start.8 = (f32[256,512]{1,0:T(8,128)S(1)}, f32[256,512]{1,0:T(8,128)}, u32[]{:S(2)}) copy-start(f32[256,512]{1,0:T(8,128)} %param.14) | copy-start | bytes 1572868
  542.9 57.6 %copy-start.9 = (f32[256,512]{1,0:T(8,128)S(1)}, f32[256,512]{1,0:T(8,128)}, u32[]{:S(2)}) copy-start(f32[256,512]{1,0:T(8,128)} %param.15) | copy-start | bytes 1572868
Sparse Core Ops, SparseCore 0:
  61.7 29.7 all-gather.2
  94.0 30.1 all-gather.4
  521.0 37.3 reduce-scatter.4
  560.8 39.6 reduce-scatter.2
where the time goes:
time: 621 us; the launch traced here: 610 us
  waiting for transfers between devices  266 us (43%)
  blocking collectives  127 us (20%)
  local copies, waits for them, and re-layouts  98.4 us (16%)
  matrix products  43.5 us (7%)
  starting transfers between devices  36.2 us (6%)
  other arithmetic  24.2 us (4%)
  between operations  14.3 us (2%)
    all_to_all x1, blocking collectives, local(): lax.all_to_all(send_err, 'latent', split_axis=0, concat_axis=1, tiled=True)  127 us
    all_to_all x1, waiting for transfers between devices, local(): lax.all_to_all(contrib, 'latent', split_axis=1, concat_axis=0, tiled=True)  102 us
    all_to_all x1, waiting for transfers between devices, local(): lax.all_to_all(send_rows, 'latent', split_axis=0, concat_axis=1, tiled=True)  77.5 us
    reduce_scatter x1, waiting for transfers between devices, local(): lax.psum_scatter(enc_grad, 'replica', scatter_dimension=0, tiled=True)  39.7 us
    all_gather x1, waiting for transfers between devices, local(): lax.all_gather(enc_master.astype(jnp.bfloat16), 'replica', axis=0, tiled=...  31.1 us
    gather x2, local copies, waits for them, and re-layouts, local(): error_rows[slot_rows]  22.5 us
    gather x2, local copies, waits for them, and re-layouts, local(): tokens[slot_rows]  16 us
    reduce_scatter x1, waiting for transfers between devices, local(): lax.psum_scatter(dec_grad, 'replica', scatter_dimension=1, tiled=True)  15.5 us
  transfers between devices with their start and end apart: 6, of which 5 were waited for; matrix products, arithmetic and copies ran while one was open for 7% of the time, Pallas kernels for 0%

commit v1 on v0

v1 whole, which is shorter than its diff:
```python
import jax
import jax.numpy as jnp
from jax import lax
from jax.sharding import Mesh, PartitionSpec as P

BLOCK = 64
CAP = 5

learn_rate = 0.001
adam_eps = 1e-08
first_fix = 1.0 - 0.9**10
second_fix = 1.0 - 0.95**10

PLANE = ("x", "y", "c")
REP = ("y", "c")


def adam(master, gradient, first, second):
    first_new = 0.9 * first + 0.1 * gradient
    second_new = 0.95 * second + 0.05 * gradient * gradient
    update = first_new / first_fix / (jnp.sqrt(second_new / second_fix) + adam_eps)
    return (master - learn_rate * update, first_new, second_new)


def slot_onehot(block_ids, block_nums):
    chosen = jnp.any(block_ids[None, :, :] == block_nums[:, None, None], axis=-1)
    places = jnp.cumsum(chosen.astype(jnp.int32), axis=1) - 1
    slots = jnp.arange(CAP, dtype=jnp.int32)
    return chosen[:, None, :] & (places[:, None, :] == slots[None, :, None])


def dot(a, b, ca, cb, out=jnp.float32):
    return lax.dot_general(a, b, (((ca,), (cb,)), ((), ())), preferred_element_type=out)


def local(
    tokens,
    block_ids,
    enc_bias,
    enc_master,
    dec_master,
    enc_first,
    enc_second,
    dec_first,
    dec_second,
):
    nz, nx = lax.axis_size("z"), lax.axis_size("x")
    nrep = lax.axis_size("y") * lax.axis_size("c")
    plane = nx * nrep
    tok, width = tokens.shape
    lat = enc_master.shape[1]
    part = width // nrep
    rep = lax.axis_index("y") * lax.axis_size("c") + lax.axis_index("c")

    def spread(w):
        w = w.reshape(nrep, BLOCK, part)
        w = lax.all_to_all(w, REP, split_axis=0, concat_axis=2, tiled=True)
        return lax.all_gather(w, "z", axis=0, tiled=True).reshape(nz * BLOCK, width)

    enc_t = spread(enc_master.astype(jnp.bfloat16).T)
    dec = spread(dec_master.astype(jnp.bfloat16))
    own_bias = lax.dynamic_slice(enc_bias, (rep * BLOCK,), (BLOCK,))
    bias = lax.all_gather(own_bias, "z", axis=0, tiled=True)

    nums = jnp.arange(nz * plane, dtype=jnp.int32).reshape(nz, plane).T.reshape(-1)
    onehot = slot_onehot(block_ids, nums).reshape(nz * plane * CAP, tok).astype(jnp.bfloat16)

    def exchange(rows):
        rows = rows.reshape(plane, nz * CAP, width)
        return lax.all_to_all(rows, PLANE, split_axis=0, concat_axis=0, tiled=True).reshape(
            plane * nz * CAP, width
        )

    arrived = exchange(dot(onehot, tokens, 1, 0, jnp.bfloat16))
    count = arrived.shape[0]
    own = (lax.broadcasted_iota(jnp.int32, (count, lat), 0) % (nz * CAP)) // CAP == (
        lax.broadcasted_iota(jnp.int32, (count, lat), 1) // BLOCK
    )
    preact = dot(arrived, enc_t, 1, 1) + bias[None, :]
    values, slopes = jax.jvp(
        lambda inner: jax.nn.gelu(inner, approximate=True), (preact,), (jnp.ones_like(preact),)
    )
    coded = jnp.where(own, values, 0.0).astype(jnp.bfloat16)
    slopes = jnp.where(own, slopes, 0.0)
    contrib = dot(coded, dec, 1, 0).astype(jnp.bfloat16)
    returned = exchange(contrib)
    rebuilt = dot(onehot, returned, 0, 0)
    error_rows = (rebuilt - tokens.astype(jnp.float32)).astype(jnp.bfloat16)
    err_in = exchange(dot(onehot, error_rows, 1, 0, jnp.bfloat16))
    dec_grad = dot(coded, err_in, 0, 0)
    pre_grad = (dot(err_in, dec, 1, 1) * slopes).astype(jnp.bfloat16)
    enc_grad = dot(pre_grad, arrived, 0, 0)

    def collect(g):
        g = g.astype(jnp.bfloat16).reshape(nz, BLOCK, width)
        g = lax.all_to_all(g, "z", split_axis=0, concat_axis=0, tiled=True)
        g = jnp.sum(g.astype(jnp.float32), axis=0)
        g = lax.all_to_all(g, REP, split_axis=1, concat_axis=0, tiled=True)
        return g.reshape(lat, part)

    dec_share = collect(dec_grad)
    enc_share = collect(enc_grad).T
    enc_new, enc_first_new, enc_second_new = adam(enc_master, enc_share, enc_first, enc_second)
    dec_new, dec_first_new, dec_second_new = adam(dec_master, dec_share, dec_first, dec_second)
    return (enc_new, dec_new, enc_first_new, enc_second_new, dec_first_new, dec_second_new)


def solution(mesh):
    grid = Mesh(mesh.devices.reshape(8, 4, 4, 2), ("z", "x", "y", "c"))
    lat, rep = ("z", "x"), REP
    tok = P(rep + lat, None)
    enc, dec = P(rep, lat), P(lat, rep)
    return jax.shard_map(
        local,
        mesh=grid,
        in_specs=(tok, tok, P(lat), enc, dec, enc, enc, dec, dec),
        out_specs=(enc, dec, enc, enc, dec, dec),
        check_vma=False,
    )
```

time: 621 us -> 452 us (0.73); the launches traced: 610 us -> 451 us
  local copies, waits for them, and re-layouts: 98.4 us -> 27 us
  waiting for transfers between devices: 266 us -> 206 us
  blocking collectives: 127 us -> 87.8 us
  starting transfers between devices: 36.2 us -> 52.1 us
  other arithmetic: 24.2 us -> 11.8 us
  matrix products: 43.5 us -> 51.2 us
    all_to_all x1, blocking collectives: 127 us -> 69.9 us  [exchange(): lax.all_to_all(rows, PLANE, split_axis=0, concat_axis=0, tiled=True)]
    reduce_scatter x2 -> x0, waiting for transfers between devices: 55.1 us -> none  [the longest x1 39.7 us: local(): lax.psum_scatter(enc_grad, 'replica', scatter_dimension=0, tiled=True)]
    gather x4 -> x0, local copies, waits for them, and re-layouts: 38.5 us -> none  [the longest x2 22.5 us: local(): error_rows[slot_rows]]
    all_gather x2, waiting for transfers between devices: 31.1 us -> 0.02 us  [spread(): return lax.all_gather(w, 'z', axis=0, tiled=True).reshape(nz * BLOCK, width)]
    all_to_all x2 -> x8, starting transfers between devices: 24.3 us -> 52 us  [the longest x2 17 us: exchange(): lax.all_to_all(rows, PLANE, split_axis=0, concat_axis=0, tiled=True)]
    all_to_all x2 -> x8, waiting for transfers between devices: 180 us -> 206 us  [the longest x2 107 us: exchange(): lax.all_to_all(rows, PLANE, split_axis=0, concat_axis=0, tiled=True)]
    select_n x4 -> x0, local copies, waits for them, and re-layouts: 20.8 us -> none  [the longest x1 11.7 us: local(): jnp.where(filled[..., None], tokens[slot_rows], jnp.zeros((), jnp.bfloat16))]
    unnamed x0 -> x1, blocking collectives: none -> 17.9 us
  transfers between devices with their start and end apart: 6 -> 10, of which waited for: 5 -> 7; matrix products, arithmetic and copies ran while one was open for 7% -> 12% of each run, Pallas kernels for 0% -> 0%
where the time goes in v1:
time: 452 us; the launch traced here: 451 us
  waiting for transfers between devices  206 us (46%)
  blocking collectives  87.8 us (19%)
  starting transfers between devices  52.1 us (12%)
  matrix products  51.2 us (11%)
  local copies, waits for them, and re-layouts  27 us (6%)
  between operations  14.9 us (3%)
  other arithmetic  11.8 us (3%)
    all_to_all x2, waiting for transfers between devices, exchange(): lax.all_to_all(rows, PLANE, split_axis=0, concat_axis=0, tiled=True)  107 us
    all_to_all x2, waiting for transfers between devices, collect(): g = lax.all_to_all(g, 'z', split_axis=0, concat_axis=0, tiled=True)  87.5 us
    all_to_all x1, blocking collectives, exchange(): lax.all_to_all(rows, PLANE, split_axis=0, concat_axis=0, tiled=True)  69.9 us
    dot_general x6, matrix products, dot(): lax.dot_general(a, b, (((ca,), (cb,)), ((), ())), preferred_element_type=...  51.2 us
    unnamed x1, blocking collectives  17.9 us
    all_to_all x2, starting transfers between devices, exchange(): lax.all_to_all(rows, PLANE, split_axis=0, concat_axis=0, tiled=True)  17 us
    all_to_all x2, starting transfers between devices, collect(): g = lax.all_to_all(g, 'z', split_axis=0, concat_axis=0, tiled=True)  13 us
    all_to_all x2, starting transfers between devices, collect(): g = lax.all_to_all(g, REP, split_axis=1, concat_axis=0, tiled=True)  11.1 us
  transfers between devices with their start and end apart: 10, of which 7 were waited for; matrix products, arithmetic and copies ran while one was open for 12% of the time, Pallas kernels for 0%

profile of v1, /device:TPU:1, one launch (start us, length us, event | category | flops | bytes accessed | tf_op | source)
XLA Modules:
  0.0 451.1 jit_solution(16298411042602340481)
XLA Ops:
  7.2 0.0 copy-start.2
  7.2 1.3 copy.73
  8.5 0.7 convert_element_type.43
  9.2 6.6 %all-to-all-start.1 = ((bf16[8,64,256]{2,1,0:T(8,128)(2,1)}), bf16[8,64,256]{2,1,0:T(8,128)(2,1)S(1)}, u32[]{:S(2)}, u32[]{:S(2)}) async-start(bf16[8,64,256]{2,1,0:T(8,128)(2,1)} %bitcast.6), calls=%async_computation.1 | async-start | bytes 524288 | tf_op jit(solution)/shard_map/all_to_all | solution.py:57
  15.8 0.1 reshape.158
  15.9 0.9 compare_reduce_fusion
  16.8 0.2 copy.64
  17.0 0.7 convert_element_type.45
  17.7 4.5 %all-to-all-done.1 = bf16[8,64,256]{2,1,0:T(8,128)(2,1)S(1)} async-done(((bf16[8,64,256]{2,1,0:T(8,128)(2,1)}), bf16[8,64,256]{2,1,0:T(8,128)(2,1)S(1)}, u32[]{:S(2)}, u32[]{:S(2)}) %all-to-all-start.1) | async-done | bytes 262176 | tf_op jit(solution)/shard_map/all_to_all | solution.py:57
  22.3 4.4 all-to-all-start.2
  26.6 0.7 copy.80
  27.4 0.0 all-gather.3.cloned.1.call-update
  27.4 0.3 fusion.30
  27.8 0.1 add_add_fusion
  27.9 0.1 copy.66
  28.0 0.2 copy.67
  28.2 0.8 copy-done
  29.0 2.5 eq.56
  31.5 3.1 eq.57
  34.6 1.5 and.46
  36.1 3.4 and.47
  39.5 0.7 eq.58
  40.2 1.0 eq.59
  41.2 1.8 compare_and_fusion
  43.0 0.8 copy-done.4
  43.8 4.7 %fusion.18 = bf16[32,40,2048]{2,1,0:T(8,128)(2,1)} fusion(pred[32,40,512]{2,1,0:T(8,128)(4,1)S(1)} %compare_and_fusion, bf16[512,2048]{1,0:T(8,128)(2,1)S(1)} %copy-done.9), kind=kOutput, calls=%fused_computation.35 | convolution fusion | flops 2684354560 | bytes 7995392 | tf_op jit(solution)/shard_map/dot_general | solution.py:33
  48.5 7.0 %all-to-all-start = ((bf16[32,40,2048]{2,1,0:T(8,128)(2,1)}), bf16[32,40,2048]{2,1,0:T(8,128)(2,1)}, u32[]{:S(2)}, u32[]{:S(2)}) async-start(bf16[32,40,2048]{2,1,0:T(8,128)(2,1)} %fusion.18), calls=%async_computation | async-start | bytes 10485760 | tf_op jit(solution)/shard_map/all_to_all | solution.py:70
  55.5 0.0 all-gather.5.cloned.1.call-start
  55.6 0.7 copy.81
  56.3 0.0 all-gather.5.cloned.1.call-update
  56.3 0.6 dynamic-slice
  57.6 0.9 dynamic-slice_dynamic-update-slice_fusion
  58.4 17.9 %all-reduce = f32[512]{0:T(512)S(1)} all-reduce(f32[512]{0:T(512)S(1)} %dynamic-slice_dynamic-update-slice_fusion), channel_id=1, replica_groups=mesh['z'=8,'x'=4,'y'=4,'c'=2] {'z'}, use_global_device_ids=true, to_apply=%add | all-reduce | flops 512 | bytes 4096
  76.3 0.0 all-gather.3.cloned.1.call-done
  76.4 43.7 %all-to-all-done = bf16[32,40,2048]{2,1,0:T(8,128)(2,1)} async-done(((bf16[32,40,2048]{2,1,0:T(8,128)(2,1)}), bf16[32,40,2048]{2,1,0:T(8,128)(2,1)}, u32[]{:S(2)}, u32[]{:S(2)}) %all-to-all-start) | async-done | bytes 5242912 | tf_op jit(solution)/shard_map/all_to_all | solution.py:70
  120.1 7.6 %convolution_add_fusion = f32[1280,512]{1,0:T(8,128)} fusion(bf16[1280,2048]{1,0:T(8,128)(2,1)} %bitcast.4, bf16[512,2048]{1,0:T(8,128)(2,1)} %bitcast.86, f32[512]{0:T(512)S(1)} %all-reduce), kind=kOutput, calls=%fused_computation.13 | convolution fusion | flops 2685009920 | bytes 9963520 | tf_op jit(solution)/shard_map/dot_general | solution.py:33
  127.7 7.6 %convolution_convert_fusion = bf16[1280,2048]{1,0:T(8,128)(2,1)} fusion(bf16[512,2048]{1,0:T(8,128)(2,1)} %bitcast.87, f32[1280,512]{1,0:T(8,128)} %convolution_add_fusion, s32[512]{0:T(512)S(1)} %get-tuple-element.38, s32[512]{0:T(512)S(1)} %get-tuple-element.39, pred[512]{0:T(512)(128)(4,1)S(1)} %fusion.38, s32[1280]{0:T(1024)S(1)} %get-tuple-element.36, ...), kind=kOutput, calls=%fused_computation | convolution fusion | flops 2700738560 | bytes 9977600 | tf_op jit(solution)/shard_map/dot_general | solution.py:33
  135.2 10.0 %all-to-all-start.3 = ((bf16[32,40,2048]{2,1,0:T(8,128)(2,1)}), bf16[32,40,2048]{2,1,0:T(8,128)(2,1)}, u32[]{:S(2)}, u32[]{:S(2)}) async-start(bf16[32,40,2048]{2,1,0:T(8,128)(2,1)} %bitcast.75), calls=%async_computation.3 | async-start | bytes 10485760 | tf_op jit(solution)/shard_map/all_to_all | solution.py:70
  145.2 0.9 fusion
  146.1 0.7 and.50
  146.8 63.0 %all-to-all-done.3 = bf16[32,40,2048]{2,1,0:T(8,128)(2,1)} async-done(((bf16[32,40,2048]{2,1,0:T(8,128)(2,1)}), bf16[32,40,2048]{2,1,0:T(8,128)(2,1)}, u32[]{:S(2)}, u32[]{:S(2)}) %all-to-all-start.3) | async-done | bytes 5242912 | tf_op jit(solution)/shard_map/all_to_all | solution.py:70
  209.8 9.6 %fusion.25 = bf16[32,40,2048]{2,1,0:T(8,128)(2,1)} fusion(pred[32,40,512]{2,1,0:T(8,128)(4,1)} %copy-done.4, bf16[512,2048]{1,0:T(8,128)(2,1)} %param.9, pred[1280,512]{1,0:T(32,128)(4,1)S(1)} %and.50, bf16[1280,2048]{1,0:T(8,128)(2,1)} %bitcast.16), kind=kOutput, calls=%fused_computation.43 | convolution fusion | flops 5371854848 | bytes 13893632 | tf_op jit(solution)/shard_map/dot_general | solution.py:33
  219.4 69.9 %all_to_all.99 = bf16[32,40,2048]{2,1,0:T(8,128)(2,1)} all-to-all(bf16[32,40,2048]{2,1,0:T(8,128)(2,1)} %fusion.25), channel_id=1, replica_groups=mesh['z'=8,'x'=4,'y'=4,'c'=2] {'x','y','c'}, dimensions={0} | all-to-all | bytes 10485760 | tf_op jit(solution)/shard_map/all_to_all | solution.py:70
  289.3 13.5 %convolution_convert_fusion.2 = bf16[512,2048]{1,0:T(8,128)(2,1)} fusion(bf16[1280,2048]{1,0:T(8,128)(2,1)} %bitcast.4, bf16[1280,2048]{1,0:T(8,128)(2,1)} %bitcast.73, bf16[512,2048]{1,0:T(8,128)(2,1)S(1)} %bitcast.88, f32[1280,512]{1,0:T(8,128)} %convolution_add_fusion, s32[512]{0:T(512)S(1)} %get-tuple-element.38, s32[512]{0:T(512)S(1)} %get-tuple-element.39, ...), kind=kOutput, calls=%fused_computation.16 | convolution fusion | flops 5389418496 | bytes 17317632 | tf_op jit(solution)/shard_map/dot_general | solution.py:33
  302.8 8.2 %all-to-all-start.5 = ((bf16[8,64,2048]{2,1,0:T(8,128)(2,1)}), bf16[8,64,2048]{2,1,0:T(8,128)(2,1)S(1)}, u32[]{:S(2)}, u32[]{:S(2)}) async-start(bf16[8,64,2048]{2,1,0:T(8,128)(2,1)} %bitcast.79), calls=%async_computation.5 | async-start | bytes 4194304 | tf_op jit(solution)/shard_map/all_to_all | solution.py:96
  311.0 8.4 %convolution_convert_fusion.1 = bf16[512,2048]{1,0:T(8,128)(2,1)} fusion(bf16[1280,2048]{1,0:T(8,128)(2,1)} %bitcast.74, f32[1280,512]{1,0:T(8,128)} %convolution_add_fusion, s32[512]{0:T(512)S(1)} %get-tuple-element.38, s32[512]{0:T(512)S(1)} %get-tuple-element.39, pred[512]{0:T(512)(128)(4,1)S(1)} %fusion.38, s32[1280]{0:T(1024)S(1)} %get-tuple-element.36, ...), kind=kOutput, calls=%fused_computation.15 | convolution fusion | flops 2699165696 | bytes 9977600 | tf_op jit(solution)/shard_map/dot_general | solution.py:33
  319.3 39.9 %all-to-all-done.5 = bf16[8,64,2048]{2,1,0:T(8,128)(2,1)S(1)} async-done(((bf16[8,64,2048]{2,1,0:T(8,128)(2,1)}), bf16[8,64,2048]{2,1,0:T(8,128)(2,1)S(1)}, u32[]{:S(2)}, u32[]{:S(2)}) %all-to-all-start.5) | async-done | bytes 2097184 | tf_op jit(solution)/shard_map/all_to_all | solution.py:96
  359.2 4.8 %all-to-all-start.7 = ((bf16[8,64,2048]{2,1,0:T(8,128)(2,1)}), bf16[8,64,2048]{2,1,0:T(8,128)(2,1)}, u32[]{:S(2)}, u32[]{:S(2)}) async-start(bf16[8,64,2048]{2,1,0:T(8,128)(2,1)} %bitcast.78), calls=%async_computation.7 | async-start | bytes 4194304 | tf_op jit(solution)/shard_map/all_to_all | solution.py:96
  364.0 0.3 convert_reduce_fusion.1
  364.4 0.8 copy.87
  365.2 47.6 %all-to-all-done.7 = bf16[8,64,2048]{2,1,0:T(8,128)(2,1)} async-done(((bf16[8,64,2048]{2,1,0:T(8,128)(2,1)}), bf16[8,64,2048]{2,1,0:T(8,128)(2,1)}, u32[]{:S(2)}, u32[]{:S(2)}) %all-to-all-start.7) | async-done | bytes 2097184 | tf_op jit(solution)/shard_map/all_to_all | solution.py:96
  412.9 6.8 %all-to-all-start.6 = ((f32[64,8,256]{2,0,1:T(8,128)}), f32[64,8,256]{2,0,1:T(8,128)S(1)}, u32[]{:S(2)}, u32[]{:S(2)}) async-start(f32[64,8,256]{2,0,1:T(8,128)} %bitcast.72), calls=%async_computation.6 | async-start | bytes 1048576 | tf_op jit(solution)/shard_map/all_to_all | solution.py:98
  419.7 2.1 convert_reduce_fusion
  421.8 0.8 copy.86
  422.6 6.6 %all-to-all-done.6 = f32[64,8,256]{2,0,1:T(8,128)S(1)} async-done(((f32[64,8,256]{2,0,1:T(8,128)}), f32[64,8,256]{2,0,1:T(8,128)S(1)}, u32[]{:S(2)}, u32[]{:S(2)}) %all-to-all-start.6) | async-done | bytes 524320 | tf_op jit(solution)/shard_map/all_to_all | solution.py:98
  429.2 4.3 all-to-all-start.8
  433.5 1.0 copy.63
  434.5 1.0 copy.72
  435.4 2.5 multiply_subtract_fusion.1
  437.9 2.1 copy.75
  440.0 1.0 copy.76
  441.0 1.0 copy.77
  442.0 0.9 all-to-all-done.8
  443.0 1.3 multiply_subtract_fusion
  (34 shorter events, 0.2 us)
Async XLA Ops:
  7.2 9.8 %copy-start.2 = (f32[512,256]{1,0:T(8,128)S(1)}, f32[512,256]{1,0:T(8,128)}, u32[]{:S(2)}) copy-start(f32[512,256]{1,0:T(8,128)} %param.13) | copy-start | bytes 1572868
  9.2 13.1 %all-to-all-start.1 = ((bf16[8,64,256]{2,1,0:T(8,128)(2,1)}), bf16[8,64,256]{2,1,0:T(8,128)(2,1)S(1)}, u32[]{:S(2)}, u32[]{:S(2)}) async-start(bf16[8,64,256]{2,1,0:T(8,128)(2,1)} %bitcast.6), calls=%async_computation.1 | async-start | bytes 524288 | tf_op jit(solution)/shard_map/all_to_all | solution.py:57
  22.3 26.2 %all-to-all-start.2 = ((bf16[8,64,256]{2,1,0:T(8,128)(2,1)}), bf16[8,64,256]{2,1,0:T(8,128)(2,1)S(1)}, u32[]{:S(2)}, u32[]{:S(2)}) async-start(bf16[8,64,256]{2,1,0:T(8,128)(2,1)} %bitcast.11), calls=%async_computation.2 | async-start | bytes 524288 | tf_op jit(solution)/shard_map/all_to_all | solution.py:57
  26.6 49.7 %all-gather.3.cloned.1.call-start = ((), (), s32[]{:S(2)}) async-start(), calls=%async_computation.9 | async-start | bytes 2359296 | tf_op jit(solution)/shard_map/all_gather | solution.py:58
  28.2 0.8 copy-start
  41.2 2.7 copy-start.9
  43.0 0.8 copy-start.4
  48.5 7.8 %copy-start.11 = (u32[256]{0:T(256)S(1)}, u32[256]{0:T(256)}, u32[]{:S(2)}) copy-start(u32[256]{0:T(256)} %constant.103) | copy-start | bytes 3076
  48.5 71.6 %all-to-all-start = ((bf16[32,40,2048]{2,1,0:T(8,128)(2,1)}), bf16[32,40,2048]{2,1,0:T(8,128)(2,1)}, u32[]{:S(2)}, u32[]{:S(2)}) async-start(bf16[32,40,2048]{2,1,0:T(8,128)(2,1)} %fusion.18), calls=%async_computation | async-start | bytes 10485760 | tf_op jit(solution)/shard_map/all_to_all | solution.py:70
  55.5 72.2 %all-gather.5.cloned.1.call-start = ((), (), s32[]{:S(2)}) async-start(), calls=%async_computation.10 | async-start | bytes 2359296 | tf_op jit(solution)/shard_map/all_gather | solution.py:58
  135.2 10.0 %copy-start.1 = (s32[256,512]{1,0:T(8,128)S(1)}, s32[256,512]{1,0:T(8,128)}, u32[]{:S(2)}) copy-start(s32[256,512]{1,0:T(8,128)} %copy-done) | copy-start | bytes 1572868
  135.2 74.6 %all-to-all-start.3 = ((bf16[32,40,2048]{2,1,0:T(8,128)(2,1)}), bf16[32,40,2048]{2,1,0:T(8,128)(2,1)}, u32[]{:S(2)}, u32[]{:S(2)}) async-start(bf16[32,40,2048]{2,1,0:T(8,128)(2,1)} %bitcast.75), calls=%async_computation.3 | async-start | bytes 10485760 | tf_op jit(solution)/shard_map/all_to_all | solution.py:70
  219.4 69.9 %copy-start.10 = (bf16[8,64,2048]{2,1,0:T(8,128)(2,1)S(1)}, bf16[8,64,2048]{2,1,0:T(8,128)(2,1)}, u32[]{:S(2)}) copy-start(bf16[8,64,2048]{2,1,0:T(8,128)(2,1)} %all-gather.5.cloned.1.call-done) | copy-start | bytes 6291460
  302.8 56.4 %all-to-all-start.5 = ((bf16[8,64,2048]{2,1,0:T(8,128)(2,1)}), bf16[8,64,2048]{2,1,0:T(8,128)(2,1)S(1)}, u32[]{:S(2)}, u32[]{:S(2)}) async-start(bf16[8,64,2048]{2,1,0:T(8,128)(2,1)} %bitcast.79), calls=%async_computation.5 | async-start | bytes 4194304 | tf_op jit(solution)/shard_map/all_to_all | solution.py:96
  359.2 53.7 %all-to-all-start.7 = ((bf16[8,64,2048]{2,1,0:T(8,128)(2,1)}), bf16[8,64,2048]{2,1,0:T(8,128)(2,1)}, u32[]{:S(2)}, u32[]{:S(2)}) async-start(bf16[8,64,2048]{2,1,0:T(8,128)(2,1)} %bitcast.78), calls=%async_computation.7 | async-start | bytes 4194304 | tf_op jit(solution)/shard_map/all_to_all | solution.py:96
  412.9 16.3 %all-to-all-start.6 = ((f32[64,8,256]{2,0,1:T(8,128)}), f32[64,8,256]{2,0,1:T(8,128)S(1)}, u32[]{:S(2)}, u32[]{:S(2)}) async-start(f32[64,8,256]{2,0,1:T(8,128)} %bitcast.72), calls=%async_computation.6 | async-start | bytes 1048576 | tf_op jit(solution)/shard_map/all_to_all | solution.py:98
  419.7 13.8 %copy-start.7 = (f32[256,512]{1,0:T(8,128)S(1)}, f32[256,512]{1,0:T(8,128)}, u32[]{:S(2)}) copy-start(f32[256,512]{1,0:T(8,128)} %param.14) | copy-start | bytes 1572868
  419.7 14.8 %copy-start.8 = (f32[256,512]{1,0:T(8,128)S(1)}, f32[256,512]{1,0:T(8,128)}, u32[]{:S(2)}) copy-start(f32[256,512]{1,0:T(8,128)} %param.15) | copy-start | bytes 1572868
  429.2 13.8 %all-to-all-start.8 = ((f32[64,8,256]{2,0,1:T(8,128)}), f32[64,8,256]{2,0,1:T(8,128)S(1)}, u32[]{:S(2)}, u32[]{:S(2)}) async-start(f32[64,8,256]{2,0,1:T(8,128)} %bitcast.71), calls=%async_computation.8 | async-start | bytes 1048576 | tf_op jit(solution)/shard_map/all_to_all | solution.py:98
  435.4 7.5 %copy-start.3 = (f32[512,256]{1,0:T(8,128)S(1)}, f32[512,256]{1,0:T(8,128)}, u32[]{:S(2)}) copy-start(f32[512,256]{1,0:T(8,128)} %param.13) | copy-start | bytes 1572868
  437.9 5.1 %copy-start.5 = (f32[512,256]{1,0:T(8,128)S(1)}, f32[512,256]{1,0:T(8,128)}, u32[]{:S(2)}) copy-start(f32[512,256]{1,0:T(8,128)} %param.16) | copy-start | bytes 1572868
  437.9 5.1 %copy-start.6 = (f32[512,256]{1,0:T(8,128)S(1)}, f32[512,256]{1,0:T(8,128)}, u32[]{:S(2)}) copy-start(f32[512,256]{1,0:T(8,128)} %param.17) | copy-start | bytes 1572868
Sparse Core Ops, SparseCore 0:
  29.8 39.4 all-gather.2
  71.7 39.8 all-gather.4

commit v2 on v1

v2 whole, which is shorter than its diff:
```python
import jax
import jax.numpy as jnp
from jax import lax
from jax.experimental import pallas as pl
from jax.experimental.pallas import tpu as pltpu
from jax.sharding import Mesh, PartitionSpec as P

BLOCK = 64
CAP = 5
LANES = 128
HOMES = 16
VMEM = 56 * 2**20

learn_rate = 0.001
adam_eps = 1e-08
first_fix = 1.0 - 0.9**10
second_fix = 1.0 - 0.95**10

REP = ("y", "c")
CHIPS = ("y", "x")


def adam(master, gradient, first, second):
    first_new = 0.9 * first + 0.1 * gradient
    second_new = 0.95 * second + 0.05 * gradient * gradient
    update = first_new / first_fix / (jnp.sqrt(second_new / second_fix) + adam_eps)
    return (master - learn_rate * update, first_new, second_new)


def dot(a, b, ca, cb):
    return lax.dot_general(a, b, (((ca,), (cb,)), ((), ())), preferred_element_type=jnp.float32)


def low_lanes(shape):
    return lax.broadcasted_iota(jnp.int32, shape, 1) < BLOCK


def split_pair(pair):
    low = low_lanes(pair.shape)
    zero = jnp.zeros_like(pair)
    return jnp.concatenate([jnp.where(low, pair, zero), jnp.where(low, zero, pair)], axis=0)


def join_pair(both):
    half = both.shape[0] // 2
    return jnp.where(low_lanes((half, LANES)), both[:half], both[half:])


def gather_onehot(pos_ref, home, slot, blocks, tok):
    rows = lax.broadcasted_iota(jnp.int32, (blocks, tok), 0) + slot * blocks
    first, second = pos_ref[home, 0:1, :], pos_ref[home, 1:2, :]
    return jnp.where((rows == first) | (rows == second), 1.0, 0.0).astype(jnp.bfloat16)


def scatter_onehot(col_ref, home, slot, blocks, tok):
    cols = lax.broadcasted_iota(jnp.int32, (tok, blocks), 1) + slot * blocks
    first, second = col_ref[home, :, 0:1], col_ref[home, :, 1:2]
    return jnp.where((cols == first) | (cols == second), 1.0, 0.0).astype(jnp.bfloat16)


def encode_kernel(tok_ref, pos_ref, enc_ref, pre_ref, rows_ref, held):
    tok = tok_ref.shape[0] // HOMES
    blocks = enc_ref.shape[0] // BLOCK
    per = CAP * HOMES

    @pl.loop(0, HOMES)
    def _(home):
        mine = tok_ref[pl.ds(pl.multiple_of(home * tok, tok), tok), :]
        for slot in range(CAP):
            picked = dot(gather_onehot(pos_ref, home, slot, blocks, tok), mine, 1, 0)
            held[pl.ds(slot * HOMES + home, blocks, per), :] = picked

    @pl.loop(0, blocks // 2, unroll=4)
    def _(pair):
        both = pl.ds(pl.multiple_of(pair * 2 * per, 2 * per), 2 * per)
        rows = held[both, :].astype(jnp.bfloat16)
        rows_ref[both, :] = rows
        weight = enc_ref[pl.ds(pl.multiple_of(pair * LANES, LANES), LANES), :]
        out = join_pair(dot(rows, weight, 1, 1)).astype(jnp.bfloat16)
        pre_ref[pl.ds(pl.multiple_of(pair * per, per), per), :] = out


def decode_kernel(code_ref, dec_ref, tok_ref, pos_ref, col_ref, cgrad_ref, dgrad_ref, held):
    tok = tok_ref.shape[0] // HOMES
    blocks = dec_ref.shape[0] // BLOCK
    per = CAP * HOMES

    @pl.loop(0, blocks // 2, unroll=4)
    def _(pair):
        both = pl.ds(pl.multiple_of(pair * 2 * per, 2 * per), 2 * per)
        code = split_pair(code_ref[pl.ds(pl.multiple_of(pair * per, per), per), :])
        weight = dec_ref[pl.ds(pl.multiple_of(pair * LANES, LANES), LANES), :]
        held[both, :] = dot(code, weight, 1, 0)

    @pl.loop(0, HOMES)
    def _(home):
        mine = tok_ref[pl.ds(pl.multiple_of(home * tok, tok), tok), :]
        rebuilt = jnp.zeros((tok, LANES), jnp.float32)
        for slot in range(CAP):
            part = held[pl.ds(slot * HOMES + home, blocks, per), :].astype(jnp.bfloat16)
            rebuilt += dot(scatter_onehot(col_ref, home, slot, blocks, tok), part, 1, 0)
        err = (rebuilt - mine.astype(jnp.float32)).astype(jnp.bfloat16)
        for slot in range(CAP):
            picked = dot(gather_onehot(pos_ref, home, slot, blocks, tok), err, 1, 0)
            held[pl.ds(slot * HOMES + home, blocks, per), :] = picked

    @pl.loop(0, blocks // 2, unroll=4)
    def _(pair):
        both = pl.ds(pl.multiple_of(pair * 2 * per, 2 * per), 2 * per)
        own = pl.ds(pl.multiple_of(pair * per, per), per)
        lanes = pl.ds(pl.multiple_of(pair * LANES, LANES), LANES)
        err = held[both, :].astype(jnp.bfloat16)
        cgrad_ref[own, :] = join_pair(dot(err, dec_ref[lanes, :], 1, 1)).astype(jnp.bfloat16)
        dgrad_ref[lanes, :] = dot(split_pair(code_ref[own, :]), err, 0, 0).astype(jnp.bfloat16)


def enc_grad_kernel(pgrad_ref, rows_ref, egrad_ref):
    per = CAP * HOMES

    @pl.loop(0, pgrad_ref.shape[0] // per, unroll=4)
    def _(pair):
        both = pl.ds(pl.multiple_of(pair * 2 * per, 2 * per), 2 * per)
        own = pl.ds(pl.multiple_of(pair * per, per), per)
        lanes = pl.ds(pl.multiple_of(pair * LANES, LANES), LANES)
        out = dot(split_pair(pgrad_ref[own, :]), rows_ref[both, :], 0, 0)
        egrad_ref[lanes, :] = out.astype(jnp.bfloat16)


def call(kernel, outs, scratch, name, *args):
    whole = pl.BlockSpec(memory_space=pltpu.VMEM)
    return pl.pallas_call(
        kernel,
        out_shape=[jax.ShapeDtypeStruct(s, jnp.bfloat16) for s in outs],
        in_specs=[whole] * len(args),
        out_specs=[whole] * len(outs),
        scratch_shapes=scratch,
        compiler_params=pltpu.CompilerParams(vmem_limit_bytes=VMEM),
        name=name,
    )(*args)


def local(
    tokens,
    block_ids,
    enc_bias,
    enc_master,
    dec_master,
    enc_first,
    enc_second,
    dec_first,
    dec_second,
):
    nz, nx = lax.axis_size("z"), lax.axis_size("x")
    ny, nc = lax.axis_size("y"), lax.axis_size("c")
    tok, width = tokens.shape
    lat, part = dec_master.shape
    blocks = lat // BLOCK * nz * nx
    half = lat // nc
    me = lax.axis_index("y") * nx + lax.axis_index("x")

    def spread(w):
        w = w.reshape(nc, half, part)
        w = lax.all_to_all(w, "c", split_axis=0, concat_axis=2, tiled=True)
        w = w.reshape(half, nx, LANES)
        w = lax.all_to_all(w, "x", split_axis=1, concat_axis=0, tiled=True)
        return lax.all_gather(w.reshape(nx * half, LANES), ("z", "c"), axis=0, tiled=True)

    per_half = half // BLOCK
    local_b = block_ids % (nc * per_half)
    shard = block_ids // (nc * per_half)
    place = (
        ((shard // nx) * nc + local_b // per_half) * nx + shard % nx
    ) * per_half + local_b % per_half
    nums = jnp.arange(blocks, dtype=jnp.int32)[:, None]
    named = [nums == place[:, k][None, :] for k in range(2)]
    count = jnp.cumsum((named[0] | named[1]).astype(jnp.int32), axis=1) - 1
    rank = jnp.stack([jnp.sum(jnp.where(n, count, 0), axis=0) for n in named])
    pos = lax.all_gather(rank * blocks + place.T, CHIPS, axis=0)
    col = pos.transpose(0, 2, 1)

    slices = tokens.reshape(tok, HOMES, LANES).transpose(1, 0, 2)
    slices = lax.all_to_all(slices, CHIPS, split_axis=0, concat_axis=0, tiled=True)
    slices = slices.reshape(HOMES * tok, LANES)

    enc = spread(enc_master.astype(jnp.bfloat16).T)
    dec = spread(dec_master.astype(jnp.bfloat16))
    bias = lax.all_gather(enc_bias, ("z", "x"), axis=0, tiled=True)
    bias = bias.reshape(nz, nx, nc, half).transpose(0, 2, 1, 3).reshape(HOMES, -1, 1, LANES)
    bias = lax.dynamic_index_in_dim(bias, me, 0, keepdims=False)

    per = CAP * HOMES
    codes = (blocks // 2 * per, LANES)
    held = [pltpu.VMEM((blocks * per, LANES), jnp.float32)]
    pre, rows = call(encode_kernel, [codes, (blocks * per, LANES)], held, "encode", slices, pos, enc)

    def reduce_own(partial):
        got = lax.all_to_all(
            partial.reshape(HOMES, -1, per, LANES), CHIPS, split_axis=0, concat_axis=0, tiled=True
        )
        return jnp.sum(got.astype(jnp.float32), axis=0)

    def share(own):
        return lax.all_gather(own, CHIPS, axis=0, tiled=True).reshape(codes)

    preact = reduce_own(pre) + bias
    values, slopes = jax.jvp(
        lambda inner: jax.nn.gelu(inner, approximate=True), (preact,), (jnp.ones_like(preact),)
    )
    coded = share(values.astype(jnp.bfloat16))
    cgrad, dgrad = call(
        decode_kernel,
        [codes, (blocks * BLOCK, LANES)],
        held,
        "decode",
        coded,
        dec,
        slices,
        pos,
        col,
    )
    pgrad = share((reduce_own(cgrad) * slopes).astype(jnp.bfloat16))
    (egrad,) = call(enc_grad_kernel, [(blocks * BLOCK, LANES)], [], "enc_grad", pgrad, rows)

    def collect(g):
        g = g.reshape(nz, nc, nx * half, LANES)
        g = lax.all_to_all(g, "c", split_axis=1, concat_axis=0, tiled=True).reshape(
            nc, nz, nx * half, LANES
        )
        g = jnp.sum(g.astype(jnp.float32), axis=0).astype(jnp.bfloat16)
        g = lax.all_to_all(g, "z", split_axis=0, concat_axis=0, tiled=True)
        g = jnp.sum(g.astype(jnp.float32), axis=0).reshape(nx, half, LANES)
        g = lax.all_to_all(g, "x", split_axis=0, concat_axis=2, tiled=True)
        g = g.reshape(1, half, nc, part)
        g = lax.all_to_all(g, "c", split_axis=2, concat_axis=0, tiled=True)
        return g.reshape(lat, part)

    dec_share = collect(dgrad)
    enc_share = collect(egrad).T
    enc_new, enc_first_new, enc_second_new = adam(enc_master, enc_share, enc_first, enc_second)
    dec_new, dec_first_new, dec_second_new = adam(dec_master, dec_share, dec_first, dec_second)
    return (enc_new, dec_new, enc_first_new, enc_second_new, dec_first_new, dec_second_new)


def solution(mesh):
    grid = Mesh(mesh.devices.reshape(8, 4, 4, 2), ("z", "x", "y", "c"))
    lat, rep = ("z", "x"), REP
    tok = P(rep + lat, None)
    enc, dec = P(rep, lat), P(lat, rep)
    return jax.shard_map(
        local,
        mesh=grid,
        in_specs=(tok, tok, P(lat), enc, dec, enc, enc, dec, dec),
        out_specs=(enc, dec, enc, enc, dec, dec),
        check_vma=False,
    )
```

time: 452 us -> 550 us (1.22)
  blocking collectives: 87.8 us -> 249 us
  waiting for transfers between devices: 206 us -> 114 us
  Pallas kernels: 0 us -> 89.9 us
  matrix products: 51.2 us -> 0 us
  starting transfers between devices: 52.1 us -> 25.9 us
  other arithmetic: 11.8 us -> 25.1 us
    all_to_all x6 -> x5, waiting for transfers between devices: 119 us -> 6.7 us  [the longest x2 6.43 us: collect(): g = lax.all_to_all(g, 'x', split_axis=0, concat_axis=2, tiled=True)]
    all_gather x0 -> x2, blocking collectives: none -> 99.5 us  [the longest x1 64.9 us: local(): bias = lax.all_gather(enc_bias, ('z', 'x'), axis=0, tiled=True)]
    pallas_call x0 -> x3, Pallas kernels: none -> 89.9 us  [call(): pl.pallas_call(kernel, out_shape=[jax.ShapeDtypeStruct(s, jnp.bfloat16) f...]
    all_to_all x1 -> x9, blocking collectives: 69.9 us -> 150 us  [the longest x1 57.6 us: collect(): g = lax.all_to_all(g, 'z', split_axis=0, concat_axis=0, tiled=True)]
    all_gather x2 -> x4, waiting for transfers between devices: 0.02 us -> 59.8 us  [the longest x2 59.8 us: share(): return lax.all_gather(own, CHIPS, axis=0, tiled=True).reshape(codes)]
    dot_general x6 -> x0, matrix products: 51.2 us -> none  [dot(): lax.dot_general(a, b, (((ca,), (cb,)), ((), ())), preferred_element_type=...]
    all_to_all x2 -> x1, waiting for transfers between devices: 87.5 us -> 47.3 us  [collect(): g = lax.all_to_all(g, 'z', split_axis=0, concat_axis=0, tiled=True)]
    unnamed x1 -> x0, blocking collectives: 17.9 us -> none
  transfers between devices with their start and end apart: 10 -> 10, of which waited for: 7 -> 5; matrix products, arithmetic and copies ran while one was open for 12% -> 6% of each run, Pallas kernels for 0% -> 4%
where the time goes in v2:
time: 550 us; the launch traced here: 548 us
  blocking collectives  249 us (45%)
  waiting for transfers between devices  114 us (21%)
  Pallas kernels  89.9 us (16%)
  local copies, waits for them, and re-layouts  30.2 us (5%)
  starting transfers between devices  25.9 us (5%)
  other arithmetic  25.1 us (5%)
  between operations  14.1 us (3%)
    pallas_call x3, Pallas kernels, call(): pl.pallas_call(kernel, out_shape=[jax.ShapeDtypeStruct(s, jnp.bfloat16) f...  89.9 us
    all_gather x1, blocking collectives, local(): bias = lax.all_gather(enc_bias, ('z', 'x'), axis=0, tiled=True)  64.9 us
    all_gather x2, waiting for transfers between devices, share(): return lax.all_gather(own, CHIPS, axis=0, tiled=True).reshape(codes)  59.8 us
    all_to_all x1, blocking collectives, collect(): g = lax.all_to_all(g, 'z', split_axis=0, concat_axis=0, tiled=True)  57.6 us
    all_to_all x1, waiting for transfers between devices, collect(): g = lax.all_to_all(g, 'z', split_axis=0, concat_axis=0, tiled=True)  47.3 us
    all_to_all x1, blocking collectives, reduce_own(): lax.all_to_all(partial.reshape(HOMES, -1, per, LANES), CHIPS, split_axis=...  36.5 us
    all_gather x1, blocking collectives, local(): pos = lax.all_gather(rank * blocks + place.T, CHIPS, axis=0)  34.7 us
    all_to_all x2, blocking collectives, collect(): lax.all_to_all(g, 'c', split_axis=1, concat_axis=0, tiled=True)  19.6 us
  transfers between devices with their start and end apart: 10, of which 5 were waited for; matrix products, arithmetic and copies ran while one was open for 6% of the time, Pallas kernels for 4%

profile of v2, /device:TPU:1, one launch (start us, length us, event | category | flops | bytes accessed | tf_op | source)
XLA Modules:
  0.0 548.1 jit_solution(7206721276624357773)
XLA Ops:
  7.2 1.4 copy.117
  8.7 6.8 %all_to_all.163 = bf16[2,256,256]{2,1,0:T(8,128)(2,1)S(1)} all-to-all(bf16[2,256,256]{2,1,0:T(8,128)(2,1)S(1)} %bitcast.100), channel_id=1, replica_groups=mesh['z'=8,'x'=4,'y'=4,'c'=2] {'c'}, dimensions={0} | all-to-all | bytes 524288 | tf_op jit(solution)/shard_map/all_to_all | solution.py:163
  15.5 0.8 copy.106
  16.4 9.8 %all_to_all.164 = bf16[256,4,128]{0,2,1:T(8,128)(2,1)S(1)} all-to-all(bf16[256,4,128]{0,2,1:T(8,128)(2,1)} %bitcast.105), channel_id=1, replica_groups=mesh['z'=8,'x'=4,'y'=4,'c'=2] {'x'}, dimensions={1} | all-to-all | bytes 524288 | tf_op jit(solution)/shard_map/all_to_all | solution.py:165
  26.2 0.8 copy.107
  27.1 4.8 all_to_all.165
  31.9 0.1 copy.109
  32.0 8.8 %all_to_all.166 = bf16[256,4,128]{0,2,1:T(8,128)(2,1)S(1)} all-to-all(bf16[256,4,128]{0,2,1:T(8,128)(2,1)S(1)} %bitcast.108), channel_id=1, replica_groups=mesh['z'=8,'x'=4,'y'=4,'c'=2] {'x'}, dimensions={1} | all-to-all | bytes 524288 | tf_op jit(solution)/shard_map/all_to_all | solution.py:165
  40.9 0.8 copy.110
  41.7 1.9 bitcast_bitcast_fusion
  43.6 3.9 all-to-all-start
  47.6 0.1 fusion.24
  47.7 0.1 copy.101
  47.8 0.1 copy.102
  47.9 0.3 fusion.4
  48.3 4.8 select_reduce_fusion.1
  53.1 0.1 copy.103
  53.2 0.1 copy.104
  53.3 0.1 fusion.26
  53.3 34.7 %all-gather.1.pos_ref = s32[16,2,512]{2,1,0:T(2,128)} all-gather(s32[1,2,512]{2,1,0:T(2,128)S(1)} %fusion.26), channel_id=2, replica_groups=mesh['z'=8,'x'=4,'y'=4,'c'=2] {'y','x'}, dimensions={0}, use_global_device_ids=true | all-gather | bytes 69632 | tf_op jit(solution)/shard_map/all_gather | solution.py:178
  88.0 1.3 copy-done.2
  89.4 23.5 %encode.1 = (bf16[10240,128]{1,0:T(8,128)(2,1)}, bf16[20480,128]{1,0:T(8,128)(2,1)}) custom-call(bf16[8192,128]{1,0:T(8,128)(2,1)} %bitcast.87, s32[16,2,512]{2,1,0:T(2,128)} %all-gather.1.pos_ref, bf16[16384,128]{1,0:T(8,128)(2,1)} %all-gather.8.cloned.1.call-done.enc_ref), custom_call_target="tpu_custom_call" | custom-call | tf_op jit(solution)/shard_map/encode/pallas_call | solution.py:131
  112.9 5.1 all-to-all-start.3
  118.1 64.9 %all-gather.2 = f32[32,1,512]{2,1,0:T(1,128)S(1)} all-gather(f32[1,1,512]{2,1,0:T(1,128)S(1)} %bitcast.115), channel_id=1, replica_groups=mesh['z'=8,'x'=4,'y'=4,'c'=2] {'z','x'}, dimensions={0}, use_global_device_ids=true | all-gather | bytes 67584 | tf_op jit(solution)/shard_map/all_gather | solution.py:187
  183.0 0.2 reduce.10
  183.3 2.1 convert_reduce_fusion.1
  185.4 0.8 multiply_convert_fusion
  186.3 2.6 copy.111
  188.9 59.8 %all-gather.10.cloned.1.call-done = bf16[128,80,128]{2,1,0:T(8,128)(2,1)} async-done(((bf16[8,80,128]{2,1,0:T(8,128)(2,1)}), bf16[128,80,128]{2,1,0:T(8,128)(2,1)}) %all-gather.10.cloned.1.call-update) | async-done | bytes 2621456 | tf_op jit(solution)/shard_map/all_gather | solution.py:203
  248.7 51.6 %decode.1 = (bf16[10240,128]{1,0:T(8,128)(2,1)}, bf16[16384,128]{1,0:T(8,128)(2,1)}) custom-call(bf16[10240,128]{1,0:T(8,128)(2,1)} %bitcast.95, bf16[16384,128]{1,0:T(8,128)(2,1)} %all-gather.12.cloned.1.call-done.dec_ref, bf16[8192,128]{1,0:T(8,128)(2,1)} %bitcast.88, s32[16,2,512]{2,1,0:T(2,128)} %all-gather.1.pos_ref, s32[16,512,2]{2,1,0:T(8,128)} %bitcast.89), custom_call_target="tpu_custom_call" | custom-call | tf_op jit(solution)/shard_map/decode/pallas_call | solution.py:131
  300.3 36.5 %all_to_all.167 = bf16[16,8,80,128]{3,2,1,0:T(8,128)(2,1)S(1)} all-to-all(bf16[16,8,80,128]{3,2,1,0:T(8,128)(2,1)} %bitcast.93), channel_id=1, replica_groups=mesh['z'=8,'x'=4,'y'=4,'c'=2] {'y','x'}, dimensions={0} | all-to-all | bytes 5242880 | tf_op jit(solution)/shard_map/all_to_all | solution.py:197
  336.8 0.4 convert_reduce_fusion
  337.2 0.9 fusion.19
  338.1 2.5 copy.118
  340.6 10.6 %all_to_all.168 = bf16[8,2,1024,128]{3,2,0,1:T(8,128)(2,1)} all-to-all(bf16[8,2,1024,128]{3,2,0,1:T(8,128)(2,1)S(1)} %copy.118), channel_id=1, replica_groups=mesh['z'=8,'x'=4,'y'=4,'c'=2] {'c'}, dimensions={1} | all-to-all | bytes 8388608 | tf_op jit(solution)/shard_map/all_to_all | solution.py:226
  351.2 3.2 reduce_sum.84
  354.4 57.6 %all_to_all.169 = bf16[8,1024,128]{2,1,0:T(8,128)(2,1)S(1)} all-to-all(bf16[8,1024,128]{2,1,0:T(8,128)(2,1)S(1)} %reduce_sum.84), channel_id=1, replica_groups=mesh['z'=8,'x'=4,'y'=4,'c'=2] {'z'}, dimensions={0} | all-to-all | bytes 4194304 | tf_op jit(solution)/shard_map/all_to_all | solution.py:230
  412.0 1.1 convert_reduce_fusion.2
  413.1 14.7 %enc_grad.1 = bf16[16384,128]{1,0:T(8,128)(2,1)} custom-call(bf16[10240,128]{1,0:T(8,128)(2,1)} %bitcast.94, bf16[20480,128]{1,0:T(8,128)(2,1)} %get-tuple-element.12.rows_ref), custom_call_target="tpu_custom_call" | custom-call | tf_op jit(solution)/shard_map/enc_grad/pallas_call | solution.py:131
  427.8 2.5 copy.112
  430.3 8.9 %all_to_all.170 = bf16[8,2,1024,128]{3,2,0,1:T(8,128)(2,1)} all-to-all(bf16[8,2,1024,128]{3,2,0,1:T(8,128)(2,1)S(1)} %copy.112), channel_id=1, replica_groups=mesh['z'=8,'x'=4,'y'=4,'c'=2] {'c'}, dimensions={1} | all-to-all | bytes 8388608 | tf_op jit(solution)/shard_map/all_to_all | solution.py:226
  439.3 3.5 all-to-all-start.13
  442.7 5.0 reduce_sum.82
  447.7 4.2 all-to-all-done.13
  451.9 3.6 all-to-all-start.8
  455.6 1.0 copy.119
  456.6 47.3 %all-to-all-done.8 = bf16[8,1024,128]{2,1,0:T(8,128)(2,1)S(1)} async-done(((bf16[8,1024,128]{2,1,0:T(8,128)(2,1)}), bf16[8,1024,128]{2,1,0:T(8,128)(2,1)S(1)}, u32[]{:S(2)}, u32[]{:S(2)}) %all-to-all-start.8) | async-done | bytes 2097184 | tf_op jit(solution)/shard_map/all_to_all | solution.py:230
  503.8 6.2 %all-to-all-start.14 = ((f32[1,256,2,256]{1,3,0,2:T(8,128)}), f32[1,256,2,256]{1,3,0,2:T(8,128)S(1)}, u32[]{:S(2)}, u32[]{:S(2)}) async-start(f32[1,256,2,256]{1,3,0,2:T(8,128)} %bitcast.98), calls=%async_computation.14 | async-start | bytes 1048576 | tf_op jit(solution)/shard_map/all_to_all | solution.py:234
  510.0 1.1 convert_reduce_fusion.3
  511.1 0.3 all-to-all-done.14
  511.4 0.8 copy-done.5
  512.2 3.5 all-to-all-start.9
  515.6 1.2 copy.116
  516.9 2.0 copy.99
  518.9 1.2 copy.121
  520.2 2.4 multiply_subtract_fusion
  522.6 2.2 all-to-all-done.9
  524.8 0.2 copy.113
  525.0 5.7 %all_to_all.171 = f32[1,256,2,256]{1,3,0,2:T(8,128)} all-to-all(f32[1,256,2,256]{1,3,0,2:T(8,128)S(1)} %bitcast.99), channel_id=1, replica_groups=mesh['z'=8,'x'=4,'y'=4,'c'=2] {'c'}, dimensions={2} | all-to-all | bytes 1048576 | tf_op jit(solution)/shard_map/all_to_all | solution.py:234
  530.8 2.2 copy.115
  533.0 2.5 multiply_subtract_fusion.1
  535.5 2.0 copy.122
  537.5 2.0 copy.123
  539.6 2.0 copy.124
  (41 shorter events, 0.5 us)
Async XLA Ops:
  7.2 34.6 %copy-start = (bf16[512,2048]{1,0:T(8,128)(2,1)S(1)}, bf16[512,2048]{1,0:T(8,128)(2,1)}, u32[]{:S(2)}) copy-start(bf16[512,2048]{1,0:T(8,128)(2,1)} %param.9) | copy-start | bytes 6291460
  7.2 19.9 %copy-start.3 = (f32[512,256]{1,0:T(8,128)S(1)}, f32[512,256]{1,0:T(8,128)}, u32[]{:S(2)}) copy-start(f32[512,256]{1,0:T(8,128)} %param.13) | copy-start | bytes 1572868
  7.2 80.8 %all-gather.8.cloned.1.call-start = ((), (), s32[]{:S(2)}) async-start(), calls=%async_computation.15 | async-start | bytes 4456448 | tf_op jit(solution)/shard_map/all_gather | solution.py:166
  27.0 161.9 %all-gather.12.cloned.1.call-start = ((), (), s32[]{:S(2)}) async-start(), calls=%async_computation.17 | async-start | bytes 4456448 | tf_op jit(solution)/shard_map/all_gather | solution.py:166
  43.6 3.9 copy-start.8
  43.6 44.4 %all-to-all-start = ((bf16[16,512,128]{2,1,0:T(8,128)(2,1)}), bf16[16,512,128]{2,1,0:T(8,128)(2,1)S(1)}, u32[]{:S(2)}, u32[]{:S(2)}) async-start(bf16[16,512,128]{2,1,0:T(8,128)(2,1)} %bitcast_bitcast_fusion), calls=%async_computation | async-start | bytes 4194304 | tf_op jit(solution)/shard_map/all_to_all | solution.py:182
  88.0 1.4 copy-start.2
  112.9 5.2 copy-start.9
  112.9 70.4 %all-to-all-start.3 = ((bf16[16,8,80,128]{3,2,1,0:T(8,128)(2,1)}), bf16[16,8,80,128]{3,2,1,0:T(8,128)(2,1)}, u32[]{:S(2)}, u32[]{:S(2)}) async-start(bf16[16,8,80,128]{3,2,1,0:T(8,128)(2,1)} %bitcast.92), calls=%async_computation.3 | async-start | bytes 5242880 | tf_op jit(solution)/shard_map/all_to_all | solution.py:197
  118.0 68.3 %copy-start.6 = (s32[16,2,512]{2,1,0:T(2,128)S(1)}, s32[16,2,512]{2,1,0:T(2,128)}, u32[]{:S(2)}) copy-start(s32[16,2,512]{2,1,0:T(2,128)} %all-gather.1.pos_ref) | copy-start | bytes 196612
  118.0 130.7 %all-gather.10.cloned.1.call-start = ((), (), s32[]{:S(2)}) async-start(), calls=%async_computation.16 | async-start | bytes 2785280 | tf_op jit(solution)/shard_map/all_gather | solution.py:203
  186.3 226.9 %all-gather.14.cloned.1.call-start = ((), (), s32[]{:S(2)}) async-start(), calls=%async_computation.18 | async-start | bytes 2785280 | tf_op jit(solution)/shard_map/all_gather | solution.py:203
  439.3 12.7 %all-to-all-start.13 = ((f32[4,256,128]{2,1,0:T(8,128)}), f32[4,256,128]{2,1,0:T(8,128)S(1)}, u32[]{:S(2)}, u32[]{:S(2)}) async-start(f32[4,256,128]{2,1,0:T(8,128)} %bitcast.46), calls=%async_computation.13 | async-start | bytes 1048576 | tf_op jit(solution)/shard_map/all_to_all | solution.py:232
  451.9 51.9 %all-to-all-start.8 = ((bf16[8,1024,128]{2,1,0:T(8,128)(2,1)}), bf16[8,1024,128]{2,1,0:T(8,128)(2,1)S(1)}, u32[]{:S(2)}, u32[]{:S(2)}) async-start(bf16[8,1024,128]{2,1,0:T(8,128)(2,1)} %reduce_sum.82), calls=%async_computation.8 | async-start | bytes 4194304 | tf_op jit(solution)/shard_map/all_to_all | solution.py:230
  503.8 7.5 %all-to-all-start.14 = ((f32[1,256,2,256]{1,3,0,2:T(8,128)}), f32[1,256,2,256]{1,3,0,2:T(8,128)S(1)}, u32[]{:S(2)}, u32[]{:S(2)}) async-start(f32[1,256,2,256]{1,3,0,2:T(8,128)} %bitcast.98), calls=%async_computation.14 | async-start | bytes 1048576 | tf_op jit(solution)/shard_map/all_to_all | solution.py:234
  511.1 9.1 %copy-start.4 = (f32[512,256]{1,0:T(8,128)S(1)}, f32[512,256]{1,0:T(8,128)}, u32[]{:S(2)}) copy-start(f32[512,256]{1,0:T(8,128)} %param.13) | copy-start | bytes 1572868
  511.1 9.1 %copy-start.7 = (f32[512,256]{1,0:T(8,128)S(1)}, f32[512,256]{1,0:T(8,128)}, u32[]{:S(2)}) copy-start(f32[512,256]{1,0:T(8,128)} %param.16) | copy-start | bytes 1572868
  511.4 0.8 copy-start.5
  512.2 12.7 %all-to-all-start.9 = ((f32[4,256,128]{2,1,0:T(8,128)}), f32[4,256,128]{2,1,0:T(8,128)S(1)}, u32[]{:S(2)}, u32[]{:S(2)}) async-start(f32[4,256,128]{2,1,0:T(8,128)} %bitcast.33), calls=%async_computation.9 | async-start | bytes 1048576 | tf_op jit(solution)/shard_map/all_to_all | solution.py:232
  530.8 10.8 %copy-start.1 = (bf16[512,2048]{1,0:T(8,128)(2,1)S(1)}, bf16[512,2048]{1,0:T(8,128)(2,1)}, u32[]{:S(2)}) copy-start(bf16[512,2048]{1,0:T(8,128)(2,1)} %param.9) | copy-start | bytes 6291460
Sparse Core Ops, SparseCore 0:
  27.2 43.0 all-gather.7
  72.7 40.6 all-gather.11
  186.4 62.2 all-gather.9
  338.2 50.5 all-gather.13

commit v3 on v2

--- a/solution.py
+++ b/solution.py
@@ -111,7 +111,7 @@
         lanes = pl.ds(pl.multiple_of(pair * LANES, LANES), LANES)
         err = held[both, :].astype(jnp.bfloat16)
         cgrad_ref[own, :] = join_pair(dot(err, dec_ref[lanes, :], 1, 1)).astype(jnp.bfloat16)
-        dgrad_ref[lanes, :] = dot(split_pair(code_ref[own, :]), err, 0, 0).astype(jnp.bfloat16)
+        dgrad_ref[lanes, :] = dot(split_pair(code_ref[own, :]), err, 0, 0)
 
 
 def enc_grad_kernel(pgrad_ref, rows_ref, egrad_ref):
@@ -122,21 +122,344 @@
         both = pl.ds(pl.multiple_of(pair * 2 * per, 2 * per), 2 * per)
         own = pl.ds(pl.multiple_of(pair * per, per), per)
         lanes = pl.ds(pl.multiple_of(pair * LANES, LANES), LANES)
-        out = dot(split_pair(pgrad_ref[own, :]), rows_ref[both, :], 0, 0)
-        egrad_ref[lanes, :] = out.astype(jnp.bfloat16)
+        egrad_ref[lanes, :] = dot(split_pair(pgrad_ref[own, :]), rows_ref[both, :], 0, 0)
 
 
 def call(kernel, outs, scratch, name, *args):
     whole = pl.BlockSpec(memory_space=pltpu.VMEM)
     return pl.pallas_call(
         kernel,
-        out_shape=[jax.ShapeDtypeStruct(s, jnp.bfloat16) for s in outs],
+        out_shape=[jax.ShapeDtypeStruct(s, t) for s, t in outs],
         in_specs=[whole] * len(args),
         out_specs=[whole] * len(outs),
         scratch_shapes=scratch,
         compiler_params=pltpu.CompilerParams(vmem_limit_bytes=VMEM),
         name=name,
     )(*args)
+
+
+MESH = pl.DeviceIdType.MESH
+
+
+def axis_ids():
+    return {a: lax.axis_index(a) for a in ("z", "x", "y", "c")}
+
+
+def step(ids, axis, d):
+    n = lax.axis_size(axis)
+    return lax.rem(ids[axis] + (d + n), n)
+
+
+def meet(peers):
+    barrier = pltpu.get_barrier_semaphore()
+    for peer in peers:
+        pl.semaphore_signal(barrier, inc=1, device_id=peer, device_id_type=MESH)
+    pl.semaphore_wait(barrier, len(peers))
+
+
+def send(src, dst, ssem, rsem, peer):
+    copy = pltpu.make_async_remote_copy(
+        src_ref=src, dst_ref=dst, send_sem=ssem, recv_sem=rsem, device_id=peer, device_id_type=MESH
+    )
+    copy.start()
+    return copy
+
+
+def finish(copies):
+    for copy in copies:
+        copy.wait()
+
+
+def ring_peers(ids, axis):
+    return [{axis: step(ids, axis, d)} for d in range(1, lax.axis_size(axis))]
+
+
+def reduce_share(ids, part, out, first, second, total, ssem, rsem, middle):
+    x, y = ids["x"], ids["y"]
+    half = part.shape[2] // 2
+    top, low = pl.ds(0, half), pl.ds(half, half)
+
+    def stage(k, pairs):
+        copies = []
+        for d in (1, 3, 2):
+            for h in range(2):
+                src, dst, peer = pairs(h, d)
+                copies.append(send(src, dst, ssem.at[k, h, d - 1], rsem.at[k, h, d - 1], peer))
+        return copies
+
+    def one(h, d):
+        if h == 0:
+            t = step(ids, "x", d)
+            return part.at[:, t, top], first.at[0, d - 1], {"x": t}
+        t = step(ids, "y", d)
+        return part.at[t, :, low], first.at[1, d - 1], {"y": t}
+
+    finish(stage(0, one))
+    for k in range(4):
+        for h, own in ((0, part.at[k, x, top]), (1, part.at[y, k, low])):
+            acc = own[...].astype(jnp.float32)
+            for d in range(3):
+                acc += first[h, d, k].astype(jnp.float32)
+            total[h, k] = acc
+
+    def two(h, d):
+        axis = "y" if h == 0 else "x"
+        t = step(ids, axis, d)
+        return total.at[h, t], second.at[h, d - 1], {axis: t}
+
+    finish(stage(1, two))
+    for h, mine in ((0, y), (1, x)):
+        acc = total[h, mine]
+        for d in range(3):
+            acc += second[h, d]
+        middle(h, acc)
+
+    def three(h, d):
+        axis, rows = ("y", top) if h == 0 else ("x", low)
+        return out.at[y, x, rows], out.at[y, x, rows], {axis: step(ids, axis, d)}
+
+    finish(stage(2, three))
+
+    def four(h, d):
+        if h == 0:
+            return out.at[:, x, top], out.at[:, x, top], {"x": step(ids, "x", d)}
+        return out.at[y, :, low], out.at[y, :, low], {"y": step(ids, "y", d)}
+
+    return stage(3, four)
+
+
+def gelu_parts(v):
+    a, b = 0.7978845608028654, 0.044715
+    t = jnp.tanh(a * (v + b * (v * v * v)))
+    value = 0.5 * v * (1.0 + t)
+    slope = 0.5 * (1.0 + t) + 0.5 * v * (1.0 - t * t) * (a * (1.0 + 3.0 * b * (v * v)))
+    return value, slope
+
+
+def code_kernel(
+    part, bias, dec_own, out, slopes, dec, first, second, total, ssem, rsem, zsend, zrecv, csend, crecv, lsem
+):
+    ids = axis_ids()
+    x, y, z, c = ids["x"], ids["y"], ids["z"], ids["c"]
+    other = {"c": 1 - c}
+    meet(ring_peers(ids, "x") + ring_peers(ids, "y") + ring_peers(ids, "z") + [other])
+    mine = pltpu.make_async_copy(dec_own, dec.at[z, c], lsem)
+    mine.start()
+    around = [
+        send(dec_own, dec.at[z, c], zsend.at[d - 1], zrecv.at[d - 1], {"z": step(ids, "z", d)})
+        for d in (1, 7, 2, 6, 3, 5, 4)
+    ]
+    half = part.shape[2] // 2
+
+    def middle(h, acc):
+        at = pl.ds(h * half, half)
+        value, slope = gelu_parts(acc + bias[at, :])
+        out[y, x, at] = value.astype(jnp.bfloat16)
+        slopes[at, :] = slope
+
+    last = reduce_share(ids, part, out, first, second, total, ssem, rsem, middle)
+    mine.wait()
+    finish(around)
+    over = send(dec.at[:, c], dec.at[:, c], csend, crecv, other)
+    finish(last)
+    over.wait()
+
+
+def grad_kernel(part, slopes, out, first, second, total, ssem, rsem):
+    ids = axis_ids()
+    meet(ring_peers(ids, "x") + ring_peers(ids, "y"))
+    half = part.shape[2] // 2
+
+    def middle(h, acc):
+        at = pl.ds(h * half, half)
+        out[ids["y"], ids["x"], at] = (acc * slopes[at, :]).astype(jnp.bfloat16)
+
+    finish(reduce_share(ids, part, out, first, second, total, ssem, rsem, middle))
+
+
+def home_peers(ids):
+    return [
+        {"x": step(ids, "x", d), "c": lax.rem(ids["c"] + e, 2)}
+        for d in range(4)
+        for e in range(2)
+        if (d, e) != (0, 0)
+    ]
+
+
+def spread_kernel(
+    slices, pos, enc, dec, tok_all, pos_all, enc_all, dec_own, tsend, trecv, psend, precv,
+    wsend, wrecv, rsend, rrecv, csend, crecv, lsem,
+):
+    ids = axis_ids()
+    x, y, z, c = ids["x"], ids["y"], ids["z"], ids["c"]
+    plane = [(a, b) for a, b in (
+        (1, 0), (0, 1), (3, 0), (0, 3), (1, 1), (3, 3), (1, 3), (3, 1),
+        (2, 0), (0, 2), (1, 2), (2, 1), (3, 2), (2, 3), (2, 2),
+    )]
+    peers = [{"y": step(ids, "y", a), "x": step(ids, "x", b)} for a, b in plane]
+    crossed = [{"x": step(ids, "x", d), "c": 1 - c} for d in range(4)]
+    meet(peers + crossed + [{"z": step(ids, "z", 1)}, {"z": step(ids, "z", -1)}])
+
+    here = []
+    lat = enc.shape[0] // 2
+
+    swap = []
+    for m, w in enumerate((enc, dec)):
+        for i in range(2):
+            for h in range(2):
+                t = 2 * c + i
+                src = w.at[pl.ds(h * lat, lat), pl.ds(i * LANES, LANES)]
+                at = pl.ds(pl.multiple_of(x * lat, lat), lat)
+                dst = enc_all.at[z, h, at] if m == 0 else dec_own.at[at]
+                own = (t == x) & (c == h)
+                copy = pltpu.make_async_remote_copy(
+                    src_ref=src, dst_ref=dst, send_sem=wsend.at[m, i, h], recv_sem=wrecv.at[m, x],
+                    device_id={"x": t, "c": h}, device_id_type=MESH,
+                )
+                keep = pltpu.make_async_copy(src, dst, wrecv.at[m, x])
+
+                @pl.when(own)
+                def _():
+                    keep.start()
+
+                @pl.when(jnp.logical_not(own))
+                def _():
+                    copy.start()
+
+                swap.append((own, copy))
+
+    for n, (a, b) in enumerate(plane):
+        t = step(ids, "y", a) * 4 + step(ids, "x", b)
+        me = y * 4 + x
+        here.append(send(pos, pos_all.at[me], psend.at[n], precv.at[n], peers[n]))
+        here.append(send(slices.at[t], tok_all.at[me], tsend.at[n], trecv.at[n], peers[n]))
+    me = y * 4 + x
+    keep_pos = pltpu.make_async_copy(pos, pos_all.at[me], lsem.at[0])
+    keep_tok = pltpu.make_async_copy(slices.at[me], tok_all.at[me], lsem.at[1])
+    keep_pos.start()
+    keep_tok.start()
+
+    def arrived(m, src):
+        at = pl.ds(src * lat, lat)
+        dst = enc_all.at[z, c, at] if m == 0 else dec_own.at[at]
+        pltpu.make_async_copy(dst, dst, wrecv.at[m, src]).wait()
+
+    for src in range(4):
+        arrived(0, src)
+    other = {"c": 1 - c}
+    right, left = {"z": step(ids, "z", 1)}, {"z": step(ids, "z", -1)}
+
+    def block(zz):
+        return enc_all.at[zz, c]
+
+    ring, over = [], []
+    over.append(send(block(z), block(z), csend.at[0], crecv.at[0], other))
+    ups = [send(block(z), block(z), rsend.at[0, 0], rrecv.at[0, 0], right)]
+    downs = [send(block(z), block(z), rsend.at[1, 0], rrecv.at[1, 0], left)]
+    for k in range(1, 5):
+        zz = step(ids, "z", -k)
+        ups[k - 1].wait_recv()
+        if k < 4:
+            ups.append(send(block(zz), block(zz), rsend.at[0, k], rrecv.at[0, k], right))
+        over.append(send(block(zz), block(zz), csend.at[k], crecv.at[k], other))
+        if k < 4:
+            zz = step(ids, "z", k)
+            downs[k - 1].wait_recv()
+            if k < 3:
+                downs.append(send(block(zz), block(zz), rsend.at[1, k], rrecv.at[1, k], left))
+            over.append(send(block(zz), block(zz), csend.at[4 + k], crecv.at[4 + k], other))
+    for copy in ups + downs:
+        copy.wait_send()
+    finish(over)
+    keep_pos.wait()
+    keep_tok.wait()
+    for src in range(4):
+        arrived(1, src)
+    for own, copy in swap:
+        @pl.when(jnp.logical_not(own))
+        def _():
+            copy.wait_send()
+    finish(here)
+
+
+def collect_kernel(
+    enc, dec, enc_out, dec_out, half_in, narrow, z_in, total, csend, crecv, zsend, zrecv, hsend, hrecv,
+):
+    ids = axis_ids()
+    x, z, c = ids["x"], ids["z"], ids["c"]
+    other = {"c": 1 - c}
+    meet(ring_peers(ids, "z") + home_peers(ids))
+    nz = lax.axis_size("z")
+    both = ((0, dec, dec_out), (1, enc, enc_out))
+    swaps = [send(g.at[:, 1 - c], half_in.at[m], csend.at[m], crecv.at[m], other) for m, g, _ in both]
+    around = []
+    for m, g, _ in both:
+        swaps[m].wait()
+        for d in (1, 7, 2, 6, 3, 5, 4, 0):
+            t = step(ids, "z", d)
+            acc = g[t, c].astype(jnp.float32) + half_in[m, t].astype(jnp.float32)
+            if d == 0:
+                total[m] = acc
+                continue
+            narrow[m, t] = acc.astype(jnp.bfloat16)
+            around.append(
+                send(narrow.at[m, t], z_in.at[m, d - 1], zsend.at[m, d - 1], zrecv.at[m, d - 1], {"z": t})
+            )
+    lat = dec_out.shape[0] // 2
+    owner_c = x // 2
+    lanes = pl.ds(pl.multiple_of(lax.rem(x, 2) * LANES, LANES), LANES)
+    rows = pl.ds(pl.multiple_of(c * lat, lat), lat)
+    homes = []
+    for m, _, out in both:
+        finish(around[m * 7 : m * 7 + 7])
+        total[m] += sum(z_in[m, d].astype(jnp.float32) for d in range(nz - 1))
+        for t in range(4):
+            src, dst = total.at[m, pl.ds(t * lat, lat)], out.at[rows, lanes]
+            own = (t == x) & (owner_c == c)
+            sem = hrecv.at[m, c, lax.rem(x, 2)]
+            copy = pltpu.make_async_remote_copy(
+                src_ref=src, dst_ref=dst, send_sem=hsend.at[m, t], recv_sem=sem,
+                device_id={"x": t, "c": owner_c}, device_id_type=MESH,
+            )
+            keep = pltpu.make_async_copy(src, dst, sem)
+
+            @pl.when(own)
+            def _():
+                keep.start()
+
+            @pl.when(jnp.logical_not(own))
+            def _():
+                copy.start()
+
+            homes.append((own, copy))
+    for m, _, out in both:
+        for h in range(2):
+            for i in range(2):
+                dst = out.at[pl.ds(h * lat, lat), pl.ds(i * LANES, LANES)]
+                pltpu.make_async_copy(dst, dst, hrecv.at[m, h, i]).wait()
+    for own, copy in homes:
+        @pl.when(jnp.logical_not(own))
+        def _():
+            copy.wait_send()
+
+
+def talk(kernel, outs, scratch, cid, *args):
+    whole = pl.BlockSpec(memory_space=pltpu.VMEM)
+    return pl.pallas_call(
+        kernel,
+        out_shape=[jax.ShapeDtypeStruct(s, t) for s, t in outs],
+        in_specs=[whole] * len(args),
+        out_specs=[whole] * len(outs),
+        scratch_shapes=scratch,
+        compiler_params=pltpu.CompilerParams(
+            collective_id=cid, has_side_effects=True, vmem_limit_bytes=VMEM
+        ),
+        name=kernel.__name__,
+    )(*args)
+
+
+def sems(*shape):
+    return pltpu.SemaphoreType.DMA(shape)
 
 
 def local(
@@ -158,13 +481,6 @@
     half = lat // nc
     me = lax.axis_index("y") * nx + lax.axis_index("x")
 
-    def spread(w):
-        w = w.reshape(nc, half, part)
-        w = lax.all_to_all(w, "c", split_axis=0, concat_axis=2, tiled=True)
-        w = w.reshape(half, nx, LANES)
-        w = lax.all_to_all(w, "x", split_axis=1, concat_axis=0, tiled=True)
-        return lax.all_gather(w.reshape(nx * half, LANES), ("z", "c"), axis=0, tiled=True)
-
     per_half = half // BLOCK
     local_b = block_ids % (nc * per_half)
     shard = block_ids // (nc * per_half)
@@ -175,67 +491,86 @@
     named = [nums == place[:, k][None, :] for k in range(2)]
     count = jnp.cumsum((named[0] | named[1]).astype(jnp.int32), axis=1) - 1
     rank = jnp.stack([jnp.sum(jnp.where(n, count, 0), axis=0) for n in named])
-    pos = lax.all_gather(rank * blocks + place.T, CHIPS, axis=0)
-    col = pos.transpose(0, 2, 1)
-
+    pos = jnp.pad(rank * blocks + place.T, ((0, 6), (0, 0)))
+
+    bf, f32 = jnp.bfloat16, jnp.float32
+    per = CAP * HOMES
+    rows_own = blocks // 2 // HOMES * per
     slices = tokens.reshape(tok, HOMES, LANES).transpose(1, 0, 2)
-    slices = lax.all_to_all(slices, CHIPS, split_axis=0, concat_axis=0, tiled=True)
+    own_w = nx * half
+    slices, pos, enc, dec_own = talk(
+        spread_kernel,
+        [
+            ((HOMES, tok, LANES), bf),
+            ((HOMES, 8, tok), jnp.int32),
+            ((nz, nc, own_w, LANES), bf),
+            ((own_w, LANES), bf),
+        ],
+        [sems(15), sems(15), sems(15), sems(15), sems(2, 2, 2), sems(2, 4), sems(2, 4), sems(2, 4),
+         sems(8), sems(8), sems(2)],
+        1,
+        slices,
+        pos,
+        enc_master.astype(bf).T,
+        dec_master.astype(bf),
+    )
     slices = slices.reshape(HOMES * tok, LANES)
-
-    enc = spread(enc_master.astype(jnp.bfloat16).T)
-    dec = spread(dec_master.astype(jnp.bfloat16))
+    col = pos[:, :2].transpose(0, 2, 1)
+    enc = enc.reshape(-1, LANES)
     bias = lax.all_gather(enc_bias, ("z", "x"), axis=0, tiled=True)
     bias = bias.reshape(nz, nx, nc, half).transpose(0, 2, 1, 3).reshape(HOMES, -1, 1, LANES)
     bias = lax.dynamic_index_in_dim(bias, me, 0, keepdims=False)
-
-    per = CAP * HOMES
+    bias = jnp.broadcast_to(bias, (bias.shape[0], per, LANES)).reshape(rows_own, LANES)
+
     codes = (blocks // 2 * per, LANES)
-    held = [pltpu.VMEM((blocks * per, LANES), jnp.float32)]
-    pre, rows = call(encode_kernel, [codes, (blocks * per, LANES)], held, "encode", slices, pos, enc)
-
-    def reduce_own(partial):
-        got = lax.all_to_all(
-            partial.reshape(HOMES, -1, per, LANES), CHIPS, split_axis=0, concat_axis=0, tiled=True
-        )
-        return jnp.sum(got.astype(jnp.float32), axis=0)
-
-    def share(own):
-        return lax.all_gather(own, CHIPS, axis=0, tiled=True).reshape(codes)
-
-    preact = reduce_own(pre) + bias
-    values, slopes = jax.jvp(
-        lambda inner: jax.nn.gelu(inner, approximate=True), (preact,), (jnp.ones_like(preact),)
+    grid4 = (ny, nx, rows_own, LANES)
+    held = [pltpu.VMEM((blocks * per, LANES), f32)]
+    stages = [
+        pltpu.VMEM((2, 3, 4, rows_own // 2, LANES), bf),
+        pltpu.VMEM((2, 3, rows_own // 2, LANES), f32),
+        pltpu.VMEM((2, 4, rows_own // 2, LANES), f32),
+        sems(4, 2, 3),
+        sems(4, 2, 3),
+    ]
+    pre, rows = call(encode_kernel, [(codes, bf), ((blocks * per, LANES), bf)], held, "encode", slices, pos, enc)
+    coded, slopes, dec = talk(
+        code_kernel,
+        [(grid4, bf), ((rows_own, LANES), f32), ((nz, nc, own_w, LANES), bf)],
+        stages + [sems(7), sems(7), pltpu.SemaphoreType.DMA, pltpu.SemaphoreType.DMA, pltpu.SemaphoreType.DMA],
+        2,
+        pre.reshape(grid4),
+        bias,
+        dec_own,
     )
-    coded = share(values.astype(jnp.bfloat16))
     cgrad, dgrad = call(
         decode_kernel,
-        [codes, (blocks * BLOCK, LANES)],
+        [(codes, bf), ((blocks * BLOCK, LANES), f32)],
         held,
         "decode",
-        coded,
-        dec,
+        coded.reshape(codes),
+        dec.reshape(-1, LANES),
         slices,
         pos,
         col,
     )
-    pgrad = share((reduce_own(cgrad) * slopes).astype(jnp.bfloat16))
-    (egrad,) = call(enc_grad_kernel, [(blocks * BLOCK, LANES)], [], "enc_grad", pgrad, rows)
-
-    def collect(g):
-        g = g.reshape(nz, nc, nx * half, LANES)
-        g = lax.all_to_all(g, "c", split_axis=1, concat_axis=0, tiled=True).reshape(
-            nc, nz, nx * half, LANES
-        )
-        g = jnp.sum(g.astype(jnp.float32), axis=0).astype(jnp.bfloat16)
-        g = lax.all_to_all(g, "z", split_axis=0, concat_axis=0, tiled=True)
-        g = jnp.sum(g.astype(jnp.float32), axis=0).reshape(nx, half, LANES)
-        g = lax.all_to_all(g, "x", split_axis=0, concat_axis=2, tiled=True)
-        g = g.reshape(1, half, nc, part)
-        g = lax.all_to_all(g, "c", split_axis=2, concat_axis=0, tiled=True)
-        return g.reshape(lat, part)
-
-    dec_share = collect(dgrad)
-    enc_share = collect(egrad).T
+    (pgrad,) = talk(grad_kernel, [(grid4, bf)], stages, 3, cgrad.reshape(grid4), slopes)
+    (egrad,) = call(enc_grad_kernel, [((blocks * BLOCK, LANES), f32)], [], "enc_grad", pgrad.reshape(codes), rows)
+    grads = (nz, nc, own_w, LANES)
+    enc_share, dec_share = talk(
+        collect_kernel,
+        [((lat, part), f32), ((lat, part), f32)],
+        [
+            pltpu.VMEM((2, nz, own_w, LANES), f32),
+            pltpu.VMEM((2, nz, own_w, LANES), bf),
+            pltpu.VMEM((2, nz - 1, own_w, LANES), bf),
+            pltpu.VMEM((2, own_w, LANES), f32),
+            sems(2), sems(2), sems(2, 7), sems(2, 7), sems(2, 4), sems(2, 2, 2),
+        ],
+        4,
+        egrad.reshape(grads),
+        dgrad.reshape(grads),
+    )
+    enc_share = enc_share.T
     enc_new, enc_first_new, enc_second_new = adam(enc_master, enc_share, enc_first, enc_second)
     dec_new, dec_first_new, dec_second_new = adam(dec_master, dec_share, dec_first, dec_second)
     return (enc_new, dec_new, enc_first_new, enc_second_new, dec_first_new, dec_second_new)

time: 550 us -> 450 us (0.82)
  Pallas kernels: 89.9 us -> 378 us
  blocking collectives: 249 us -> 39.2 us
  waiting for transfers between devices: 114 us -> 0 us
  starting transfers between devices: 25.9 us -> 0 us
  local copies, waits for them, and re-layouts: 30.2 us -> 16.2 us
  between operations: 14.1 us -> 0.82 us
  other arithmetic: 25.1 us -> 12.3 us
    pallas_call x3 -> x7, Pallas kernels: 89.9 us -> 378 us  [the longest x4 286 us: talk(): pl.pallas_call(kernel, out_shape=[jax.ShapeDtypeStruct(s, t) for s, t in...]
    all_to_all x9 -> x0, blocking collectives: 150 us -> none  [the longest x1 57.6 us: collect(): g = lax.all_to_all(g, 'z', split_axis=0, concat_axis=0, tiled=True)]
    all_gather x4 -> x0, waiting for transfers between devices: 59.8 us -> none  [the longest x2 59.8 us: share(): return lax.all_gather(own, CHIPS, axis=0, tiled=True).reshape(codes)]
    all_to_all x6 -> x0, waiting for transfers between devices: 54 us -> none  [the longest x1 47.3 us: collect(): g = lax.all_to_all(g, 'z', split_axis=0, concat_axis=0, tiled=True)]
    all_gather x1 -> x0, blocking collectives: 34.7 us -> none  [local(): pos = lax.all_gather(rank * blocks + place.T, CHIPS, axis=0)]
    all_to_all x6 -> x0, starting transfers between devices: 25.8 us -> none  [the longest x2 6.94 us: collect(): g = lax.all_to_all(g, 'x', split_axis=0, concat_axis=2, tiled=True)]
    all_gather x1, blocking collectives: 64.9 us -> 39.2 us  [local(): bias = lax.all_gather(enc_bias, ('z', 'x'), axis=0, tiled=True)]
    reduce_sum x6 -> x0, other arithmetic: 12.9 us -> none  [the longest x2 8.24 us: collect(): g = jnp.sum(g.astype(jnp.float32), axis=0).astype(jnp.bfloat16)]
  transfers between devices with their start and end apart: 10 -> 0, of which waited for: 5 -> 0; matrix products, arithmetic and copies ran while one was open for 6% -> 0% of each run, Pallas kernels for 4% -> 0%
where the time goes in v3:
time: 450 us; the launch traced here: 446 us
  Pallas kernels  378 us (84%)
  blocking collectives  39.2 us (9%)
  local copies, waits for them, and re-layouts  16.2 us (4%)
  other arithmetic  12.3 us (3%)
    pallas_call x4, Pallas kernels, talk(): pl.pallas_call(kernel, out_shape=[jax.ShapeDtypeStruct(s, t) for s, t in...  286 us
    pallas_call x3, Pallas kernels, call(): pl.pallas_call(kernel, out_shape=[jax.ShapeDtypeStruct(s, t) for s, t in...  92.1 us
    all_gather x1, blocking collectives, local(): bias = lax.all_gather(enc_bias, ('z', 'x'), axis=0, tiled=True)  39.2 us

profile of v3, /device:TPU:1, one launch (start us, length us, event | category | flops | bytes accessed | tf_op | source)
XLA Modules:
  0.0 446.1 jit_solution(5063280288310165969)
XLA Ops:
  0.6 0.7 fusion.11
  1.4 0.1 copy.53
  1.5 0.1 copy.54
  1.6 0.3 fusion.3
  2.0 4.8 %select_reduce_fusion.1 = (s32[4,128]{0,1:T(8,128)S(1)}, s32[4,128]{0,1:T(8,128)S(1)}) fusion(s32[256,4,128]{0,1,2:T(4,128)S(1)} %fusion.3, s32[256,4]{0,1:T(4,128)S(1)} %slice.23, s32[4,128]{0,1:T(8,128)S(1)} %copy.53, s32[4,128]{0,1:T(8,128)S(1)} %copy.54), kind=kLoop, calls=%fused_computation.10 | loop fusion | flops 1047552 | bytes 536576 | tf_op jit(solution)/shard_map/reduce_sum | solution.py:493
  6.9 0.1 copy.55
  6.9 0.1 copy.56
  7.0 0.8 fusion.12
  7.8 0.6 pad.4.pos
  8.4 1.2 copy.61
  9.6 0.7 convert_bitcast_fusion.enc
  10.3 2.9 copy.51
  13.2 0.0 copy-start
  13.2 2.4 copy.52
  15.6 0.0 copy-done
  15.6 0.7 convert_element_type.12.dec
  16.4 49.8 %spread_kernel.1 = (bf16[16,512,128]{2,1,0:T(8,128)(2,1)}, s32[16,8,512]{2,1,0:T(8,128)}, bf16[8,2,1024,128]{3,2,1,0:T(8,128)(2,1)}, bf16[1024,128]{1,0:T(8,128)(2,1)}) custom-call(bf16[16,512,128]{2,1,0:T(8,128)(2,1)} %bitcast.39, s32[8,512]{1,0:T(8,128)} %pad.4.pos, bf16[512,256]{1,0:T(8,128)(2,1)} %convert_bitcast_fusion.enc, ...), custom_call_target="tpu_custom_call" | custom-call | tf_op jit(solution)/shard_map/spread_kernel/pallas_call | solution.py:448
  66.2 0.0 copy-start.5
  66.2 23.6 %encode.1 = (bf16[10240,128]{1,0:T(8,128)(2,1)}, bf16[20480,128]{1,0:T(8,128)(2,1)}) custom-call(bf16[8192,128]{1,0:T(8,128)(2,1)} %bitcast.37, s32[16,8,512]{2,1,0:T(8,128)} %get-tuple-element.20.pos_ref, bf16[16384,128]{1,0:T(8,128)(2,1)} %bitcast.43), custom_call_target="tpu_custom_call" | custom-call | tf_op jit(solution)/shard_map/encode/pallas_call | solution.py:130
  89.8 0.0 copy-done.5
  89.8 39.2 %all-gather = f32[32,1,512]{2,1,0:T(1,128)S(1)} all-gather(f32[1,1,512]{2,1,0:T(1,128)S(1)} %bitcast.53), channel_id=1, replica_groups=mesh['z'=8,'x'=4,'y'=4,'c'=2] {'z','x'}, dimensions={0}, use_global_device_ids=true | all-gather | bytes 67584 | tf_op jit(solution)/shard_map/all_gather | solution.py:520
  128.9 0.2 reduce.2
  129.2 0.7 broadcast_in_dim.15
  130.0 67.6 %code_kernel.1 = (bf16[4,4,640,128]{3,2,1,0:T(8,128)(2,1)}, f32[640,128]{1,0:T(8,128)}, bf16[8,2,1024,128]{3,2,1,0:T(8,128)(2,1)}) custom-call(bf16[4,4,640,128]{3,2,1,0:T(8,128)(2,1)} %bitcast.45, f32[640,128]{1,0:T(8,128)} %bitcast.47, bf16[1024,128]{1,0:T(8,128)(2,1)} %get-tuple-element.23.dec_own), custom_call_target="tpu_custom_call" | custom-call | tf_op jit(solution)/shard_map/code_kernel/pallas_call | solution.py:448
  197.6 1.0 slice.19
  198.6 2.6 copy.59
  201.2 52.9 %decode.1 = (bf16[10240,128]{1,0:T(8,128)(2,1)}, f32[16384,128]{1,0:T(8,128)}) custom-call(bf16[10240,128]{1,0:T(8,128)(2,1)} %bitcast.44, bf16[16384,128]{1,0:T(8,128)(2,1)} %bitcast.42, bf16[8192,128]{1,0:T(8,128)(2,1)} %bitcast.38, s32[16,8,512]{2,1,0:T(8,128)} %get-tuple-element.20.pos_ref, s32[16,512,2]{2,1,0:T(8,128)} %bitcast.35), custom_call_target="tpu_custom_call" | custom-call | tf_op jit(solution)/shard_map/decode/pallas_call | solution.py:130
  254.2 50.3 %grad_kernel.1 = bf16[4,4,640,128]{3,2,1,0:T(8,128)(2,1)} custom-call(bf16[4,4,640,128]{3,2,1,0:T(8,128)(2,1)} %bitcast.46, f32[640,128]{1,0:T(8,128)} %get-tuple-element.27.slopes), custom_call_target="tpu_custom_call" | custom-call | tf_op jit(solution)/shard_map/grad_kernel/pallas_call | solution.py:448
  304.5 15.6 %enc_grad.1 = f32[16384,128]{1,0:T(8,128)} custom-call(bf16[10240,128]{1,0:T(8,128)(2,1)} %bitcast.36, bf16[20480,128]{1,0:T(8,128)(2,1)} %get-tuple-element.28.rows_ref), custom_call_target="tpu_custom_call" | custom-call | tf_op jit(solution)/shard_map/enc_grad/pallas_call | solution.py:130
  320.1 0.0 copy-start.3
  320.1 0.0 copy-start.4
  320.1 117.8 %collect_kernel.1 = (f32[512,256]{1,0:T(8,128)}, f32[512,256]{1,0:T(8,128)}) custom-call(f32[8,2,1024,128]{3,2,1,0:T(8,128)} %bitcast.34, f32[8,2,1024,128]{3,2,1,0:T(8,128)} %bitcast.40), custom_call_target="tpu_custom_call" | custom-call | tf_op jit(solution)/shard_map/collect_kernel/pallas_call | solution.py:448
  437.9 0.0 copy-done.3
  437.9 0.2 copy.50
  438.1 0.0 copy-done.4
  438.1 1.0 copy.60
  439.1 1.6 multiply_subtract_fusion.1
  440.7 0.0 copy-start.1
  440.7 0.0 copy-start.2
  440.7 1.0 copy.62
  441.7 1.0 copy.63
  442.7 1.0 copy.64
  443.7 0.0 copy-done.1
  443.7 0.0 copy-done.2
  443.7 2.4 multiply_subtract_fusion
  (8 shorter events, 0.1 us)
Async XLA Ops:
  13.2 2.4 copy-start
  66.2 23.6 %copy-start.5 = (f32[512]{0:T(512)S(1)}, f32[512]{0:T(512)}, u32[]{:S(2)}) copy-start(f32[512]{0:T(512)} %param.11) | copy-start | bytes 6148
  320.1 117.8 %copy-start.3 = (f32[256,512]{1,0:T(8,128)S(1)}, f32[256,512]{1,0:T(8,128)}, u32[]{:S(2)}) copy-start(f32[256,512]{1,0:T(8,128)} %param.14) | copy-start | bytes 1572868
  320.1 118.0 %copy-start.4 = (f32[256,512]{1,0:T(8,128)S(1)}, f32[256,512]{1,0:T(8,128)}, u32[]{:S(2)}) copy-start(f32[256,512]{1,0:T(8,128)} %param.15) | copy-start | bytes 1572868
  440.7 3.0 copy-start.1
  440.7 3.0 copy-start.2

commit v4 on v3

--- a/solution.py
+++ b/solution.py
@@ -46,16 +46,12 @@
     return jnp.where(low_lanes((half, LANES)), both[:half], both[half:])
 
 
-def gather_onehot(pos_ref, home, slot, blocks, tok):
-    rows = lax.broadcasted_iota(jnp.int32, (blocks, tok), 0) + slot * blocks
-    first, second = pos_ref[home, 0:1, :], pos_ref[home, 1:2, :]
-    return jnp.where((rows == first) | (rows == second), 1.0, 0.0).astype(jnp.bfloat16)
-
-
-def scatter_onehot(col_ref, home, slot, blocks, tok):
-    cols = lax.broadcasted_iota(jnp.int32, (tok, blocks), 1) + slot * blocks
-    first, second = col_ref[home, :, 0:1], col_ref[home, :, 1:2]
-    return jnp.where((cols == first) | (cols == second), 1.0, 0.0).astype(jnp.bfloat16)
+def slot_onehot(pos_ref, home, slot, blocks, tok):
+    rows = (lax.broadcasted_iota(jnp.int32, (blocks, tok), 0) + slot * blocks).astype(jnp.int16)
+    first = pos_ref[home, 0:1, :].astype(jnp.int16)
+    second = pos_ref[home, 1:2, :].astype(jnp.int16)
+    one, zero = jnp.ones((), jnp.bfloat16), jnp.zeros((), jnp.bfloat16)
+    return jnp.where((rows == first) | (rows == second), one, zero)
 
 
 def encode_kernel(tok_ref, pos_ref, enc_ref, pre_ref, rows_ref, held):
@@ -67,10 +63,10 @@
     def _(home):
         mine = tok_ref[pl.ds(pl.multiple_of(home * tok, tok), tok), :]
         for slot in range(CAP):
-            picked = dot(gather_onehot(pos_ref, home, slot, blocks, tok), mine, 1, 0)
+            picked = dot(slot_onehot(pos_ref, home, slot, blocks, tok), mine, 1, 0)
             held[pl.ds(slot * HOMES + home, blocks, per), :] = picked
 
-    @pl.loop(0, blocks // 2, unroll=4)
+    @pl.loop(0, blocks // 2, unroll=8)
     def _(pair):
         both = pl.ds(pl.multiple_of(pair * 2 * per, 2 * per), 2 * per)
         rows = held[both, :].astype(jnp.bfloat16)
@@ -80,12 +76,12 @@
         pre_ref[pl.ds(pl.multiple_of(pair * per, per), per), :] = out
 
 
-def decode_kernel(code_ref, dec_ref, tok_ref, pos_ref, col_ref, cgrad_ref, dgrad_ref, held):
+def decode_kernel(code_ref, dec_ref, tok_ref, pos_ref, cgrad_ref, dgrad_ref, held):
     tok = tok_ref.shape[0] // HOMES
     blocks = dec_ref.shape[0] // BLOCK
     per = CAP * HOMES
 
-    @pl.loop(0, blocks // 2, unroll=4)
+    @pl.loop(0, blocks // 2, unroll=8)
     def _(pair):
         both = pl.ds(pl.multiple_of(pair * 2 * per, 2 * per), 2 * per)
         code = split_pair(code_ref[pl.ds(pl.multiple_of(pair * per, per), per), :])
@@ -98,13 +94,13 @@
         rebuilt = jnp.zeros((tok, LANES), jnp.float32)
         for slot in range(CAP):
             part = held[pl.ds(slot * HOMES + home, blocks, per), :].astype(jnp.bfloat16)
-            rebuilt += dot(scatter_onehot(col_ref, home, slot, blocks, tok), part, 1, 0)
+            rebuilt += dot(slot_onehot(pos_ref, home, slot, blocks, tok), part, 0, 0)
         err = (rebuilt - mine.astype(jnp.float32)).astype(jnp.bfloat16)
         for slot in range(CAP):
-            picked = dot(gather_onehot(pos_ref, home, slot, blocks, tok), err, 1, 0)
+            picked = dot(slot_onehot(pos_ref, home, slot, blocks, tok), err, 1, 0)
             held[pl.ds(slot * HOMES + home, blocks, per), :] = picked
 
-    @pl.loop(0, blocks // 2, unroll=4)
+    @pl.loop(0, blocks // 2, unroll=8)
     def _(pair):
         both = pl.ds(pl.multiple_of(pair * 2 * per, 2 * per), 2 * per)
         own = pl.ds(pl.multiple_of(pair * per, per), per)
@@ -112,17 +108,6 @@
         err = held[both, :].astype(jnp.bfloat16)
         cgrad_ref[own, :] = join_pair(dot(err, dec_ref[lanes, :], 1, 1)).astype(jnp.bfloat16)
         dgrad_ref[lanes, :] = dot(split_pair(code_ref[own, :]), err, 0, 0)
-
-
-def enc_grad_kernel(pgrad_ref, rows_ref, egrad_ref):
-    per = CAP * HOMES
-
-    @pl.loop(0, pgrad_ref.shape[0] // per, unroll=4)
-    def _(pair):
-        both = pl.ds(pl.multiple_of(pair * 2 * per, 2 * per), 2 * per)
-        own = pl.ds(pl.multiple_of(pair * per, per), per)
-        lanes = pl.ds(pl.multiple_of(pair * LANES, LANES), LANES)
-        egrad_ref[lanes, :] = dot(split_pair(pgrad_ref[own, :]), rows_ref[both, :], 0, 0)
 
 
 def call(kernel, outs, scratch, name, *args):
@@ -174,7 +159,7 @@
     return [{axis: step(ids, axis, d)} for d in range(1, lax.axis_size(axis))]
 
 
-def reduce_share(ids, part, out, first, second, total, ssem, rsem, middle):
+def reduce_share(ids, part, out, first, second, total, ssem, rsem, middle, beside=None):
     x, y = ids["x"], ids["y"]
     half = part.shape[2] // 2
     top, low = pl.ds(0, half), pl.ds(half, half)
@@ -194,7 +179,10 @@
         t = step(ids, "y", d)
         return part.at[t, :, low], first.at[1, d - 1], {"y": t}
 
-    finish(stage(0, one))
+    copies = stage(0, one)
+    if beside is not None:
+        beside()
+    finish(copies)
     for k in range(4):
         for h, own in ((0, part.at[k, x, top]), (1, part.at[y, k, low])):
             acc = own[...].astype(jnp.float32)
@@ -265,18 +253,6 @@
     over.wait()
 
 
-def grad_kernel(part, slopes, out, first, second, total, ssem, rsem):
-    ids = axis_ids()
-    meet(ring_peers(ids, "x") + ring_peers(ids, "y"))
-    half = part.shape[2] // 2
-
-    def middle(h, acc):
-        at = pl.ds(h * half, half)
-        out[ids["y"], ids["x"], at] = (acc * slopes[at, :]).astype(jnp.bfloat16)
-
-    finish(reduce_share(ids, part, out, first, second, total, ssem, rsem, middle))
-
-
 def home_peers(ids):
     return [
         {"x": step(ids, "x", d), "c": lax.rem(ids["c"] + e, 2)}
@@ -287,8 +263,8 @@
 
 
 def spread_kernel(
-    slices, pos, enc, dec, tok_all, pos_all, enc_all, dec_own, tsend, trecv, psend, precv,
-    wsend, wrecv, rsend, rrecv, csend, crecv, lsem,
+    slices, pos, enc, dec, bias, tok_all, pos_all, enc_all, dec_own, bias_all, tsend, trecv, psend, precv,
+    wsend, wrecv, rsend, rrecv, csend, crecv, lsem, bsend, brecv, zsend, zrecv,
 ):
     ids = axis_ids()
     x, y, z, c = ids["x"], ids["y"], ids["z"], ids["c"]
@@ -298,9 +274,15 @@
     )]
     peers = [{"y": step(ids, "y", a), "x": step(ids, "x", b)} for a, b in plane]
     crossed = [{"x": step(ids, "x", d), "c": 1 - c} for d in range(4)]
-    meet(peers + crossed + [{"z": step(ids, "z", 1)}, {"z": step(ids, "z", -1)}])
+    meet(peers + crossed + ring_peers(ids, "z"))
 
     here = []
+    bias_x = [
+        send(bias, bias_all.at[z, x], bsend.at[d - 1], brecv.at[d - 1], {"x": step(ids, "x", d)})
+        for d in range(1, 4)
+    ]
+    keep_bias = pltpu.make_async_copy(bias, bias_all.at[z, x], lsem.at[2])
+    keep_bias.start()
     lat = enc.shape[0] // 2
 
     swap = []
@@ -347,6 +329,12 @@
     for src in range(4):
         arrived(0, src)
     other = {"c": 1 - c}
+    finish(bias_x)
+    keep_bias.wait()
+    here += [
+        send(bias_all.at[z], bias_all.at[z], zsend.at[d - 1], zrecv.at[d - 1], {"z": step(ids, "z", d)})
+        for d in range(1, 8)
+    ]
     right, left = {"z": step(ids, "z", 1)}, {"z": step(ids, "z", -1)}
 
     def block(zz):
@@ -382,39 +370,79 @@
     finish(here)
 
 
-def collect_kernel(
-    enc, dec, enc_out, dec_out, half_in, narrow, z_in, total, csend, crecv, zsend, zrecv, hsend, hrecv,
+def tail_kernel(
+    part, slopes, dec, rows, enc_out, dec_out, codes, first, second, total, ssem, rsem,
+    enc, half_in, narrow, z_in, sums, csend, crecv, zsend, zrecv, hsend, hrecv,
 ):
     ids = axis_ids()
-    x, z, c = ids["x"], ids["z"], ids["c"]
+    x, y, z, c = ids["x"], ids["y"], ids["z"], ids["c"]
     other = {"c": 1 - c}
-    meet(ring_peers(ids, "z") + home_peers(ids))
+    meet(ring_peers(ids, "y") + ring_peers(ids, "z") + home_peers(ids))
     nz = lax.axis_size("z")
-    both = ((0, dec, dec_out), (1, enc, enc_out))
-    swaps = [send(g.at[:, 1 - c], half_in.at[m], csend.at[m], crecv.at[m], other) for m, g, _ in both]
-    around = []
-    for m, g, _ in both:
-        swaps[m].wait()
-        for d in (1, 7, 2, 6, 3, 5, 4, 0):
-            t = step(ids, "z", d)
-            acc = g[t, c].astype(jnp.float32) + half_in[m, t].astype(jnp.float32)
-            if d == 0:
-                total[m] = acc
-                continue
-            narrow[m, t] = acc.astype(jnp.bfloat16)
-            around.append(
-                send(narrow.at[m, t], z_in.at[m, d - 1], zsend.at[m, d - 1], zrecv.at[m, d - 1], {"z": t})
-            )
+    half = part.shape[2] // 2
+    per = CAP * HOMES
+    pairs = part.shape[2] // per
+    around = {0: [], 1: []}
+    far = (4, 3, 5, 2, 6, 1, 7)
+
+    def swap(m, g, k, t):
+        return send(g.at[t, 1 - c], half_in.at[m, t], csend.at[m, k], crecv.at[m, k], other)
+
+    def pass_on(m, g, copy, d, t):
+        copy.wait()
+        acc = g[t, c] + half_in[m, t]
+        if d == 0:
+            sums[m] = acc
+            return
+        narrow[m, t] = acc.astype(jnp.bfloat16)
+        around[m].append(
+            send(narrow.at[m, t], z_in.at[m, d - 1], zsend.at[m, d - 1], zrecv.at[m, d - 1], {"z": t})
+        )
+
+    order = [(d, step(ids, "z", d)) for d in far + (0,)]
+    swaps = [swap(0, dec, k, t) for k, (d, t) in enumerate(order)]
+
+    def beside():
+        for copy, (d, t) in zip(swaps, order):
+            pass_on(0, dec, copy, d, t)
+
+    def middle(h, acc):
+        at = pl.ds(h * half, half)
+        codes[y, x, at] = (acc * slopes[at, :]).astype(jnp.bfloat16)
+
+    finish(reduce_share(ids, part, codes, first, second, total, ssem, rsem, middle, beside))
+
+    def make(t, h):
+        q = 2 * t + h
+
+        @pl.loop(0, pairs, unroll=True)
+        def _(j):
+            own = pl.ds(pl.multiple_of(j * per, per), per)
+            code = codes[q // 4, lax.rem(q, 4), own, :]
+            at = pl.ds(pl.multiple_of((q * pairs + j) * 2 * per, 2 * per), 2 * per)
+            lanes = pl.ds(pl.multiple_of(j * LANES, LANES), LANES)
+            enc[t, h, lanes, :] = dot(split_pair(code), rows[at, :], 0, 0)
+
+    held = None
+    for k, (d, t) in enumerate(order):
+        make(t, 1 - c)
+        copy = swap(1, enc, k, t)
+        make(t, c)
+        if held is not None:
+            pass_on(1, enc, *held)
+        held = (copy, d, t)
+    pass_on(1, enc, *held)
+
     lat = dec_out.shape[0] // 2
     owner_c = x // 2
     lanes = pl.ds(pl.multiple_of(lax.rem(x, 2) * LANES, LANES), LANES)
-    rows = pl.ds(pl.multiple_of(c * lat, lat), lat)
+    at = pl.ds(pl.multiple_of(c * lat, lat), lat)
     homes = []
-    for m, _, out in both:
-        finish(around[m * 7 : m * 7 + 7])
-        total[m] += sum(z_in[m, d].astype(jnp.float32) for d in range(nz - 1))
+    for m, out in ((0, dec_out), (1, enc_out)):
+        finish(around[m])
+        sums[m] += sum(z_in[m, d].astype(jnp.float32) for d in range(nz - 1))
         for t in range(4):
-            src, dst = total.at[m, pl.ds(t * lat, lat)], out.at[rows, lanes]
+            src, dst = sums.at[m, pl.ds(t * lat, lat)], out.at[at, lanes]
             own = (t == x) & (owner_c == c)
             sem = hrecv.at[m, c, lax.rem(x, 2)]
             copy = pltpu.make_async_remote_copy(
@@ -432,7 +460,7 @@
                 copy.start()
 
             homes.append((own, copy))
-    for m, _, out in both:
+    for m, out in ((0, dec_out), (1, enc_out)):
         for h in range(2):
             for i in range(2):
                 dst = out.at[pl.ds(h * lat, lat), pl.ds(i * LANES, LANES)]
@@ -498,26 +526,26 @@
     rows_own = blocks // 2 // HOMES * per
     slices = tokens.reshape(tok, HOMES, LANES).transpose(1, 0, 2)
     own_w = nx * half
-    slices, pos, enc, dec_own = talk(
+    slices, pos, enc, dec_own, bias = talk(
         spread_kernel,
         [
             ((HOMES, tok, LANES), bf),
             ((HOMES, 8, tok), jnp.int32),
             ((nz, nc, own_w, LANES), bf),
             ((own_w, LANES), bf),
+            ((nz, nx, lat // LANES, LANES), f32),
         ],
         [sems(15), sems(15), sems(15), sems(15), sems(2, 2, 2), sems(2, 4), sems(2, 4), sems(2, 4),
-         sems(8), sems(8), sems(2)],
+         sems(8), sems(8), sems(3), sems(3), sems(3), sems(7), sems(7)],
         1,
         slices,
         pos,
         enc_master.astype(bf).T,
         dec_master.astype(bf),
+        enc_bias.reshape(-1, LANES),
     )
     slices = slices.reshape(HOMES * tok, LANES)
-    col = pos[:, :2].transpose(0, 2, 1)
     enc = enc.reshape(-1, LANES)
-    bias = lax.all_gather(enc_bias, ("z", "x"), axis=0, tiled=True)
     bias = bias.reshape(nz, nx, nc, half).transpose(0, 2, 1, 3).reshape(HOMES, -1, 1, LANES)
     bias = lax.dynamic_index_in_dim(bias, me, 0, keepdims=False)
     bias = jnp.broadcast_to(bias, (bias.shape[0], per, LANES)).reshape(rows_own, LANES)
@@ -551,24 +579,26 @@
         dec.reshape(-1, LANES),
         slices,
         pos,
-        col,
     )
-    (pgrad,) = talk(grad_kernel, [(grid4, bf)], stages, 3, cgrad.reshape(grid4), slopes)
-    (egrad,) = call(enc_grad_kernel, [((blocks * BLOCK, LANES), f32)], [], "enc_grad", pgrad.reshape(codes), rows)
-    grads = (nz, nc, own_w, LANES)
+    whole = (nz, nc, own_w, LANES)
     enc_share, dec_share = talk(
-        collect_kernel,
+        tail_kernel,
         [((lat, part), f32), ((lat, part), f32)],
-        [
+        [pltpu.VMEM(grid4, bf)]
+        + stages
+        + [
+            pltpu.VMEM(whole, f32),
             pltpu.VMEM((2, nz, own_w, LANES), f32),
             pltpu.VMEM((2, nz, own_w, LANES), bf),
             pltpu.VMEM((2, nz - 1, own_w, LANES), bf),
             pltpu.VMEM((2, own_w, LANES), f32),
-            sems(2), sems(2), sems(2, 7), sems(2, 7), sems(2, 4), sems(2, 2, 2),
+            sems(2, 8), sems(2, 8), sems(2, 7), sems(2, 7), sems(2, 4), sems(2, 2, 2),
         ],
-        4,
-        egrad.reshape(grads),
-        dgrad.reshape(grads),
+        3,
+        cgrad.reshape(grid4),
+        slopes,
+        dgrad.reshape(whole),
+        rows,
     )
     enc_share = enc_share.T
     enc_new, enc_first_new, enc_second_new = adam(enc_master, enc_share, enc_first, enc_second)

time: 450 us -> 323 us (0.72)
  Pallas kernels: 378 us -> 297 us
  blocking collectives: 39.2 us -> 0 us
    pallas_call x4 -> x3, Pallas kernels: 286 us -> 233 us  [talk(): pl.pallas_call(kernel, out_shape=[jax.ShapeDtypeStruct(s, t) for s, t in...]
    all_gather x1 -> x0, blocking collectives: 39.2 us -> none  [local(): bias = lax.all_gather(enc_bias, ('z', 'x'), axis=0, tiled=True)]
    pallas_call x3 -> x2, Pallas kernels: 92.1 us -> 64.6 us  [call(): pl.pallas_call(kernel, out_shape=[jax.ShapeDtypeStruct(s, t) for s, t in...]
where the time goes in v4:
time: 323 us
  Pallas kernels  297 us (92%)
  local copies, waits for them, and re-layouts  12.5 us (4%)
  other arithmetic  12.1 us (4%)
    pallas_call x3, Pallas kernels, talk(): pl.pallas_call(kernel, out_shape=[jax.ShapeDtypeStruct(s, t) for s, t in...  233 us
    pallas_call x2, Pallas kernels, call(): pl.pallas_call(kernel, out_shape=[jax.ShapeDtypeStruct(s, t) for s, t in...  64.6 us
    unnamed x19, local copies, waits for them, and re-layouts  8.3 us

profile of v4, /device:TPU:1, one launch (start us, length us, event | category | flops | bytes accessed | tf_op | source)
XLA Modules:
  0.0 322.9 jit_solution(10989722234128618096)
XLA Ops:
  0.6 0.7 fusion.11
  1.4 0.1 copy.39
  1.5 0.1 copy.40
  1.6 0.3 fusion.3
  2.0 4.8 %select_reduce_fusion.1 = (s32[4,128]{0,1:T(8,128)S(1)}, s32[4,128]{0,1:T(8,128)S(1)}) fusion(s32[256,4,128]{0,1,2:T(4,128)S(1)} %fusion.3, s32[256,4]{0,1:T(4,128)S(1)} %slice.19, s32[4,128]{0,1:T(8,128)S(1)} %copy.39, s32[4,128]{0,1:T(8,128)S(1)} %copy.40), kind=kLoop, calls=%fused_computation.10 | loop fusion | flops 1047552 | bytes 536576 | tf_op jit(solution)/shard_map/reduce_sum | solution.py:521
  6.9 0.1 copy.41
  6.9 0.1 copy.42
  7.0 0.8 fusion.12
  7.8 0.6 pad.4.pos
  8.4 1.2 copy.46
  9.6 0.7 convert_bitcast_fusion.enc
  10.4 2.9 copy.37
  13.2 0.0 copy-start
  13.2 2.4 copy.38
  15.6 0.0 copy-done
  15.6 0.7 convert_element_type.12.dec
  16.3 53.5 %spread_kernel.1 = (bf16[16,512,128]{2,1,0:T(8,128)(2,1)}, s32[16,8,512]{2,1,0:T(8,128)}, bf16[8,2,1024,128]{3,2,1,0:T(8,128)(2,1)}, bf16[1024,128]{1,0:T(8,128)(2,1)}, f32[8,4,4,128]{3,2,1,0:T(4,128)}) custom-call(bf16[16,512,128]{2,1,0:T(8,128)(2,1)} %bitcast.36, s32[8,512]{1,0:T(8,128)} %pad.4.pos, bf16[512,256]{1,0:T(8,128)(2,1)} %convert_bitcast_fusion.enc, ...), custom_call_target="tpu_custom_call" | custom-call | tf_op jit(solution)/shard_map/spread_kernel/pallas_call | solution.py:476
  69.8 0.0 copy-start.5
  69.9 19.6 %encode.1 = (bf16[10240,128]{1,0:T(8,128)(2,1)}, bf16[20480,128]{1,0:T(8,128)(2,1)}) custom-call(bf16[8192,128]{1,0:T(8,128)(2,1)} %bitcast.34, s32[16,8,512]{2,1,0:T(8,128)} %get-tuple-element.21.pos_ref, bf16[16384,128]{1,0:T(8,128)(2,1)} %bitcast.38), custom_call_target="tpu_custom_call" | custom-call | tf_op jit(solution)/shard_map/encode/pallas_call | solution.py:115
  89.4 0.0 copy-done.5
  89.4 0.1 reshape.104
  89.6 0.7 broadcast_in_dim.15
  90.3 57.2 %code_kernel.1 = (bf16[4,4,640,128]{3,2,1,0:T(8,128)(2,1)}, f32[640,128]{1,0:T(8,128)}, bf16[8,2,1024,128]{3,2,1,0:T(8,128)(2,1)}) custom-call(bf16[4,4,640,128]{3,2,1,0:T(8,128)(2,1)} %bitcast.41, f32[640,128]{1,0:T(8,128)} %bitcast.43, bf16[1024,128]{1,0:T(8,128)(2,1)} %get-tuple-element.25.dec_own), custom_call_target="tpu_custom_call" | custom-call | tf_op jit(solution)/shard_map/code_kernel/pallas_call | solution.py:476
  147.6 45.1 %decode.1 = (bf16[10240,128]{1,0:T(8,128)(2,1)}, f32[16384,128]{1,0:T(8,128)}) custom-call(bf16[10240,128]{1,0:T(8,128)(2,1)} %bitcast.42, bf16[16384,128]{1,0:T(8,128)(2,1)} %bitcast.39, bf16[8192,128]{1,0:T(8,128)(2,1)} %bitcast.35, s32[16,8,512]{2,1,0:T(8,128)} %get-tuple-element.21.pos_ref), custom_call_target="tpu_custom_call" | custom-call | tf_op jit(solution)/shard_map/decode/pallas_call | solution.py:115
  192.6 0.0 copy-start.3
  192.6 0.0 copy-start.4
  192.6 122.1 %tail_kernel.1 = (f32[512,256]{1,0:T(8,128)}, f32[512,256]{1,0:T(8,128)}) custom-call(bf16[4,4,640,128]{3,2,1,0:T(8,128)(2,1)} %bitcast.40, f32[640,128]{1,0:T(8,128)} %get-tuple-element.29.slopes, f32[8,2,1024,128]{3,2,1,0:T(8,128)} %bitcast.33, bf16[20480,128]{1,0:T(8,128)(2,1)} %get-tuple-element.31.rows), custom_call_target="tpu_custom_call" | custom-call | tf_op jit(solution)/shard_map/tail_kernel/pallas_call | solution.py:476
  314.7 0.0 copy-done.3
  314.7 0.2 copy.36
  314.9 0.0 copy-done.4
  315.0 1.0 copy.45
  316.0 1.6 multiply_subtract_fusion.1
  317.5 0.0 copy-start.1
  317.5 0.0 copy-start.2
  317.6 1.0 copy.47
  318.5 1.0 copy.48
  319.5 1.0 copy.49
  320.5 0.0 copy-done.1
  320.5 0.0 copy-done.2
  320.5 2.4 multiply_subtract_fusion
  (7 shorter events, 0.1 us)
Async XLA Ops:
  13.2 2.4 copy-start
  69.8 19.6 %copy-start.5 = (f32[8,4,4,128]{3,2,1,0:T(4,128)S(1)}, f32[8,4,4,128]{3,2,1,0:T(4,128)}, u32[]{:S(2)}) copy-start(f32[8,4,4,128]{3,2,1,0:T(4,128)} %get-tuple-element.24) | copy-start | bytes 196612
  192.6 122.1 %copy-start.3 = (f32[256,512]{1,0:T(8,128)S(1)}, f32[256,512]{1,0:T(8,128)}, u32[]{:S(2)}) copy-start(f32[256,512]{1,0:T(8,128)} %param.14) | copy-start | bytes 1572868
  192.6 122.3 %copy-start.4 = (f32[256,512]{1,0:T(8,128)S(1)}, f32[256,512]{1,0:T(8,128)}, u32[]{:S(2)}) copy-start(f32[256,512]{1,0:T(8,128)} %param.15) | copy-start | bytes 1572868
  317.5 3.0 copy-start.1
  317.5 3.0 copy-start.2

commit v5 on v1

v5 whole, which is shorter than its diff:
```python
import functools

import jax
import jax.numpy as jnp
from jax import lax
from jax.experimental import pallas as pl
from jax.experimental.pallas import tpu as pltpu
from jax.sharding import Mesh, PartitionSpec as P

BLOCK = 64
CAP = 5
LANES = 128
HOMES = 16
VMEM = 62 * 2**20

learn_rate = 0.001
adam_eps = 1e-08
first_fix = 1.0 - 0.9**10
second_fix = 1.0 - 0.95**10

REP = ("y", "c")
CHIPS = ("y", "x")


def adam(master, gradient, first, second):
    first_new = 0.9 * first + 0.1 * gradient
    second_new = 0.95 * second + 0.05 * gradient * gradient
    update = first_new / first_fix / (jnp.sqrt(second_new / second_fix) + adam_eps)
    return (master - learn_rate * update, first_new, second_new)


def dot(a, b, ca, cb):
    return lax.dot_general(a, b, (((ca,), (cb,)), ((), ())), preferred_element_type=jnp.float32)


def low_lanes(shape):
    return lax.broadcasted_iota(jnp.int32, shape, 1) < BLOCK


def split_pair(pair):
    low = low_lanes(pair.shape)
    zero = jnp.zeros_like(pair)
    return jnp.concatenate([jnp.where(low, pair, zero), jnp.where(low, zero, pair)], axis=0)


def join_pair(both):
    half = both.shape[0] // 2
    return jnp.where(low_lanes((half, LANES)), both[:half], both[half:])


def slot_onehot(pos_ref, home, slot, blocks, tok):
    rows = (lax.broadcasted_iota(jnp.int32, (blocks, tok), 0) + slot * blocks).astype(jnp.int16)
    first = pos_ref[home, 0:1, :].astype(jnp.int16)
    second = pos_ref[home, 1:2, :].astype(jnp.int16)
    one, zero = jnp.ones((), jnp.bfloat16), jnp.zeros((), jnp.bfloat16)
    return jnp.where((rows == first) | (rows == second), one, zero)


MESH = pl.DeviceIdType.MESH


def axis_ids():
    return {a: lax.axis_index(a) for a in ("z", "x", "y", "c")}


def step(ids, axis, d):
    n = lax.axis_size(axis)
    return lax.rem(ids[axis] + (d + n), n)


def meet(peers):
    barrier = pltpu.get_barrier_semaphore()
    for peer in peers:
        pl.semaphore_signal(barrier, inc=1, device_id=peer, device_id_type=MESH)
    pl.semaphore_wait(barrier, len(peers))


def send(src, dst, ssem, rsem, peer):
    copy = pltpu.make_async_remote_copy(
        src_ref=src, dst_ref=dst, send_sem=ssem, recv_sem=rsem, device_id=peer, device_id_type=MESH
    )
    copy.start()
    return copy


def finish(copies):
    for copy in copies:
        copy.wait()


def ring_peers(ids, axis):
    return [{axis: step(ids, axis, d)} for d in range(1, lax.axis_size(axis))]


def reduce_share(ids, part, out, first, second, total, ssem, rsem, produce, middle, hooks):
    x, y = ids["x"], ids["y"]
    half = part.shape[2] // 2
    top, low = pl.ds(0, half), pl.ds(half, half)

    def stage(k, pairs, before=None):
        copies = []
        for d in (1, 3, 2):
            for h in range(2):
                if before is not None:
                    before(h, d)
                src, dst, peer = pairs(h, d)
                copies.append(send(src, dst, ssem.at[k, h, d - 1], rsem.at[k, h, d - 1], peer))
        return copies

    def one(h, d):
        if h == 0:
            t = step(ids, "x", d)
            return part.at[:, t, top], first.at[0, d - 1], {"x": t}
        t = step(ids, "y", d)
        return part.at[t, :, low], first.at[1, d - 1], {"y": t}

    copies = stage(0, one, produce)
    produce(0, 0)
    produce(1, 0)
    hooks[0]()
    finish(copies)
    hooks[1]()
    for k in range(4):
        for h, own in ((0, part.at[k, x, top]), (1, part.at[y, k, low])):
            acc = own[...].astype(jnp.float32)
            for d in range(3):
                acc += first[h, d, k].astype(jnp.float32)
            total[h, k] = acc

    def two(h, d):
        axis = "y" if h == 0 else "x"
        t = step(ids, axis, d)
        return total.at[h, t], second.at[h, d - 1], {axis: t}

    copies = stage(1, two)
    hooks[2]()
    finish(copies)
    for h, mine in ((0, y), (1, x)):
        acc = total[h, mine]
        for d in range(3):
            acc += second[h, d]
        middle(h, acc)

    def three(h, d):
        axis, rows = ("y", top) if h == 0 else ("x", low)
        return out.at[y, x, rows], out.at[y, x, rows], {axis: step(ids, axis, d)}

    copies = stage(2, three)
    hooks[3]()
    finish(copies)

    def four(h, d):
        if h == 0:
            return out.at[:, x, top], out.at[:, x, top], {"x": step(ids, "x", d)}
        return out.at[y, :, low], out.at[y, :, low], {"y": step(ids, "y", d)}

    copies = stage(3, four)
    hooks[4]()
    finish(copies)


def gelu_parts(v):
    a, b = 0.7978845608028654, 0.044715
    t = jnp.tanh(a * (v + b * (v * v * v)))
    value = 0.5 * v * (1.0 + t)
    slope = 0.5 * (1.0 + t) + 0.5 * v * (1.0 - t * t) * (a * (1.0 + 3.0 * b * (v * v)))
    return value, slope


class ZRing:
    def __init__(self, ids, buf, rsend, rrecv, csend, crecv):
        self.ids, self.buf, self.c = ids, buf, ids["c"]
        self.sems, self.core = (rsend, rrecv), (csend, crecv)
        self.half = buf.shape[2] // 2
        self.sent, self.over = {}, []

    def launch(self, k, s):
        for way, sign in ((0, 1), (1, -1)):
            if k < 3 or s == way:
                zz = step(self.ids, "z", -sign * k)
                piece = self.buf.at[zz, self.c, pl.ds(s * self.half, self.half)]
                sems = [sem.at[way, k, s] for sem in self.sems]
                self.sent[way, k, s] = send(piece, piece, *sems, {"z": step(self.ids, "z", sign)})

    def share(self, zz):
        n = len(self.over)
        block = self.buf.at[zz, self.c]
        sems = [sem.at[n] for sem in self.core]
        self.over.append(send(block, block, *sems, {"c": 1 - self.c}))

    def begin(self):
        for s in range(2):
            self.launch(0, s)
        self.share(self.ids["z"])

    def arrive(self, k):
        for s in range(2):
            for way in range(2):
                if k < 4 or s == way:
                    self.sent[way, k - 1, s].wait_recv()
            if k < 4:
                self.launch(k, s)
        self.share(step(self.ids, "z", -k))
        if k < 4:
            self.share(step(self.ids, "z", k))

    def end(self):
        for copy in self.sent.values():
            copy.wait_send()
        finish(self.over)


def swap_homes(ids, items, ssem, rsem):
    started = []
    for n, r, src, dst, tx, tc in items:
        own = (tx == ids["x"]) & (tc == ids["c"])
        copy = pltpu.make_async_remote_copy(
            src_ref=src, dst_ref=dst, send_sem=ssem.at[n], recv_sem=rsem.at[r],
            device_id={"x": tx, "c": tc}, device_id_type=MESH,
        )
        keep = pltpu.make_async_copy(src, dst, rsem.at[r])

        @pl.when(own)
        def _():
            keep.start()

        @pl.when(jnp.logical_not(own))
        def _():
            copy.start()

        started.append((own, copy))
    return started


def sent_homes(started):
    for own, copy in started:
        @pl.when(jnp.logical_not(own))
        def _():
            copy.wait_send()


def landed(dst, sem):
    pltpu.make_async_copy(dst, dst, sem).wait()


PLANE = (
    (1, 0), (0, 1), (3, 0), (0, 3), (1, 1), (3, 3), (1, 3), (3, 1),
    (2, 0), (0, 2), (1, 2), (2, 1), (3, 2), (2, 3), (2, 2),
)
FAR = (4, 3, 5, 2, 6, 1, 7, 0)


def train_kernel(names, *refs):
    tokens, place, enc, dec, bias, enc_out, dec_out = refs[:7]
    v = dict(zip(names, refs[7:]))
    ids = axis_ids()
    x, y, z, c = ids["x"], ids["y"], ids["z"], ids["c"]
    me = y * 4 + x
    other = {"c": 1 - c}
    per = CAP * HOMES
    held, rows, part, codes, pgrad = v["held"], v["rows"], v["part"], v["codes"], v["pgrad"]
    tok_all, pos_all, enc_all, dec_all = v["tok_all"], v["pos_all"], v["enc_all"], v["dec_all"]
    slopes, bias_all = v["slopes"], v["bias_all"]
    tok = tok_all.shape[1]
    pairs = part.shape[2] // per
    blocks = HOMES * pairs * 2
    lat = dec.shape[0] // 2
    bf, f32 = jnp.bfloat16, jnp.float32

    peers = [{"y": step(ids, "y", a), "x": step(ids, "x", b)} for a, b in PLANE]
    crossed = [{"x": step(ids, "x", d), "c": 1 - c} for d in range(4)]
    meet(peers + crossed + ring_peers(ids, "z"))

    swaps = []
    for m in range(2):
        for i in range(2):
            for h in range(2):
                at = pl.ds(pl.multiple_of(x * lat, lat), lat)
                if m == 0:
                    src = enc.at[pl.ds(i * LANES, LANES), pl.ds(h * lat, lat)]
                    dst = enc_all.at[z, h, :, at]
                else:
                    src = dec.at[pl.ds(h * lat, lat), pl.ds(i * LANES, LANES)]
                    dst = dec_all.at[z, h, at]
                swaps.append(((m, i, h), (m, x), src, dst, 2 * c + i, h))
    swaps = swap_homes(ids, swaps, _At(v["wsend"]), _At(v["wrecv"]))
    bias_x = [
        send(bias, bias_all.at[z, x], v["bsend"].at[d - 1], v["brecv"].at[d - 1], {"x": step(ids, "x", d)})
        for d in range(1, 4)
    ]
    keep = [
        pltpu.make_async_copy(bias, bias_all.at[z, x], v["lsem"].at[0]),
        pltpu.make_async_copy(
            tokens.at[:, pl.ds(pl.multiple_of(me * LANES, LANES), LANES)], tok_all.at[me], v["lsem"].at[1]
        ),
    ]
    for copy in keep:
        copy.start()
    got = []
    for n, (a, b) in enumerate(PLANE):
        t = step(ids, "y", a) * 4 + step(ids, "x", b)
        src = tokens.at[:, pl.ds(pl.multiple_of(t * LANES, LANES), LANES)]
        got.append(send(src, tok_all.at[me], v["tsend"].at[n], v["trecv"].at[n], peers[n]))

    numbers = lax.broadcasted_iota(jnp.int32, (blocks, tok), 0)
    named = [numbers == place[k : k + 1, :] for k in range(2)]
    one, zero = jnp.ones((), f32), jnp.zeros((), f32)
    either = jnp.where(named[0] | named[1], one, zero).astype(bf)
    before = lax.broadcasted_iota(jnp.int32, (tok, tok), 0) < lax.broadcasted_iota(jnp.int32, (tok, tok), 1)
    count = dot(either, jnp.where(before, one, zero).astype(bf), 1, 0)
    pos_all[me] = jnp.zeros(pos_all.shape[1:], jnp.int32)
    for k in range(2):
        rank = jnp.sum(jnp.where(named[k], count, zero), axis=0, keepdims=True).astype(jnp.int32)
        pos_all[me, k : k + 1, :] = rank * blocks + place[k : k + 1, :]
    got += [
        send(pos_all.at[me], pos_all.at[me], v["psend"].at[n], v["precv"].at[n], peers[n]) for n in range(15)
    ]

    ring = ZRing(ids, enc_all, v["ersend"], v["errecv"], v["ecsend"], v["ecrecv"])
    for src in range(4):
        landed(enc_all.at[z, c, :, pl.ds(src * lat, lat)], v["wrecv"].at[0, src])
    ring.begin()
    finish(bias_x)
    keep[0].wait()
    bias_z = [
        send(bias_all.at[z], bias_all.at[z], v["bzsend"].at[d - 1], v["bzrecv"].at[d - 1], {"z": step(ids, "z", d)})
        for d in range(1, 8)
    ]
    ring.arrive(1)
    ring.arrive(2)
    finish(got)
    keep[1].wait()

    def gather(homes):
        @pl.loop(*homes)
        def _(home):
            mine = tok_all[home]
            for slot in range(CAP):
                picked = dot(slot_onehot(pos_all, home, slot, blocks, tok), mine, 1, 0)
                held[pl.ds(slot * HOMES + home, blocks, per), :] = picked

    gather((0, 8))
    ring.arrive(3)
    gather((8, 16))
    ring.arrive(4)
    around = ZRing(ids, dec_all, v["drsend"], v["drrecv"], v["dcsend"], v["dcrecv"])
    for src in range(4):
        landed(dec_all.at[z, c, pl.ds(src * lat, lat)], v["wrecv"].at[1, src])
    around.begin()
    finish(bias_z)
    ring.end()

    def pair_rows(q, j):
        return pl.ds(pl.multiple_of((q * pairs + j) * 2 * per, 2 * per), 2 * per)

    def code_rows(j):
        return pl.ds(pl.multiple_of(j * per, per), per)

    def weight_rows(j):
        return pl.ds(pl.multiple_of(j * LANES, LANES), LANES)

    def own_pairs(ref, q, j):
        return ref.at[lax.div(q, 4), lax.rem(q, 4), code_rows(j), :]

    def groups(body):
        def produce(h, d):
            t = step(ids, "xy"[h], d)

            @pl.loop(0, 4)
            def _(k):
                q = 4 * k + t if h == 0 else 4 * t + k
                for j in range(pairs // 2):
                    body(q, h * (pairs // 2) + j)

        return produce

    def encode(q, j):
        mine = held[pair_rows(q, j), :].astype(bf)
        rows[pair_rows(q, j), :] = mine
        weight = enc_all[lax.div(q, 2), lax.rem(q, 2), :, weight_rows(j)]
        own_pairs(part, q, j)[...] = join_pair(dot(mine, weight, 1, 0)).astype(bf)

    def activate(h, acc):
        for k in range(pairs // 2):
            j = h * (pairs // 2) + k
            shift = bias_all[lax.div(me, 2), j // 2, pl.ds(2 * lax.rem(me, 2) + j % 2, 1), :]
            value, slope = gelu_parts(acc[k * per : (k + 1) * per] + shift)
            codes[y, x, j * per : (j + 1) * per] = value.astype(bf)
            slopes[j * per : (j + 1) * per, :] = slope

    stages = [v[k] for k in ("first", "second", "total")]
    nothing = lambda: None
    reduce_share(
        ids, part, codes, *stages, v["ssend"].at[0], v["srecv"].at[0], groups(encode), activate,
        [lambda: around.arrive(1), lambda: around.arrive(2), lambda: around.arrive(3), lambda: around.arrive(4), nothing],
    )
    around.end()

    @pl.loop(0, HOMES)
    def _(q):
        for j in range(pairs):
            weight = dec_all[lax.div(q, 2), lax.rem(q, 2), weight_rows(j), :]
            held[pair_rows(q, j), :] = dot(split_pair(own_pairs(codes, q, j)[...]), weight, 1, 0)

    @pl.loop(0, HOMES)
    def _(home):
        hots = [slot_onehot(pos_all, home, slot, blocks, tok) for slot in range(CAP)]
        rebuilt = jnp.zeros((tok, LANES), f32)
        for slot in range(CAP):
            some = held[pl.ds(slot * HOMES + home, blocks, per), :].astype(bf)
            rebuilt += dot(hots[slot], some, 0, 0)
        err = (rebuilt - tok_all[home].astype(f32)).astype(bf)
        for slot in range(CAP):
            held[pl.ds(slot * HOMES + home, blocks, per), :] = dot(hots[slot], err, 1, 0)

    def code_grad(q, j):
        err = held[pair_rows(q, j), :].astype(bf)
        weight = dec_all[lax.div(q, 2), lax.rem(q, 2), weight_rows(j), :]
        own_pairs(part, q, j)[...] = join_pair(dot(err, weight, 1, 1)).astype(bf)

    def dec_grad(q, j):
        err = held[pair_rows(q, j), :].astype(bf)
        return dot(split_pair(own_pairs(codes, q, j)[...]), err, 0, 0)

    def enc_grad(q, j):
        return dot(rows[pair_rows(q, j), :], split_pair(own_pairs(pgrad, q, j)[...]), 0, 0)

    def collect(m, grad, name):
        out, half_in, narrow, z_in, sums = (v[name + k] for k in ("out", "half", "narrow", "z_in", "sums"))

        def slot(ref, j, *lead):
            return ref.at[(*lead, slice(None), weight_rows(j))] if m else ref.at[(*lead, weight_rows(j))]

        sent = []

        def pass_on(copy, d, t):
            copy.wait()
            for j in range(pairs):
                acc = grad(2 * t + c, j) + slot(half_in, j, t)[...]
                if d == 0:
                    slot(sums, j)[...] = acc
                else:
                    slot(narrow, j, t)[...] = acc.astype(bf)
            if d:
                sems = [v[k].at[m, d - 1] for k in ("zsend", "zrecv")]
                sent.append(send(narrow.at[t], z_in.at[d - 1], *sems, {"z": t}))

        last = None
        for k, d in enumerate(FAR):
            t = step(ids, "z", d)
            for j in range(pairs):
                slot(out, j, k % 2)[...] = grad(2 * t + 1 - c, j)
            copy = send(out.at[k % 2], half_in.at[t], v["csend"].at[m, k], v["crecv"].at[m, k], other)
            if last is not None:
                pass_on(*last)
            last = (copy, d, t)
        pass_on(*last)
        return sent

    sent = []

    def multiply(h, acc):
        at = pl.ds(h * acc.shape[0], acc.shape[0])
        pgrad[y, x, at] = (acc * slopes[at, :]).astype(bf)

    reduce_share(
        ids, part, pgrad, *stages, v["ssend"].at[1], v["srecv"].at[1], groups(code_grad), multiply,
        [lambda: sent.extend(collect(0, dec_grad, "d_")), nothing, nothing, nothing, nothing],
    )
    dec_sent = list(sent)
    enc_sent = collect(1, enc_grad, "e_")

    homes = []
    for m, name, around_z, dst in ((0, "d_", dec_sent, dec_out), (1, "e_", enc_sent, enc_out)):
        finish(around_z)
        sums, z_in = v[name + "sums"], v[name + "z_in"]
        sums[...] += sum(z_in[d].astype(f32) for d in range(z_in.shape[0]))
        at = pl.ds(pl.multiple_of(c * lat, lat), lat)
        lanes = pl.ds(pl.multiple_of(lax.rem(x, 2) * LANES, LANES), LANES)
        items = []
        for t in range(4):
            piece = pl.ds(t * lat, lat)
            if m == 0:
                src, to = sums.at[piece], dst.at[at, lanes]
            else:
                src, to = sums.at[:, piece], dst.at[lanes, at]
            items.append(((m, t), (m, c, lax.rem(x, 2)), src, to, t, lax.div(x, 2)))
        homes += swap_homes(ids, items, _At(v["hsend"]), _At(v["hrecv"]))
    for m, dst in ((0, dec_out), (1, enc_out)):
        for h in range(2):
            for i in range(2):
                at, lanes = pl.ds(h * lat, lat), pl.ds(i * LANES, LANES)
                landed(dst.at[at, lanes] if m == 0 else dst.at[lanes, at], v["hrecv"].at[m, h, i])
    sent_homes(swaps)
    sent_homes(homes)


class _At:
    def __init__(self, ref):
        self.ref = ref

    @property
    def at(self):
        return self

    def __getitem__(self, index):
        return self.ref.at[index]


def sems(*shape):
    return pltpu.SemaphoreType.DMA(shape)


def local(
    tokens,
    block_ids,
    enc_bias,
    enc_master,
    dec_master,
    enc_first,
    enc_second,
    dec_first,
    dec_second,
):
    nz, nx = lax.axis_size("z"), lax.axis_size("x")
    ny, nc = lax.axis_size("y"), lax.axis_size("c")
    tok, width = tokens.shape
    lat, part = dec_master.shape
    blocks = lat // BLOCK * nz * nx
    half = lat // nc
    bf, f32 = jnp.bfloat16, jnp.float32

    per_half = half // BLOCK
    local_b = block_ids % (nc * per_half)
    shard = block_ids // (nc * per_half)
    place = (
        ((shard // nx) * nc + local_b // per_half) * nx + shard % nx
    ) * per_half + local_b % per_half

    per = CAP * HOMES
    rows_own = blocks // 2 // HOMES * per
    own_w = nx * half
    grid4 = (ny, nx, rows_own, LANES)
    w_enc, w_dec = (LANES, own_w), (own_w, LANES)
    scratch = {
        "held": pltpu.VMEM((blocks * per, LANES), f32),
        "rows": pltpu.VMEM((blocks * per, LANES), bf),
        "part": pltpu.VMEM(grid4, bf),
        "codes": pltpu.VMEM(grid4, bf),
        "pgrad": pltpu.VMEM(grid4, bf),
        "tok_all": pltpu.VMEM((HOMES, tok, LANES), bf),
        "pos_all": pltpu.VMEM((HOMES, 8, tok), jnp.int32),
        "enc_all": pltpu.VMEM((nz, nc) + w_enc, bf),
        "dec_all": pltpu.VMEM((nz, nc) + w_dec, bf),
        "slopes": pltpu.VMEM((rows_own, LANES), f32),
        "bias_all": pltpu.VMEM((nz, nx, lat // LANES, LANES), f32),
        "first": pltpu.VMEM((2, 3, 4, rows_own // 2, LANES), bf),
        "second": pltpu.VMEM((2, 3, rows_own // 2, LANES), f32),
        "total": pltpu.VMEM((2, 4, rows_own // 2, LANES), f32),
    }
    for name, shape in (("d_", w_dec), ("e_", w_enc)):
        scratch[name + "out"] = pltpu.VMEM((2,) + shape, f32)
        scratch[name + "half"] = pltpu.VMEM((nz,) + shape, f32)
        scratch[name + "narrow"] = pltpu.VMEM((nz,) + shape, bf)
        scratch[name + "z_in"] = pltpu.VMEM((nz - 1,) + shape, bf)
        scratch[name + "sums"] = pltpu.VMEM(shape, f32)
    for name, shape in (
        ("w", (2, 2, 2)), ("b", (3,)), ("t", (15,)), ("p", (15,)), ("er", (2, 4, 2)), ("ec", (8,)),
        ("dr", (2, 4, 2)), ("dc", (8,)), ("bz", (7,)), ("s", (2, 4, 2, 3)), ("c", (2, 8)), ("z", (2, 7)),
    ):
        scratch[name + "send"] = sems(*shape)
        scratch[name + "recv"] = sems(*((2, 4) if name == "w" else shape))
    scratch.update(lsem=sems(2), hsend=sems(2, 4), hrecv=sems(2, 2, 2))

    vmem = pl.BlockSpec(memory_space=pltpu.VMEM)
    enc_share, dec_share = pl.pallas_call(
        functools.partial(train_kernel, tuple(scratch)),
        out_shape=[jax.ShapeDtypeStruct((part, lat), f32), jax.ShapeDtypeStruct((lat, part), f32)],
        in_specs=[pl.BlockSpec(memory_space=pl.ANY)] + [vmem] * 4,
        out_specs=[vmem] * 2,
        scratch_shapes=list(scratch.values()),
        compiler_params=pltpu.CompilerParams(
            collective_id=1, has_side_effects=True, vmem_limit_bytes=VMEM
        ),
        name="train",
    )(tokens, place.T, enc_master.astype(bf), dec_master.astype(bf), enc_bias.reshape(-1, LANES))
    enc_new, enc_first_new, enc_second_new = adam(enc_master, enc_share, enc_first, enc_second)
    dec_new, dec_first_new, dec_second_new = adam(dec_master, dec_share, dec_first, dec_second)
    return (enc_new, dec_new, enc_first_new, enc_second_new, dec_first_new, dec_second_new)


def solution(mesh):
    grid = Mesh(mesh.devices.reshape(8, 4, 4, 2), ("z", "x", "y", "c"))
    lat, rep = ("z", "x"), REP
    tok = P(rep + lat, None)
    enc, dec = P(rep, lat), P(lat, rep)
    return jax.shard_map(
        local,
        mesh=grid,
        in_specs=(tok, tok, P(lat), enc, dec, enc, enc, dec, dec),
        out_specs=(enc, dec, enc, enc, dec, dec),
        check_vma=False,
    )
```

time: 452 us -> 265 us (0.59)
  Pallas kernels: 0 us -> 255 us
  waiting for transfers between devices: 206 us -> 0 us
  blocking collectives: 87.8 us -> 0 us
  starting transfers between devices: 52.1 us -> 0 us
  matrix products: 51.2 us -> 0 us
  local copies, waits for them, and re-layouts: 27 us -> 0.03 us
  between operations: 14.9 us -> 0.71 us
    pallas_call x0 -> x1, Pallas kernels: none -> 255 us  [local(): pl.pallas_call(functools.partial(train_kernel, tuple(scratch)), out_shape...]
    all_to_all x8 -> x0, waiting for transfers between devices: 206 us -> none  [the longest x2 107 us: exchange(): lax.all_to_all(rows, PLANE, split_axis=0, concat_axis=0, tiled=True)]
    all_to_all x1 -> x0, blocking collectives: 69.9 us -> none  [exchange(): lax.all_to_all(rows, PLANE, split_axis=0, concat_axis=0, tiled=True)]
    all_to_all x8 -> x0, starting transfers between devices: 52 us -> none  [the longest x2 17 us: exchange(): lax.all_to_all(rows, PLANE, split_axis=0, concat_axis=0, tiled=True)]
    dot_general x6 -> x0, matrix products: 51.2 us -> none  [dot(): lax.dot_general(a, b, (((ca,), (cb,)), ((), ())), preferred_element_type=...]
    unnamed x1 -> x0, blocking collectives: 17.9 us -> none
    unnamed x33 -> x14, local copies, waits for them, and re-layouts: 10.5 us -> 0.03 us
    eq x4 -> x0, local copies, waits for them, and re-layouts: 7.24 us -> none  [slot_onehot(): return chosen[:, None, :] & (places[:, None, :] == slots[None, :, None])]
  transfers between devices with their start and end apart: 10 -> 0, of which waited for: 7 -> 0; matrix products, arithmetic and copies ran while one was open for 12% -> 0% of each run, Pallas kernels for 0% -> 0%
where the time goes in v5:
time: 265 us
  Pallas kernels  255 us (96%)
  other arithmetic  8.91 us (3%)
    pallas_call x1, Pallas kernels, local(): pl.pallas_call(functools.partial(train_kernel, tuple(scratch)), out_shape...  255 us

profile of v5, /device:TPU:1, one launch (start us, length us, event | category | flops | bytes accessed | tf_op | source)
XLA Modules:
  0.0 264.8 jit_solution(6658918439639739196)
XLA Ops:
  0.6 1.3 fusion.5.refs_1_
  2.0 0.0 copy-start
  2.0 0.0 copy-start.2
  2.0 0.0 copy-start.3
  2.0 1.9 convert_element_type.6.refs_2_
  3.9 1.8 convert_element_type.7.refs_3_
  5.6 255.2 %train.1 = (f32[256,512]{1,0:T(8,128)}, f32[512,256]{1,0:T(8,128)}) custom-call(bf16[512,2048]{1,0:T(8,128)(2,1)} %refs_0_.1, s32[2,512]{1,0:T(2,128)} %fusion.5.refs_1_, bf16[256,512]{1,0:T(8,128)(2,1)} %convert_element_type.6.refs_2_, bf16[512,256]{1,0:T(8,128)(2,1)} %convert_element_type.7.refs_3_, f32[4,128]{1,0:T(4,128)} %bitcast.3), custom_call_target="tpu_custom_call" | custom-call | tf_op jit(solution)/shard_map/train/pallas_call | solution.py:576
  260.8 0.0 copy-start.1
  260.8 0.0 copy-start.4
  260.8 0.0 copy-start.5
  260.8 0.0 copy-start.6
  260.8 0.0 copy-done
  260.9 0.0 copy-done.2
  260.9 0.0 copy-done.3
  260.9 2.6 multiply_subtract_fusion.1
  263.4 0.0 copy-done.1
  263.4 0.0 copy-done.4
  263.4 0.0 copy-done.5
  263.4 0.0 copy-done.6
  263.5 1.4 multiply_subtract_fusion
Async XLA Ops:
  2.0 258.9 %copy-start = (f32[256,512]{1,0:T(8,128)S(1)}, f32[256,512]{1,0:T(8,128)}, u32[]{:S(2)}) copy-start(f32[256,512]{1,0:T(8,128)} %param.12) | copy-start | bytes 1572868
  2.0 258.9 %copy-start.2 = (f32[256,512]{1,0:T(8,128)S(1)}, f32[256,512]{1,0:T(8,128)}, u32[]{:S(2)}) copy-start(f32[256,512]{1,0:T(8,128)} %param.14) | copy-start | bytes 1572868
  2.0 258.9 %copy-start.3 = (f32[256,512]{1,0:T(8,128)S(1)}, f32[256,512]{1,0:T(8,128)}, u32[]{:S(2)}) copy-start(f32[256,512]{1,0:T(8,128)} %param.15) | copy-start | bytes 1572868
  260.8 2.6 copy-start.1
  260.8 2.6 copy-start.4
  260.8 2.6 copy-start.5
  260.8 2.6 copy-start.6

commit v6 on v5

--- a/solution.py
+++ b/solution.py
@@ -97,14 +97,11 @@
     half = part.shape[2] // 2
     top, low = pl.ds(0, half), pl.ds(half, half)
 
-    def stage(k, pairs, before=None):
+    def stage(k, h, pairs):
         copies = []
         for d in (1, 3, 2):
-            for h in range(2):
-                if before is not None:
-                    before(h, d)
-                src, dst, peer = pairs(h, d)
-                copies.append(send(src, dst, ssem.at[k, h, d - 1], rsem.at[k, h, d - 1], peer))
+            src, dst, peer = pairs(h, d)
+            copies.append(send(src, dst, ssem.at[k, h, d - 1], rsem.at[k, h, d - 1], peer))
         return copies
 
     def one(h, d):
@@ -114,49 +111,52 @@
         t = step(ids, "y", d)
         return part.at[t, :, low], first.at[1, d - 1], {"y": t}
 
-    copies = stage(0, one, produce)
+    def two(h, d):
+        axis = "y" if h == 0 else "x"
+        t = step(ids, axis, d)
+        return total.at[h, t], second.at[h, d - 1], {axis: t}
+
+    def three(h, d):
+        axis, rows = ("y", top) if h == 0 else ("x", low)
+        return out.at[y, x, rows], out.at[y, x, rows], {axis: step(ids, axis, d)}
+
+    def four(h, d):
+        if h == 0:
+            return out.at[:, x, top], out.at[:, x, top], {"x": step(ids, "x", d)}
+        return out.at[y, :, low], out.at[y, :, low], {"y": step(ids, "y", d)}
+
+    sent = [[], []]
+    for d in (1, 3, 2):
+        for h in range(2):
+            produce(h, d)
+            src, dst, peer = one(h, d)
+            sent[h].append(send(src, dst, ssem.at[0, h, d - 1], rsem.at[0, h, d - 1], peer))
     produce(0, 0)
     produce(1, 0)
     hooks[0]()
-    finish(copies)
-    hooks[1]()
-    for k in range(4):
-        for h, own in ((0, part.at[k, x, top]), (1, part.at[y, k, low])):
+    for h in range(2):
+        finish(sent[h])
+        for k in range(4):
+            own = part.at[k, x, top] if h == 0 else part.at[y, k, low]
             acc = own[...].astype(jnp.float32)
             for d in range(3):
                 acc += first[h, d, k].astype(jnp.float32)
             total[h, k] = acc
-
-    def two(h, d):
-        axis = "y" if h == 0 else "x"
-        t = step(ids, axis, d)
-        return total.at[h, t], second.at[h, d - 1], {axis: t}
-
-    copies = stage(1, two)
-    hooks[2]()
-    finish(copies)
+        sent[h] = stage(1, h, two)
+    hooks[1]()
     for h, mine in ((0, y), (1, x)):
+        finish(sent[h])
         acc = total[h, mine]
         for d in range(3):
             acc += second[h, d]
         middle(h, acc)
-
-    def three(h, d):
-        axis, rows = ("y", top) if h == 0 else ("x", low)
-        return out.at[y, x, rows], out.at[y, x, rows], {axis: step(ids, axis, d)}
-
-    copies = stage(2, three)
+        sent[h] = stage(2, h, three)
+    hooks[2]()
+    for h in range(2):
+        finish(sent[h])
+        sent[h] = stage(3, h, four)
     hooks[3]()
-    finish(copies)
-
-    def four(h, d):
-        if h == 0:
-            return out.at[:, x, top], out.at[:, x, top], {"x": step(ids, "x", d)}
-        return out.at[y, :, low], out.at[y, :, low], {"y": step(ids, "y", d)}
-
-    copies = stage(3, four)
-    hooks[4]()
-    finish(copies)
+    finish(sent[0] + sent[1])
 
 
 def gelu_parts(v):
@@ -389,10 +389,9 @@
             slopes[j * per : (j + 1) * per, :] = slope
 
     stages = [v[k] for k in ("first", "second", "total")]
-    nothing = lambda: None
     reduce_share(
         ids, part, codes, *stages, v["ssend"].at[0], v["srecv"].at[0], groups(encode), activate,
-        [lambda: around.arrive(1), lambda: around.arrive(2), lambda: around.arrive(3), lambda: around.arrive(4), nothing],
+        [lambda k=k: around.arrive(k) for k in range(1, 5)],
     )
     around.end()
 
@@ -402,16 +401,16 @@
             weight = dec_all[lax.div(q, 2), lax.rem(q, 2), weight_rows(j), :]
             held[pair_rows(q, j), :] = dot(split_pair(own_pairs(codes, q, j)[...]), weight, 1, 0)
 
-    @pl.loop(0, HOMES)
+    @pl.loop(0, HOMES, unroll=2)
     def _(home):
-        hots = [slot_onehot(pos_all, home, slot, blocks, tok) for slot in range(CAP)]
-        rebuilt = jnp.zeros((tok, LANES), f32)
+        hots = jnp.concatenate([slot_onehot(pos_all, home, slot, blocks, tok) for slot in range(CAP)], axis=0)
+        at = [pl.ds(slot * HOMES + home, blocks, per) for slot in range(CAP)]
+        some = jnp.concatenate([held[a, :].astype(bf) for a in at], axis=0)
+        rebuilt = dot(some, hots, 0, 0)
+        err = (rebuilt - tok_all[home].astype(f32).T).astype(bf)
+        picked = dot(hots, err, 1, 1)
         for slot in range(CAP):
-            some = held[pl.ds(slot * HOMES + home, blocks, per), :].astype(bf)
-            rebuilt += dot(hots[slot], some, 0, 0)
-        err = (rebuilt - tok_all[home].astype(f32)).astype(bf)
-        for slot in range(CAP):
-            held[pl.ds(slot * HOMES + home, blocks, per), :] = dot(hots[slot], err, 1, 0)
+            held[at[slot], :] = picked[slot * blocks : (slot + 1) * blocks]
 
     def code_grad(q, j):
         err = held[pair_rows(q, j), :].astype(bf)
@@ -431,17 +430,54 @@
         def slot(ref, j, *lead):
             return ref.at[(*lead, slice(None), weight_rows(j))] if m else ref.at[(*lead, weight_rows(j))]
 
-        sent = []
+        sent, chain = [], {}
+
+        def cut_rows(way):
+            cut = z_in.shape[2] // 2
+            return pl.ds(way * cut, cut)
+
+        def ring_on(d, t):
+            ways = (0, 1) if d == 4 else (0,) if 0 < d < 4 else (1,) if d else ()
+            for way in ways:
+                k = min(d, 8 - d)
+                src, dst = narrow.at[t], z_in.at[way, k - 1]
+                if k == 4:
+                    src, dst = narrow.at[t, cut_rows(way)], z_in.at[way, 3, cut_rows(way)]
+                sems = [v[n].at[way, k - 1] for n in ("grsend", "grrecv")]
+                chain[way, k] = send(src, dst, *sems, {"z": step(ids, "z", 1 - 2 * way)})
+                sent.append(chain[way, k])
 
         def pass_on(copy, d, t):
             copy.wait()
+            way, k = (0, d) if d < 4 else (1, 8 - d)
+            if m and d == 0:
+                chain[0, 1].wait_recv()
+                chain[1, 1].wait_recv()
+            elif m and d != 4:
+                chain[way, k + 1].wait_recv()
             for j in range(pairs):
                 acc = grad(2 * t + c, j) + slot(half_in, j, t)[...]
+                if m and d and d != 4:
+                    came = slot(z_in, j, way, k)
+                    if k == 3:
+                        cut = acc.shape[0] // 2
+                        lower, upper = acc[:cut], acc[cut:]
+                        if way == 0:
+                            lower += came[:cut].astype(f32)
+                        else:
+                            upper += came[cut:].astype(f32)
+                        acc = jnp.concatenate([lower, upper], axis=0)
+                    else:
+                        acc += came[...].astype(f32)
+                if m and d == 0:
+                    acc += slot(z_in, j, 0, 0)[...].astype(f32) + slot(z_in, j, 1, 0)[...].astype(f32)
                 if d == 0:
                     slot(sums, j)[...] = acc
                 else:
                     slot(narrow, j, t)[...] = acc.astype(bf)
-            if d:
+            if m:
+                ring_on(d, t)
+            elif d:
                 sems = [v[k].at[m, d - 1] for k in ("zsend", "zrecv")]
                 sent.append(send(narrow.at[t], z_in.at[d - 1], *sems, {"z": t}))
 
@@ -465,16 +501,20 @@
 
     reduce_share(
         ids, part, pgrad, *stages, v["ssend"].at[1], v["srecv"].at[1], groups(code_grad), multiply,
-        [lambda: sent.extend(collect(0, dec_grad, "d_")), nothing, nothing, nothing, nothing],
+        [lambda: sent.extend(collect(0, dec_grad, "d_"))] + [lambda: None] * 3,
     )
     dec_sent = list(sent)
     enc_sent = collect(1, enc_grad, "e_")
 
     homes = []
     for m, name, around_z, dst in ((0, "d_", dec_sent, dec_out), (1, "e_", enc_sent, enc_out)):
-        finish(around_z)
         sums, z_in = v[name + "sums"], v[name + "z_in"]
-        sums[...] += sum(z_in[d].astype(f32) for d in range(z_in.shape[0]))
+        if m == 0:
+            finish(around_z)
+            sums[...] += sum(z_in[d].astype(f32) for d in range(z_in.shape[0]))
+        else:
+            for copy in around_z:
+                copy.wait_send()
         at = pl.ds(pl.multiple_of(c * lat, lat), lat)
         lanes = pl.ds(pl.multiple_of(lax.rem(x, 2) * LANES, LANES), LANES)
         items = []
@@ -562,11 +602,12 @@
         scratch[name + "out"] = pltpu.VMEM((2,) + shape, f32)
         scratch[name + "half"] = pltpu.VMEM((nz,) + shape, f32)
         scratch[name + "narrow"] = pltpu.VMEM((nz,) + shape, bf)
-        scratch[name + "z_in"] = pltpu.VMEM((nz - 1,) + shape, bf)
+        lead = (nz - 1,) if name == "d_" else (2, nz // 2)
+        scratch[name + "z_in"] = pltpu.VMEM(lead + shape, bf)
         scratch[name + "sums"] = pltpu.VMEM(shape, f32)
     for name, shape in (
         ("w", (2, 2, 2)), ("b", (3,)), ("t", (15,)), ("p", (15,)), ("er", (2, 4, 2)), ("ec", (8,)),
-        ("dr", (2, 4, 2)), ("dc", (8,)), ("bz", (7,)), ("s", (2, 4, 2, 3)), ("c", (2, 8)), ("z", (2, 7)),
+        ("dr", (2, 4, 2)), ("dc", (8,)), ("bz", (7,)), ("s", (2, 4, 2, 3)), ("gr", (2, 4)), ("c", (2, 8)), ("z", (1, 7)),
     ):
         scratch[name + "send"] = sems(*shape)
         scratch[name + "recv"] = sems(*((2, 4) if name == "w" else shape))

time: 265 us -> 237 us (0.89)
  Pallas kernels: 255 us -> 227 us
    pallas_call x1, Pallas kernels: 255 us -> 227 us  [local(): pl.pallas_call(functools.partial(train_kernel, tuple(scratch)), out_shape...]
where the time goes in v6:
time: 237 us
  Pallas kernels  227 us (96%)
  other arithmetic  8.91 us (4%)
    pallas_call x1, Pallas kernels, local(): pl.pallas_call(functools.partial(train_kernel, tuple(scratch)), out_shape...  227 us

profile of v6, /device:TPU:1, one launch (start us, length us, event | category | flops | bytes accessed | tf_op | source)
XLA Modules:
  0.0 237.1 jit_solution(4851011382372862952)
XLA Ops:
  0.6 1.3 fusion.5.refs_1_
  2.0 0.0 copy-start
  2.0 0.0 copy-start.2
  2.0 0.0 copy-start.3
  2.0 1.9 convert_element_type.6.refs_2_
  3.9 1.8 convert_element_type.7.refs_3_
  5.6 227.5 %train.1 = (f32[256,512]{1,0:T(8,128)}, f32[512,256]{1,0:T(8,128)}) custom-call(bf16[512,2048]{1,0:T(8,128)(2,1)} %refs_0_.1, s32[2,512]{1,0:T(2,128)} %fusion.5.refs_1_, bf16[256,512]{1,0:T(8,128)(2,1)} %convert_element_type.6.refs_2_, bf16[512,256]{1,0:T(8,128)(2,1)} %convert_element_type.7.refs_3_, f32[4,128]{1,0:T(4,128)} %bitcast.3), custom_call_target="tpu_custom_call" | custom-call | tf_op jit(solution)/shard_map/train/pallas_call | solution.py:617
  233.1 0.0 copy-start.1
  233.1 0.0 copy-start.4
  233.1 0.0 copy-start.5
  233.1 0.0 copy-start.6
  233.1 0.0 copy-done
  233.2 0.0 copy-done.2
  233.2 0.0 copy-done.3
  233.2 2.6 %multiply_subtract_fusion.1 = (f32[256,512]{1,0:T(8,128)}, f32[256,512]{1,0:T(8,128)}, f32[256,512]{1,0:T(8,128)}) fusion(f32[256,512]{1,0:T(8,128)S(1)} %copy-done, f32[256,512]{1,0:T(8,128)} %get-tuple-element.8, f32[256,512]{1,0:T(8,128)S(1)} %copy-done.2, f32[256,512]{1,0:T(8,128)S(1)} %copy-done.3), kind=kLoop, calls=%fused_computation.6 | loop fusion | flops 1703936 | bytes 3670016 | tf_op jit(solution)/shard_map/sub | solution.py:29
  235.7 0.0 copy-done.1
  235.7 0.0 copy-done.4
  235.7 0.0 copy-done.5
  235.7 0.0 copy-done.6
  235.8 1.4 multiply_subtract_fusion
Async XLA Ops:
  2.0 231.2 %copy-start = (f32[256,512]{1,0:T(8,128)S(1)}, f32[256,512]{1,0:T(8,128)}, u32[]{:S(2)}) copy-start(f32[256,512]{1,0:T(8,128)} %param.12) | copy-start | bytes 1572868
  2.0 231.2 %copy-start.2 = (f32[256,512]{1,0:T(8,128)S(1)}, f32[256,512]{1,0:T(8,128)}, u32[]{:S(2)}) copy-start(f32[256,512]{1,0:T(8,128)} %param.14) | copy-start | bytes 1572868
  2.0 231.2 %copy-start.3 = (f32[256,512]{1,0:T(8,128)S(1)}, f32[256,512]{1,0:T(8,128)}, u32[]{:S(2)}) copy-start(f32[256,512]{1,0:T(8,128)} %param.15) | copy-start | bytes 1572868
  233.1 2.6 %copy-start.1 = (f32[512,256]{1,0:T(8,128)S(1)}, f32[512,256]{1,0:T(8,128)}, u32[]{:S(2)}) copy-start(f32[512,256]{1,0:T(8,128)} %param.13) | copy-start | bytes 1572868
  233.1 2.6 %copy-start.4 = (f32[512,256]{1,0:T(8,128)S(1)}, f32[512,256]{1,0:T(8,128)}, u32[]{:S(2)}) copy-start(f32[512,256]{1,0:T(8,128)} %param.16) | copy-start | bytes 1572868
  233.1 2.6 %copy-start.5 = (f32[512,256]{1,0:T(8,128)S(1)}, f32[512,256]{1,0:T(8,128)}, u32[]{:S(2)}) copy-start(f32[512,256]{1,0:T(8,128)} %param.17) | copy-start | bytes 1572868
  233.1 2.6 %copy-start.6 = (f32[512,256]{1,0:T(8,128)S(1)}, f32[512,256]{1,0:T(8,128)}, u32[]{:S(2)}) copy-start(f32[512,256]{1,0:T(8,128)} %get-tuple-element.9) | copy-start | bytes 1572868

commit v7 on v6

--- a/solution.py
+++ b/solution.py
@@ -92,71 +92,75 @@
     return [{axis: step(ids, axis, d)} for d in range(1, lax.axis_size(axis))]
 
 
+CHAINS = 2
+
+
 def reduce_share(ids, part, out, first, second, total, ssem, rsem, produce, middle, hooks):
     x, y = ids["x"], ids["y"]
-    half = part.shape[2] // 2
-    top, low = pl.ds(0, half), pl.ds(half, half)
+    count = part.shape[2] // CHAINS
+    chains = range(CHAINS)
+    cut = [pl.ds(h * count, count) for h in chains]
+
+    def start(k, h, d, src, dst, peer):
+        return send(src, dst, ssem.at[k, h, d - 1], rsem.at[k, h, d - 1], peer)
 
     def stage(k, h, pairs):
-        copies = []
-        for d in (1, 3, 2):
-            src, dst, peer = pairs(h, d)
-            copies.append(send(src, dst, ssem.at[k, h, d - 1], rsem.at[k, h, d - 1], peer))
-        return copies
+        return [start(k, h, d, *pairs(h, d)) for d in (1, 3, 2)]
 
     def one(h, d):
-        if h == 0:
-            t = step(ids, "x", d)
-            return part.at[:, t, top], first.at[0, d - 1], {"x": t}
-        t = step(ids, "y", d)
-        return part.at[t, :, low], first.at[1, d - 1], {"y": t}
+        axis = "xy"[h % 2]
+        t = step(ids, axis, d)
+        src = part.at[:, t, cut[h]] if axis == "x" else part.at[t, :, cut[h]]
+        return src, first.at[h, d - 1], {axis: t}
 
     def two(h, d):
-        axis = "y" if h == 0 else "x"
+        axis = "yx"[h % 2]
         t = step(ids, axis, d)
         return total.at[h, t], second.at[h, d - 1], {axis: t}
 
     def three(h, d):
-        axis, rows = ("y", top) if h == 0 else ("x", low)
-        return out.at[y, x, rows], out.at[y, x, rows], {axis: step(ids, axis, d)}
+        axis = "yx"[h % 2]
+        mine = out.at[y, x, cut[h]]
+        return mine, mine, {axis: step(ids, axis, d)}
 
     def four(h, d):
-        if h == 0:
-            return out.at[:, x, top], out.at[:, x, top], {"x": step(ids, "x", d)}
-        return out.at[y, :, low], out.at[y, :, low], {"y": step(ids, "y", d)}
-
-    sent = [[], []]
-    for d in (1, 3, 2):
-        for h in range(2):
-            produce(h, d)
-            src, dst, peer = one(h, d)
-            sent[h].append(send(src, dst, ssem.at[0, h, d - 1], rsem.at[0, h, d - 1], peer))
-    produce(0, 0)
-    produce(1, 0)
+        axis = "xy"[h % 2]
+        mine = out.at[:, x, cut[h]] if axis == "x" else out.at[y, :, cut[h]]
+        return mine, mine, {axis: step(ids, axis, d)}
+
+    sent = [[] for h in chains]
+    for pair in range(0, CHAINS, 2):
+        for d in (1, 3, 2):
+            for h in (pair, pair + 1):
+                produce(h, d)
+                sent[h].append(start(0, h, d, *one(h, d)))
+    for h in chains:
+        produce(h, 0)
     hooks[0]()
-    for h in range(2):
+    for h in chains:
         finish(sent[h])
         for k in range(4):
-            own = part.at[k, x, top] if h == 0 else part.at[y, k, low]
+            own = part.at[k, x, cut[h]] if h % 2 == 0 else part.at[y, k, cut[h]]
             acc = own[...].astype(jnp.float32)
             for d in range(3):
                 acc += first[h, d, k].astype(jnp.float32)
             total[h, k] = acc
         sent[h] = stage(1, h, two)
     hooks[1]()
-    for h, mine in ((0, y), (1, x)):
+    for h in chains:
         finish(sent[h])
-        acc = total[h, mine]
+        acc = total[h, x if h % 2 else y]
         for d in range(3):
             acc += second[h, d]
         middle(h, acc)
         sent[h] = stage(2, h, three)
     hooks[2]()
-    for h in range(2):
+    for h in chains:
         finish(sent[h])
         sent[h] = stage(3, h, four)
     hooks[3]()
-    finish(sent[0] + sent[1])
+    for h in chains:
+        finish(sent[h])
 
 
 def gelu_parts(v):
@@ -247,12 +251,17 @@
     (1, 0), (0, 1), (3, 0), (0, 3), (1, 1), (3, 3), (1, 3), (3, 1),
     (2, 0), (0, 2), (1, 2), (2, 1), (3, 2), (2, 3), (2, 2),
 )
+NEAR = 8
 FAR = (4, 3, 5, 2, 6, 1, 7, 0)
+SLOTS = 4
 
 
 def train_kernel(names, *refs):
-    tokens, place, enc, dec, bias, enc_out, dec_out = refs[:7]
+    tokens, place, enc_wide, dec_wide, bias, enc_out, dec_out = refs[:7]
     v = dict(zip(names, refs[7:]))
+    enc, dec = v["enc"], v["dec"]
+    enc[...] = enc_wide[...].astype(jnp.bfloat16)
+    dec[...] = dec_wide[...].astype(jnp.bfloat16)
     ids = axis_ids()
     x, y, z, c = ids["x"], ids["y"], ids["z"], ids["c"]
     me = y * 4 + x
@@ -296,11 +305,16 @@
     ]
     for copy in keep:
         copy.start()
-    got = []
-    for n, (a, b) in enumerate(PLANE):
-        t = step(ids, "y", a) * 4 + step(ids, "x", b)
-        src = tokens.at[:, pl.ds(pl.multiple_of(t * LANES, LANES), LANES)]
-        got.append(send(src, tok_all.at[me], v["tsend"].at[n], v["trecv"].at[n], peers[n]))
+    def send_tokens(numbers):
+        copies = []
+        for n in numbers:
+            a, b = PLANE[n]
+            t = step(ids, "y", a) * 4 + step(ids, "x", b)
+            src = tokens.at[:, pl.ds(pl.multiple_of(t * LANES, LANES), LANES)]
+            copies.append(send(src, tok_all.at[me], v["tsend"].at[n], v["trecv"].at[n], peers[n]))
+        return copies
+
+    near = send_tokens(range(NEAR))
 
     numbers = lax.broadcasted_iota(jnp.int32, (blocks, tok), 0)
     named = [numbers == place[k : k + 1, :] for k in range(2)]
@@ -312,9 +326,10 @@
     for k in range(2):
         rank = jnp.sum(jnp.where(named[k], count, zero), axis=0, keepdims=True).astype(jnp.int32)
         pos_all[me, k : k + 1, :] = rank * blocks + place[k : k + 1, :]
-    got += [
+    ranks = [
         send(pos_all.at[me], pos_all.at[me], v["psend"].at[n], v["precv"].at[n], peers[n]) for n in range(15)
     ]
+    distant = send_tokens(range(NEAR, 15))
 
     ring = ZRing(ids, enc_all, v["ersend"], v["errecv"], v["ecsend"], v["ecrecv"])
     for src in range(4):
@@ -328,20 +343,26 @@
     ]
     ring.arrive(1)
     ring.arrive(2)
-    finish(got)
-    keep[1].wait()
-
-    def gather(homes):
-        @pl.loop(*homes)
-        def _(home):
+    def gather(count, offsets):
+        @pl.loop(0, count)
+        def _(n):
+            a, b = offsets(n)
+            home = lax.rem(y + 4 - a, 4) * 4 + lax.rem(x + 4 - b, 4)
             mine = tok_all[home]
             for slot in range(CAP):
                 picked = dot(slot_onehot(pos_all, home, slot, blocks, tok), mine, 1, 0)
                 held[pl.ds(slot * HOMES + home, blocks, per), :] = picked
 
-    gather((0, 8))
+    def skip_two(n):
+        return n + lax.div(n, 2)
+
+    finish(near + ranks[:NEAR])
+    keep[1].wait()
+    gather(NEAR + 1, lambda n: (skip_two(lax.div(n, 3)), skip_two(lax.rem(n, 3))))
     ring.arrive(3)
-    gather((8, 16))
+    finish(distant + ranks[NEAR:])
+    gather(4, lambda n: (2, n))
+    gather(3, lambda n: (skip_two(n), 2))
     ring.arrive(4)
     around = ZRing(ids, dec_all, v["drsend"], v["drrecv"], v["dcsend"], v["dcrecv"])
     for src in range(4):
@@ -364,13 +385,13 @@
 
     def groups(body):
         def produce(h, d):
-            t = step(ids, "xy"[h], d)
+            t = step(ids, "xy"[h % 2], d)
 
             @pl.loop(0, 4)
             def _(k):
-                q = 4 * k + t if h == 0 else 4 * t + k
-                for j in range(pairs // 2):
-                    body(q, h * (pairs // 2) + j)
+                q = 4 * k + t if h % 2 == 0 else 4 * t + k
+                for j in range(pairs // CHAINS):
+                    body(q, h * (pairs // CHAINS) + j)
 
         return produce
 
@@ -381,8 +402,8 @@
         own_pairs(part, q, j)[...] = join_pair(dot(mine, weight, 1, 0)).astype(bf)
 
     def activate(h, acc):
-        for k in range(pairs // 2):
-            j = h * (pairs // 2) + k
+        for k in range(pairs // CHAINS):
+            j = h * (pairs // CHAINS) + k
             shift = bias_all[lax.div(me, 2), j // 2, pl.ds(2 * lax.rem(me, 2) + j % 2, 1), :]
             value, slope = gelu_parts(acc[k * per : (k + 1) * per] + shift)
             codes[y, x, j * per : (j + 1) * per] = value.astype(bf)
@@ -424,42 +445,47 @@
     def enc_grad(q, j):
         return dot(rows[pair_rows(q, j), :], split_pair(own_pairs(pgrad, q, j)[...]), 0, 0)
 
-    def collect(m, grad, name):
+    def collect(m, grad, name, chain):
         out, half_in, narrow, z_in, sums = (v[name + k] for k in ("out", "half", "narrow", "z_in", "sums"))
 
         def slot(ref, j, *lead):
             return ref.at[(*lead, slice(None), weight_rows(j))] if m else ref.at[(*lead, weight_rows(j))]
 
-        sent, chain = [], {}
 
         def cut_rows(way):
             cut = z_in.shape[2] // 2
             return pl.ds(way * cut, cut)
 
-        def ring_on(d, t):
+        def ring_on(d, n):
             ways = (0, 1) if d == 4 else (0,) if 0 < d < 4 else (1,) if d else ()
             for way in ways:
                 k = min(d, 8 - d)
-                src, dst = narrow.at[t], z_in.at[way, k - 1]
+                src, dst = narrow.at[n % SLOTS], z_in.at[way, k - 1]
                 if k == 4:
-                    src, dst = narrow.at[t, cut_rows(way)], z_in.at[way, 3, cut_rows(way)]
-                sems = [v[n].at[way, k - 1] for n in ("grsend", "grrecv")]
+                    src, dst = narrow.at[n % SLOTS, cut_rows(way)], z_in.at[way, 3, cut_rows(way)]
+                sems = [v[e].at[m, way, k - 1] for e in ("grsend", "grrecv")]
                 chain[way, k] = send(src, dst, *sems, {"z": step(ids, "z", 1 - 2 * way)})
-                sent.append(chain[way, k])
-
-        def pass_on(copy, d, t):
+
+        def pass_on(copy, d, t, n):
             copy.wait()
+            if d and n >= SLOTS:
+                freed = FAR[n - SLOTS]
+                for way in range(2) if freed == 4 else [int(freed > 4)]:
+                    chain.pop((way, min(freed, 8 - freed))).wait_send()
             way, k = (0, d) if d < 4 else (1, 8 - d)
-            if m and d == 0:
+            if d == 0:
                 chain[0, 1].wait_recv()
                 chain[1, 1].wait_recv()
-            elif m and d != 4:
+            elif d != 4:
                 chain[way, k + 1].wait_recv()
             for j in range(pairs):
                 acc = grad(2 * t + c, j) + slot(half_in, j, t)[...]
-                if m and d and d != 4:
+                if d and d != 4:
                     came = slot(z_in, j, way, k)
-                    if k == 3:
+                    if k == 3 and m == 0:
+                        if (j >= pairs // 2) == (way == 1):
+                            acc += came[...].astype(f32)
+                    elif k == 3:
                         cut = acc.shape[0] // 2
                         lower, upper = acc[:cut], acc[cut:]
                         if way == 0:
@@ -469,17 +495,13 @@
                         acc = jnp.concatenate([lower, upper], axis=0)
                     else:
                         acc += came[...].astype(f32)
-                if m and d == 0:
+                if d == 0:
                     acc += slot(z_in, j, 0, 0)[...].astype(f32) + slot(z_in, j, 1, 0)[...].astype(f32)
                 if d == 0:
                     slot(sums, j)[...] = acc
                 else:
-                    slot(narrow, j, t)[...] = acc.astype(bf)
-            if m:
-                ring_on(d, t)
-            elif d:
-                sems = [v[k].at[m, d - 1] for k in ("zsend", "zrecv")]
-                sent.append(send(narrow.at[t], z_in.at[d - 1], *sems, {"z": t}))
+                    slot(narrow, j, n % SLOTS)[...] = acc.astype(bf)
+            ring_on(d, n)
 
         last = None
         for k, d in enumerate(FAR):
@@ -489,11 +511,16 @@
             copy = send(out.at[k % 2], half_in.at[t], v["csend"].at[m, k], v["crecv"].at[m, k], other)
             if last is not None:
                 pass_on(*last)
-            last = (copy, d, t)
+            last = (copy, d, t, k)
+            yield
         pass_on(*last)
-        return sent
-
-    sent = []
+        yield
+
+    dec_chain, enc_chain = {}, {}
+    dec_steps = collect(0, dec_grad, "d_", dec_chain)
+
+    def advance(n):
+        return lambda: [next(dec_steps) for _ in range(n)]
 
     def multiply(h, acc):
         at = pl.ds(h * acc.shape[0], acc.shape[0])
@@ -501,20 +528,16 @@
 
     reduce_share(
         ids, part, pgrad, *stages, v["ssend"].at[1], v["srecv"].at[1], groups(code_grad), multiply,
-        [lambda: sent.extend(collect(0, dec_grad, "d_"))] + [lambda: None] * 3,
+        [advance(4), advance(2), advance(2), advance(1)],
     )
-    dec_sent = list(sent)
-    enc_sent = collect(1, enc_grad, "e_")
+    for _ in collect(1, enc_grad, "e_", enc_chain):
+        pass
 
     homes = []
-    for m, name, around_z, dst in ((0, "d_", dec_sent, dec_out), (1, "e_", enc_sent, enc_out)):
-        sums, z_in = v[name + "sums"], v[name + "z_in"]
-        if m == 0:
-            finish(around_z)
-            sums[...] += sum(z_in[d].astype(f32) for d in range(z_in.shape[0]))
-        else:
-            for copy in around_z:
-                copy.wait_send()
+    for m, name, chain, dst in ((0, "d_", dec_chain, dec_out), (1, "e_", enc_chain, enc_out)):
+        sums = v[name + "sums"]
+        for copy in chain.values():
+            copy.wait_send()
         at = pl.ds(pl.multiple_of(c * lat, lat), lat)
         lanes = pl.ds(pl.multiple_of(lax.rem(x, 2) * LANES, LANES), LANES)
         items = []
@@ -583,6 +606,8 @@
     grid4 = (ny, nx, rows_own, LANES)
     w_enc, w_dec = (LANES, own_w), (own_w, LANES)
     scratch = {
+        "enc": pltpu.VMEM((part, lat), bf),
+        "dec": pltpu.VMEM((lat, part), bf),
         "held": pltpu.VMEM((blocks * per, LANES), f32),
         "rows": pltpu.VMEM((blocks * per, LANES), bf),
         "part": pltpu.VMEM(grid4, bf),
@@ -594,20 +619,19 @@
         "dec_all": pltpu.VMEM((nz, nc) + w_dec, bf),
         "slopes": pltpu.VMEM((rows_own, LANES), f32),
         "bias_all": pltpu.VMEM((nz, nx, lat // LANES, LANES), f32),
-        "first": pltpu.VMEM((2, 3, 4, rows_own // 2, LANES), bf),
-        "second": pltpu.VMEM((2, 3, rows_own // 2, LANES), f32),
-        "total": pltpu.VMEM((2, 4, rows_own // 2, LANES), f32),
+        "first": pltpu.VMEM((CHAINS, 3, 4, rows_own // CHAINS, LANES), bf),
+        "second": pltpu.VMEM((CHAINS, 3, rows_own // CHAINS, LANES), f32),
+        "total": pltpu.VMEM((CHAINS, 4, rows_own // CHAINS, LANES), f32),
     }
     for name, shape in (("d_", w_dec), ("e_", w_enc)):
         scratch[name + "out"] = pltpu.VMEM((2,) + shape, f32)
         scratch[name + "half"] = pltpu.VMEM((nz,) + shape, f32)
-        scratch[name + "narrow"] = pltpu.VMEM((nz,) + shape, bf)
-        lead = (nz - 1,) if name == "d_" else (2, nz // 2)
-        scratch[name + "z_in"] = pltpu.VMEM(lead + shape, bf)
+        scratch[name + "narrow"] = pltpu.VMEM((SLOTS,) + shape, bf)
+        scratch[name + "z_in"] = pltpu.VMEM((2, nz // 2) + shape, bf)
         scratch[name + "sums"] = pltpu.VMEM(shape, f32)
     for name, shape in (
         ("w", (2, 2, 2)), ("b", (3,)), ("t", (15,)), ("p", (15,)), ("er", (2, 4, 2)), ("ec", (8,)),
-        ("dr", (2, 4, 2)), ("dc", (8,)), ("bz", (7,)), ("s", (2, 4, 2, 3)), ("gr", (2, 4)), ("c", (2, 8)), ("z", (1, 7)),
+        ("dr", (2, 4, 2)), ("dc", (8,)), ("bz", (7,)), ("s", (2, 4, CHAINS, 3)), ("gr", (2, 2, 4)), ("c", (2, 8)),
     ):
         scratch[name + "send"] = sems(*shape)
         scratch[name + "recv"] = sems(*((2, 4) if name == "w" else shape))
@@ -624,7 +648,7 @@
             collective_id=1, has_side_effects=True, vmem_limit_bytes=VMEM
         ),
         name="train",
-    )(tokens, place.T, enc_master.astype(bf), dec_master.astype(bf), enc_bias.reshape(-1, LANES))
+    )(tokens, place.T, enc_master, dec_master, enc_bias.reshape(-1, LANES))
     enc_new, enc_first_new, enc_second_new = adam(enc_master, enc_share, enc_first, enc_second)
     dec_new, dec_first_new, dec_second_new = adam(dec_master, dec_share, dec_first, dec_second)
     return (enc_new, dec_new, enc_first_new, enc_second_new, dec_first_new, dec_second_new)

time: 237 us -> 223 us (0.941)
  Pallas kernels: 227 us -> 217 us
  other arithmetic: 8.91 us -> 5.36 us
    pallas_call x1, Pallas kernels: 227 us -> 217 us  [local(): pl.pallas_call(functools.partial(train_kernel, tuple(scratch)), out_shape...]
    convert_element_type x2 -> x0, other arithmetic: 3.66 us -> none  [the longest x1 1.89 us: local(): enc_master.astype(bf)]
where the time goes in v7:
time: 223 us
  Pallas kernels  217 us (97%)
  other arithmetic  5.36 us (2%)
    pallas_call x1, Pallas kernels, local(): pl.pallas_call(functools.partial(train_kernel, tuple(scratch)), out_shape...  217 us

profile of v7, /device:TPU:1, one launch (start us, length us, event | category | flops | bytes accessed | tf_op | source)
XLA Modules:
  0.0 223.1 jit_solution(15522007357446842685)
XLA Ops:
  0.6 0.0 copy-start
  0.6 0.0 copy-start.3
  0.7 0.0 copy-start.2
  0.7 1.4 fusion.5.refs_1_
  2.1 217.0 %train.1 = (f32[256,512]{1,0:T(8,128)}, f32[512,256]{1,0:T(8,128)}) custom-call(bf16[512,2048]{1,0:T(8,128)(2,1)} %refs_0_.1, s32[2,512]{1,0:T(2,128)} %fusion.5.refs_1_, f32[256,512]{1,0:T(8,128)} %refs_2_.1, f32[512,256]{1,0:T(8,128)} %refs_3_.1, f32[4,128]{1,0:T(4,128)} %bitcast.3), custom_call_target="tpu_custom_call" | custom-call | tf_op jit(solution)/shard_map/train/pallas_call | solution.py:641
  219.1 0.0 copy-start.1
  219.1 0.0 copy-start.4
  219.1 0.0 copy-start.5
  219.2 0.0 copy-start.6
  219.2 0.0 copy-done
  219.2 0.0 copy-done.3
  219.2 0.0 copy-done.2
  219.2 2.6 %multiply_subtract_fusion.1 = (f32[256,512]{1,0:T(8,128)}, f32[256,512]{1,0:T(8,128)}, f32[256,512]{1,0:T(8,128)}) fusion(f32[256,512]{1,0:T(8,128)S(1)} %copy-done, f32[256,512]{1,0:T(8,128)} %get-tuple-element.8, f32[256,512]{1,0:T(8,128)S(1)} %copy-done.2, f32[256,512]{1,0:T(8,128)S(1)} %copy-done.3), kind=kLoop, calls=%fused_computation.6 | loop fusion | flops 1703936 | bytes 3670016 | tf_op jit(solution)/shard_map/sub | solution.py:29
  221.8 0.0 copy-done.1
  221.8 0.0 copy-done.4
  221.8 0.0 copy-done.5
  221.8 0.0 copy-done.6
  221.8 1.4 multiply_subtract_fusion
Async XLA Ops:
  0.6 218.5 %copy-start = (f32[256,512]{1,0:T(8,128)S(1)}, f32[256,512]{1,0:T(8,128)}, u32[]{:S(2)}) copy-start(f32[256,512]{1,0:T(8,128)} %refs_2_.1) | copy-start | bytes 1572868
  0.6 218.5 %copy-start.3 = (f32[256,512]{1,0:T(8,128)S(1)}, f32[256,512]{1,0:T(8,128)}, u32[]{:S(2)}) copy-start(f32[256,512]{1,0:T(8,128)} %param.15) | copy-start | bytes 1572868
  0.7 218.5 %copy-start.2 = (f32[256,512]{1,0:T(8,128)S(1)}, f32[256,512]{1,0:T(8,128)}, u32[]{:S(2)}) copy-start(f32[256,512]{1,0:T(8,128)} %param.14) | copy-start | bytes 1572868
  219.1 2.6 %copy-start.1 = (f32[512,256]{1,0:T(8,128)S(1)}, f32[512,256]{1,0:T(8,128)}, u32[]{:S(2)}) copy-start(f32[512,256]{1,0:T(8,128)} %refs_3_.1) | copy-start | bytes 1572868
  219.1 2.6 %copy-start.4 = (f32[512,256]{1,0:T(8,128)S(1)}, f32[512,256]{1,0:T(8,128)}, u32[]{:S(2)}) copy-start(f32[512,256]{1,0:T(8,128)} %param.16) | copy-start | bytes 1572868
  219.1 2.6 %copy-start.5 = (f32[512,256]{1,0:T(8,128)S(1)}, f32[512,256]{1,0:T(8,128)}, u32[]{:S(2)}) copy-start(f32[512,256]{1,0:T(8,128)} %param.17) | copy-start | bytes 1572868
  219.2 2.6 %copy-start.6 = (f32[512,256]{1,0:T(8,128)S(1)}, f32[512,256]{1,0:T(8,128)}, u32[]{:S(2)}) copy-start(f32[512,256]{1,0:T(8,128)} %get-tuple-element.9) | copy-start | bytes 1572868

commit v8 on v7

--- a/solution.py
+++ b/solution.py
@@ -344,7 +344,7 @@
     ring.arrive(1)
     ring.arrive(2)
     def gather(count, offsets):
-        @pl.loop(0, count)
+        @pl.loop(0, count, unroll=count if count < 5 else 3)
         def _(n):
             a, b = offsets(n)
             home = lax.rem(y + 4 - a, 4) * 4 + lax.rem(x + 4 - b, 4)
@@ -528,7 +528,7 @@
 
     reduce_share(
         ids, part, pgrad, *stages, v["ssend"].at[1], v["srecv"].at[1], groups(code_grad), multiply,
-        [advance(4), advance(2), advance(2), advance(1)],
+        [advance(3), advance(2), advance(2), advance(2)],
     )
     for _ in collect(1, enc_grad, "e_", enc_chain):
         pass

time: 223 us -> 224 us (level)
  no operation moved by 1% of the time
where the time goes in v8:
time: 224 us; the launch traced here: 223 us
  Pallas kernels  217 us (97%)
  other arithmetic  5.36 us (2%)
    pallas_call x1, Pallas kernels, local(): pl.pallas_call(functools.partial(train_kernel, tuple(scratch)), out_shape...  217 us

profile of v8, /device:TPU:1, one launch (start us, length us, event | category | flops | bytes accessed | tf_op | source)
XLA Modules:
  0.0 223.5 jit_solution(2832704048615678728)
XLA Ops:
  0.6 0.0 copy-start
  0.6 0.0 copy-start.3
  0.7 0.0 copy-start.2
  0.7 1.4 fusion.5.refs_1_
  2.1 217.3 %train.1 = (f32[256,512]{1,0:T(8,128)}, f32[512,256]{1,0:T(8,128)}) custom-call(bf16[512,2048]{1,0:T(8,128)(2,1)} %refs_0_.1, s32[2,512]{1,0:T(2,128)} %fusion.5.refs_1_, f32[256,512]{1,0:T(8,128)} %refs_2_.1, f32[512,256]{1,0:T(8,128)} %refs_3_.1, f32[4,128]{1,0:T(4,128)} %bitcast.3), custom_call_target="tpu_custom_call" | custom-call | tf_op jit(solution)/shard_map/train/pallas_call | solution.py:641
  219.4 0.0 copy-start.1
  219.5 0.0 copy-start.4
  219.5 0.0 copy-start.5
  219.5 0.0 copy-start.6
  219.5 0.0 copy-done
  219.5 0.0 copy-done.3
  219.5 0.0 copy-done.2
  219.5 2.6 %multiply_subtract_fusion.1 = (f32[256,512]{1,0:T(8,128)}, f32[256,512]{1,0:T(8,128)}, f32[256,512]{1,0:T(8,128)}) fusion(f32[256,512]{1,0:T(8,128)S(1)} %copy-done, f32[256,512]{1,0:T(8,128)} %get-tuple-element.8, f32[256,512]{1,0:T(8,128)S(1)} %copy-done.2, f32[256,512]{1,0:T(8,128)S(1)} %copy-done.3), kind=kLoop, calls=%fused_computation.6 | loop fusion | flops 1703936 | bytes 3670016 | tf_op jit(solution)/shard_map/sub | solution.py:29
  222.1 0.0 copy-done.1
  222.1 0.0 copy-done.4
  222.1 0.0 copy-done.5
  222.1 0.0 copy-done.6
  222.1 1.4 multiply_subtract_fusion
Async XLA Ops:
  0.6 218.9 %copy-start = (f32[256,512]{1,0:T(8,128)S(1)}, f32[256,512]{1,0:T(8,128)}, u32[]{:S(2)}) copy-start(f32[256,512]{1,0:T(8,128)} %refs_2_.1) | copy-start | bytes 1572868
  0.6 218.9 %copy-start.3 = (f32[256,512]{1,0:T(8,128)S(1)}, f32[256,512]{1,0:T(8,128)}, u32[]{:S(2)}) copy-start(f32[256,512]{1,0:T(8,128)} %param.15) | copy-start | bytes 1572868
  0.7 218.9 %copy-start.2 = (f32[256,512]{1,0:T(8,128)S(1)}, f32[256,512]{1,0:T(8,128)}, u32[]{:S(2)}) copy-start(f32[256,512]{1,0:T(8,128)} %param.14) | copy-start | bytes 1572868
  219.4 2.6 %copy-start.1 = (f32[512,256]{1,0:T(8,128)S(1)}, f32[512,256]{1,0:T(8,128)}, u32[]{:S(2)}) copy-start(f32[512,256]{1,0:T(8,128)} %refs_3_.1) | copy-start | bytes 1572868
  219.5 2.6 %copy-start.4 = (f32[512,256]{1,0:T(8,128)S(1)}, f32[512,256]{1,0:T(8,128)}, u32[]{:S(2)}) copy-start(f32[512,256]{1,0:T(8,128)} %param.16) | copy-start | bytes 1572868
  219.5 2.6 %copy-start.5 = (f32[512,256]{1,0:T(8,128)S(1)}, f32[512,256]{1,0:T(8,128)}, u32[]{:S(2)}) copy-start(f32[512,256]{1,0:T(8,128)} %param.17) | copy-start | bytes 1572868
  219.5 2.6 %copy-start.6 = (f32[512,256]{1,0:T(8,128)S(1)}, f32[512,256]{1,0:T(8,128)}, u32[]{:S(2)}) copy-start(f32[512,256]{1,0:T(8,128)} %get-tuple-element.9) | copy-start | bytes 1572868
